TPU v7x, 128 devices: a whole 4x4x4 slice. The times are simulated.
128 devices in a mesh: leaf: 128 (over y, x, z, core).
Axes of the slice: x: 4, y: 4, z: 4, core: 2. Of those that a mesh axis runs over, the one named last changes fastest.
Arguments:
- points: bfloat16 [32, 1048576], P(None, 'leaf'), may hold values from -1 to 1
- rhs: bfloat16 [16, 1048576], P(None, 'leaf'), may hold values from -6 to 6
- basis: bfloat16 [64, 1048576], P(None, 'leaf'), may hold values from -0.375 to 0.375
- transfer_one: bfloat16 [1024, 64, 256], P('leaf'), may hold values from -0.75 to 0.75
- transfer_two: bfloat16 [256, 64, 256], P('leaf'), may hold values from -0.75 to 0.75
- skeleton_one: bfloat16 [32, 65536], P(None, 'leaf'), may hold values from -1 to 1
- skeleton_two: bfloat16 [32, 16384], P(None, 'leaf'), may hold values from -1 to 1
- near_source: int32 [4096, 10], replicated, may hold values from 0 to 4095, as said below
- far_one: int32 [1024, 8], P('leaf'), may hold values from 0 to 1023, as said below
- far_two: int32 [256, 8], P('leaf'), may hold values from 0 to 255, as said below
Outputs:
- potential: bfloat16 [16, 1048576], P(None, 'leaf')
Inputs may be any that keep to these rules, and one draw needn't show every extreme that they name: `near_source`: entry 0 of row t is t itself. The rows of the 32 leaves of one device name, of each other device, at most 4 distinct leaves: exactly 4 of each of the two devices whose index differs by one modulo 128, and 1 to 2 of every other device; all other entries name leaves of the row's own device. `far_one`: no row names a cluster of its own device (clusters are spread in order, 8 a device). The rows of one device name, of each other device, at most 2 distinct clusters, exactly 2 of the device whose index is one higher modulo 128; repeats within a row are possible. `far_two`: no row names a cluster of its own device (clusters are spread in order, 2 a device). The rows of one device name, of each other device, at most 2 distinct clusters, exactly 2 of the device whose index is one higher modulo 128; repeats within a row are possible.
All inputs are finite; a program needn't handle non-finite values.
Results may differ from a plain program's by a relative error of at most 0.009.
Values may be sent and summed in bfloat16 or wider, within the bound.
No kernel may reach another device: no remote copies, remote signals or barrier semaphores. Data moves between devices by JAX's collectives and lax.ppermute only.
A program may use at most 128 MiB of HBM per device.

v0:
```python
import jax
import jax.numpy as jnp
from jax import lax
from jax.sharding import PartitionSpec as P

DIM = 32
NRHS = 16
RANK = 64
LEAF = 256
NEAR = 10
CAP = 4


kernel_scale = 2.0


def near_terms(target_block, sources):
    target_points = target_block[:, :DIM]
    source_points = sources[:, :, :DIM]
    target_float = target_points.astype(jnp.float32)
    source_float = source_points.astype(jnp.float32)
    target_sq = jnp.sum(target_float * target_float, axis=1)
    source_sq = jnp.sum(source_float * source_float, axis=2)
    inner_prod = jnp.einsum(
        "gdp,gkdq->gkpq", target_points, source_points, preferred_element_type=jnp.float32
    )
    distance = target_sq[:, None, :, None] + source_sq[:, :, None, :] - 2.0 * inner_prod
    weights = jnp.exp(-kernel_scale * distance).astype(jnp.bfloat16)
    return jnp.einsum(
        "gkpq,gknq->gnp", weights, sources[:, :, DIM:], preferred_element_type=jnp.float32
    )


def far_terms(targets, every_cluster, partners):
    cluster_count = partners.shape[0]
    target_grid = targets.reshape(DIM, cluster_count, RANK)
    cluster_points = every_cluster[:DIM].astype(jnp.float32)
    every_sq = jnp.sum(cluster_points * cluster_points, axis=0)
    target_float = target_grid.astype(jnp.float32)
    target_sq = jnp.sum(target_float * target_float, axis=0)
    picked = every_cluster[:, partners]
    picked_sq = every_sq[partners]
    inner_prod = jnp.einsum(
        "dcr,dcfq->cfrq", target_grid, picked[:DIM], preferred_element_type=jnp.float32
    )
    distance = target_sq[:, None, :, None] + picked_sq[:, :, None, :] - 2.0 * inner_prod
    weights = jnp.exp(-kernel_scale * distance).astype(jnp.bfloat16)
    return jnp.einsum("cfrq,ncfq->cnr", weights, picked[DIM:], preferred_element_type=jnp.float32)


def lift(children, transfer):
    clusters = transfer.shape[0]
    joined = (
        children.reshape(clusters, 4, NRHS, RANK)
        .transpose(0, 2, 1, 3)
        .reshape(clusters, NRHS, 4 * RANK)
    )
    return jnp.einsum("cnk,crk->cnr", joined, transfer, preferred_element_type=jnp.float32).astype(
        jnp.bfloat16
    )


def lower(parents, transfer):
    clusters = transfer.shape[0]
    joined = jnp.einsum(
        "cnr,crk->cnk", parents, transfer.astype(jnp.float32), precision=lax.Precision.HIGHEST
    )
    return (
        joined.reshape(clusters, NRHS, 4, RANK)
        .transpose(0, 2, 1, 3)
        .reshape(4 * clusters, NRHS, RANK)
    )


def for_transport(skeleton, coeffs):
    return jnp.concatenate([skeleton, coeffs.transpose(1, 0, 2).reshape(NRHS, -1)], axis=0)


def local(
    points,
    rhs,
    basis,
    transfer_one,
    transfer_two,
    skeleton_one,
    skeleton_two,
    near_source,
    far_one,
    far_two,
):
    peer_count = lax.axis_size("leaf")
    myself = lax.axis_index("leaf")
    leaf_count = points.shape[1] // LEAF
    row_width = DIM + NRHS
    rhs_grid = rhs.reshape(NRHS, leaf_count, LEAF)
    basis_grid = basis.reshape(RANK, leaf_count, LEAF)
    local_blocks = jnp.concatenate(
        [points.reshape(DIM, leaf_count, LEAF), rhs_grid], axis=0
    ).transpose(1, 0, 2)
    leaf_range = jnp.arange(leaf_count, dtype=jnp.int32)
    all_rows = near_source.reshape(peer_count, leaf_count * NEAR)
    hits = all_rows[:, :, None] == (myself * leaf_count + leaf_range)[None, None, :]
    wanted = jnp.any(hits, axis=1) & (jnp.arange(peer_count, dtype=jnp.int32)[:, None] != myself)
    wanted_int = wanted.astype(jnp.int32)
    wanted_rank = jnp.cumsum(wanted_int, axis=1) - wanted_int
    slot_hit = wanted[:, :, None] & (
        wanted_rank[:, :, None] == jnp.arange(CAP, dtype=jnp.int32)[None, None, :]
    )
    leaf_choice = jnp.sum(jnp.where(slot_hit, leaf_range[None, :, None], 0), axis=1)
    my_rows = jnp.where(jnp.any(slot_hit, axis=1), leaf_choice, -1)
    my_near = lax.dynamic_slice_in_dim(near_source, myself * leaf_count, leaf_count, 0)
    source_dev = my_near // leaf_count
    source_leaf = my_near % leaf_count
    remote = source_dev != myself
    every_leaf = jnp.arange(peer_count * leaf_count, dtype=jnp.int32)
    matches = (my_near.reshape(-1)[:, None] == every_leaf[None, :]) & remote.reshape(-1)[:, None]
    requested = jnp.any(matches, axis=0).reshape(peer_count, leaf_count).astype(jnp.int32)
    position = (jnp.cumsum(requested, axis=1) - requested).reshape(-1)
    slot_rank = jnp.sum(jnp.where(matches, position[None, :], 0), axis=1).reshape(leaf_count, NEAR)
    safe_ids = jnp.clip(my_rows, 0, leaf_count - 1)
    packed = local_blocks[safe_ids]
    arrived = lax.all_to_all(
        jnp.where((my_rows >= 0)[..., None, None], packed, jnp.zeros_like(packed)),
        "leaf",
        split_axis=0,
        concat_axis=0,
        tiled=True,
    )
    table_rows = jnp.concatenate(
        [arrived.reshape(peer_count * CAP, row_width, LEAF), local_blocks], axis=0
    )
    slot_index = jnp.where(remote, source_dev * CAP + slot_rank, peer_count * CAP + source_leaf)
    leaf_coeff = jnp.einsum(
        "nlp,rlp->lnr", rhs_grid, basis_grid, preferred_element_type=jnp.float32
    ).astype(jnp.bfloat16)
    coeff_one = lift(leaf_coeff, transfer_one)
    coeff_two = lift(coeff_one, transfer_two)
    columns_one = for_transport(skeleton_one, coeff_one)
    columns_two = for_transport(skeleton_two, coeff_two)
    gathered_one = lax.all_gather(columns_one, "leaf", axis=1, tiled=True)
    gathered_two = lax.all_gather(columns_two, "leaf", axis=1, tiled=True)
    table_one = gathered_one.reshape(row_width, -1, RANK)
    table_two = gathered_two.reshape(row_width, -1, RANK)
    index_one, index_two = (far_one, far_two)

    def near_step(group_items):
        target_block, leaf_ids = group_items
        return near_terms(target_block, table_rows[leaf_ids])

    groups = leaf_count // 2
    near_part = lax.map(
        near_step,
        (local_blocks.reshape(groups, 2, row_width, LEAF), slot_index.reshape(groups, 2, NEAR)),
    )
    near_field = near_part.reshape(leaf_count, NRHS, LEAF).transpose(1, 0, 2)
    field_one = far_terms(skeleton_one, table_one, index_one)
    field_two = far_terms(skeleton_two, table_two, index_two)
    down_one = field_one + lower(field_two, transfer_two)
    down_leaf = lower(down_one, transfer_one).astype(jnp.bfloat16)
    far_out = jnp.einsum("lnr,rlp->nlp", down_leaf, basis_grid, preferred_element_type=jnp.float32)
    return (near_field + far_out).reshape(NRHS, leaf_count * LEAF).astype(jnp.bfloat16)


def solution(mesh):
    placed = (
        P(None, "leaf"),
        P(None, "leaf"),
        P(None, "leaf"),
        P("leaf", None, None),
        P("leaf", None, None),
        P(None, "leaf"),
        P(None, "leaf"),
        P(),
        P("leaf", None),
        P("leaf", None),
    )
    return jax.shard_map(
        local, mesh=mesh, in_specs=placed, out_specs=P(None, "leaf"), check_vma=False
    )
```

profile of v0, /device:TPU:1, one launch (start us, length us, event | category | flops | bytes accessed | tf_op | source)
XLA Modules:
  0.0 455.2 jit_solution(14101491463423326010)
XLA Ops:
  18.5 14.5 %gather_fusion.1 = bf16[512,48,256]{2,1,0:T(8,128)(2,1)} fusion(bf16[32,48,256]{2,1,0:T(8,128)(2,1)S(1)} %bitcast.139, s32[1024]{0:T(1024)S(1)} %pad_clamp_fusion.3), kind=kCustom, calls=%fused_computation.1 | custom fusion | bytes 25167872 | tf_op jit(solution)/shard_map/gather | solution.py:121
  33.1 10.8 %broadcast_select_fusion = bf16[128,4,48,256]{3,2,1,0:T(8,128)(2,1)} fusion(bf16[128,4,48,256]{3,2,1,0:T(8,128)(2,1)} %bitcast.142, pred[128,4]{1,0:T(8,128)(4,1)S(1)} %copy.66), kind=kLoop, calls=%fused_computation.26 | loop fusion | flops 6291456 | bytes 25166336 | tf_op jit(solution)/shard_map/jit(_where)/select_n | solution.py:123
  43.9 11.9 %all-to-all-start = ((bf16[128,4,48,256]{3,2,1,0:T(8,128)(2,1)}), bf16[128,4,48,256]{3,2,1,0:T(8,128)(2,1)}, u32[]{:S(2)}, u32[]{:S(2)}) async-start(bf16[128,4,48,256]{3,2,1,0:T(8,128)(2,1)} %broadcast_select_fusion), calls=%async_computation | async-start | bytes 25165824 | tf_op jit(solution)/shard_map/all_to_all | solution.py:122
  60.0 113.6 %all-gather.5.cloned.1.call-done = bf16[48,16384]{1,0:T(8,128)(2,1)} async-done(((bf16[48,128]{1,0:T(8,128)(2,1)}), bf16[48,16384]{1,0:T(8,128)(2,1)}) %all-gather.5.cloned.1.call-update) | async-done | bytes 1572880 | tf_op jit(solution)/shard_map/all_gather | solution.py:141
  175.2 5.4 %reshape.235 = bf16[48,256,64]{2,1,0:T(8,128)(2,1)} reshape(bf16[48,16384]{1,0:T(8,128)(2,1)} %all-gather.5.cloned.1.call-done) | data formatting | bytes 3145728 | tf_op jit(solution)/shard_map/reshape | solution.py:143
  180.7 5.6 %copy.79 = bf16[48,256,64]{2,0,1:T(8,128)(2,1)} copy(bf16[48,256,64]{2,1,0:T(8,128)(2,1)} %reshape.235) | data formatting | bytes 3145728 | tf_op jit(solution)/shard_map/reshape | solution.py:143
  190.0 86.2 %all-gather.3.cloned.1.call-done = bf16[48,65536]{1,0:T(8,128)(2,1)} async-done(((bf16[48,512]{1,0:T(8,128)(2,1)}), bf16[48,65536]{1,0:T(8,128)(2,1)}) %all-gather.3.cloned.1.call-update) | async-done | bytes 6291472 | tf_op jit(solution)/shard_map/all_gather | solution.py:140
  279.8 14.3 %reshape.230 = bf16[48,1024,64]{2,1,0:T(8,128)(2,1)} reshape(bf16[48,65536]{1,0:T(8,128)(2,1)} %all-gather.3.cloned.1.call-done) | data formatting | bytes 12582912 | tf_op jit(solution)/shard_map/reshape | solution.py:142
  294.1 14.7 %copy.74 = bf16[48,1024,64]{2,0,1:T(8,128)(2,1)} copy(bf16[48,1024,64]{2,1,0:T(8,128)(2,1)} %reshape.230) | data formatting | bytes 12582912 | tf_op jit(solution)/shard_map/reshape | solution.py:142
  316.1 11.0 %pad_maximum_fusion = bf16[544,48,256]{2,1,0:T(8,128)(2,1)} fusion(bf16[32,48,256]{2,1,0:T(8,128)(2,1)S(1)} %bitcast.140, bf16[512,48,256]{2,1,0:T(8,128)(2,1)} %bitcast.13), kind=kLoop, calls=%fused_computation.25 | loop fusion | flops 6684672 | bytes 26738688 | tf_op jit(solution)/shard_map/concatenate | solution.py:129
  327.1 120.3 %while.10 = (s32[]{:T(128)}, f32[16,2,16,256]{3,2,1,0:T(8,128)S(1)}, s32[16,2,10]{2,1,0:T(2,128)S(1)}, bf16[544,48,256]{2,1,0:T(8,128)(2,1)}, bf16[16,2,48,256]{3,2,1,0:T(8,128)(2,1)S(1)}, /*index=5*/s32[]{:T(128)}) while((s32[]{:T(128)}, f32[16,2,16,256]{3,2,1,0:T(8,128)S(1)}, s32[16,2,10]{2,1,0:T(2,128)S(1)}, ...), condition=%wide.region_10.11_spmd, body=%wide.region_7.10_spmd.sunk | while | flops 132918848 | bytes 2060857 | solution.py:151
  327.2 5.4 %gather_fusion = bf16[20,48,256]{2,1,0:T(8,128)(2,1)S(1)} fusion(bf16[544,48,256]{2,1,0:T(8,128)(2,1)} %get-tuple-element.106, s32[1024]{0:T(1024)S(1)} %pad_clamp_fusion.5), kind=kCustom, calls=%fused_computation.clone.1 | custom fusion | bytes 983120 | tf_op jit(solution)/shard_map/while/body/eval_jaxpr/gather | solution.py:148
  334.8 5.4 %gather_fusion = bf16[20,48,256]{2,1,0:T(8,128)(2,1)S(1)} fusion(bf16[544,48,256]{2,1,0:T(8,128)(2,1)} %get-tuple-element.106, s32[1024]{0:T(1024)S(1)} %pad_clamp_fusion.5), kind=kCustom, calls=%fused_computation.clone.1 | custom fusion | bytes 983120 | tf_op jit(solution)/shard_map/while/body/eval_jaxpr/gather | solution.py:148
  342.3 5.4 %gather_fusion = bf16[20,48,256]{2,1,0:T(8,128)(2,1)S(1)} fusion(bf16[544,48,256]{2,1,0:T(8,128)(2,1)} %get-tuple-element.106, s32[1024]{0:T(1024)S(1)} %pad_clamp_fusion.5), kind=kCustom, calls=%fused_computation.clone.1 | custom fusion | bytes 983120 | tf_op jit(solution)/shard_map/while/body/eval_jaxpr/gather | solution.py:148
  349.8 5.4 %gather_fusion = bf16[20,48,256]{2,1,0:T(8,128)(2,1)S(1)} fusion(bf16[544,48,256]{2,1,0:T(8,128)(2,1)} %get-tuple-element.106, s32[1024]{0:T(1024)S(1)} %pad_clamp_fusion.5), kind=kCustom, calls=%fused_computation.clone.1 | custom fusion | bytes 983120 | tf_op jit(solution)/shard_map/while/body/eval_jaxpr/gather | solution.py:148
  357.3 5.4 %gather_fusion = bf16[20,48,256]{2,1,0:T(8,128)(2,1)S(1)} fusion(bf16[544,48,256]{2,1,0:T(8,128)(2,1)} %get-tuple-element.106, s32[1024]{0:T(1024)S(1)} %pad_clamp_fusion.5), kind=kCustom, calls=%fused_computation.clone.1 | custom fusion | bytes 983120 | tf_op jit(solution)/shard_map/while/body/eval_jaxpr/gather | solution.py:148
  364.8 5.4 %gather_fusion = bf16[20,48,256]{2,1,0:T(8,128)(2,1)S(1)} fusion(bf16[544,48,256]{2,1,0:T(8,128)(2,1)} %get-tuple-element.106, s32[1024]{0:T(1024)S(1)} %pad_clamp_fusion.5), kind=kCustom, calls=%fused_computation.clone.1 | custom fusion | bytes 983120 | tf_op jit(solution)/shard_map/while/body/eval_jaxpr/gather | solution.py:148
  372.3 5.4 %gather_fusion = bf16[20,48,256]{2,1,0:T(8,128)(2,1)S(1)} fusion(bf16[544,48,256]{2,1,0:T(8,128)(2,1)} %get-tuple-element.106, s32[1024]{0:T(1024)S(1)} %pad_clamp_fusion.5), kind=kCustom, calls=%fused_computation.clone.1 | custom fusion | bytes 983120 | tf_op jit(solution)/shard_map/while/body/eval_jaxpr/gather | solution.py:148
  379.8 5.4 %gather_fusion = bf16[20,48,256]{2,1,0:T(8,128)(2,1)S(1)} fusion(bf16[544,48,256]{2,1,0:T(8,128)(2,1)} %get-tuple-element.106, s32[1024]{0:T(1024)S(1)} %pad_clamp_fusion.5), kind=kCustom, calls=%fused_computation.clone.1 | custom fusion | bytes 983120 | tf_op jit(solution)/shard_map/while/body/eval_jaxpr/gather | solution.py:148
  387.4 5.4 %gather_fusion = bf16[20,48,256]{2,1,0:T(8,128)(2,1)S(1)} fusion(bf16[544,48,256]{2,1,0:T(8,128)(2,1)} %get-tuple-element.106, s32[1024]{0:T(1024)S(1)} %pad_clamp_fusion.5), kind=kCustom, calls=%fused_computation.clone.1 | custom fusion | bytes 983120 | tf_op jit(solution)/shard_map/while/body/eval_jaxpr/gather | solution.py:148
  394.9 5.4 %gather_fusion = bf16[20,48,256]{2,1,0:T(8,128)(2,1)S(1)} fusion(bf16[544,48,256]{2,1,0:T(8,128)(2,1)} %get-tuple-element.106, s32[1024]{0:T(1024)S(1)} %pad_clamp_fusion.5), kind=kCustom, calls=%fused_computation.clone.1 | custom fusion | bytes 983120 | tf_op jit(solution)/shard_map/while/body/eval_jaxpr/gather | solution.py:148
  402.4 5.4 %gather_fusion = bf16[20,48,256]{2,1,0:T(8,128)(2,1)S(1)} fusion(bf16[544,48,256]{2,1,0:T(8,128)(2,1)} %get-tuple-element.106, s32[1024]{0:T(1024)S(1)} %pad_clamp_fusion.5), kind=kCustom, calls=%fused_computation.clone.1 | custom fusion | bytes 983120 | tf_op jit(solution)/shard_map/while/body/eval_jaxpr/gather | solution.py:148
  417.4 5.4 %gather_fusion = bf16[20,48,256]{2,1,0:T(8,128)(2,1)S(1)} fusion(bf16[544,48,256]{2,1,0:T(8,128)(2,1)} %get-tuple-element.106, s32[1024]{0:T(1024)S(1)} %pad_clamp_fusion.5), kind=kCustom, calls=%fused_computation.clone.1 | custom fusion | bytes 983120 | tf_op jit(solution)/shard_map/while/body/eval_jaxpr/gather | solution.py:148
  424.9 5.4 %gather_fusion = bf16[20,48,256]{2,1,0:T(8,128)(2,1)S(1)} fusion(bf16[544,48,256]{2,1,0:T(8,128)(2,1)} %get-tuple-element.106, s32[1024]{0:T(1024)S(1)} %pad_clamp_fusion.5), kind=kCustom, calls=%fused_computation.clone.1 | custom fusion | bytes 983120 | tf_op jit(solution)/shard_map/while/body/eval_jaxpr/gather | solution.py:148
  (215 shorter events, 82.8 us)
Async XLA Ops:
  6.5 2.0 copy-start
  6.5 11.6 %copy-start.5 = (bf16[16,8192]{1,0:T(8,128)(2,1)S(1)}, bf16[16,8192]{1,0:T(8,128)(2,1)}, u32[]{:S(2)}) copy-start(bf16[16,8192]{1,0:T(8,128)(2,1)} %param.13) | copy-start | bytes 786436
  6.5 167.1 %all-gather.5.cloned.1.call-start = ((), (), s32[]{:S(2)}) async-start(), calls=%async_computation.2 | async-start | bytes 1585152 | tf_op jit(solution)/shard_map/all_gather | solution.py:141
  11.2 265.0 %all-gather.3.cloned.1.call-start = ((), (), s32[]{:S(2)}) async-start(), calls=%async_computation.1 | async-start | bytes 6340608 | tf_op jit(solution)/shard_map/all_gather | solution.py:140
  43.9 12.0 %copy-start.6 = (bf16[32,128]{1,0:T(8,128)(2,1)S(1)}, bf16[32,128]{1,0:T(8,128)(2,1)}, u32[]{:S(2)}) copy-start(bf16[32,128]{1,0:T(8,128)(2,1)} %param.18) | copy-start | bytes 24580
  43.9 12.0 %copy-start.3 = (bf16[32,512]{1,0:T(8,128)(2,1)S(1)}, bf16[32,512]{1,0:T(8,128)(2,1)}, u32[]{:S(2)}) copy-start(bf16[32,512]{1,0:T(8,128)(2,1)} %param.17) | copy-start | bytes 98308
  43.9 15.6 %copy-start.8 = (s32[2,8]{1,0:T(2,128)S(1)}, s32[2,8]{1,0:T(2,128)}, u32[]{:S(2)}) copy-start(s32[2,8]{1,0:T(2,128)} %param.21) | copy-start | bytes 196
  43.9 15.8 %copy-start.7 = (s32[8,8]{1,0:T(8,128)S(1)}, s32[8,8]{1,0:T(8,128)}, u32[]{:S(2)}) copy-start(s32[8,8]{1,0:T(8,128)} %param.20) | copy-start | bytes 772
  43.9 272.2 %all-to-all-start = ((bf16[128,4,48,256]{3,2,1,0:T(8,128)(2,1)}), bf16[128,4,48,256]{3,2,1,0:T(8,128)(2,1)}, u32[]{:S(2)}, u32[]{:S(2)}) async-start(bf16[128,4,48,256]{3,2,1,0:T(8,128)(2,1)} %broadcast_select_fusion), calls=%async_computation | async-start | bytes 25165824 | tf_op jit(solution)/shard_map/all_to_all | solution.py:122
  175.2 14.6 %copy-start.4 = (bf16[2,64,256]{2,1,0:T(8,128)(2,1)S(1)}, bf16[2,64,256]{2,1,0:T(8,128)(2,1)}, u32[]{:S(2)}) copy-start(bf16[2,64,256]{2,1,0:T(8,128)(2,1)} %param.16) | copy-start | bytes 196612
  316.1 11.0 %copy-start.2 = (f32[16,2,16,256]{3,2,1,0:T(8,128)S(1)}, f32[16,2,16,256]{3,2,1,0:T(8,128)}, u32[]{:S(2)}) copy-start(f32[16,2,16,256]{3,2,1,0:T(8,128)} %custom-call.13) | copy-start | bytes 1572868
  327.1 120.3 %copy-start.1 = (bf16[64,8192]{1,0:T(8,128)(2,1)S(1)}, bf16[64,8192]{1,0:T(8,128)(2,1)}, u32[]{:S(2)}) copy-start(bf16[64,8192]{1,0:T(8,128)(2,1)} %param.14) | copy-start | bytes 3145732
Sparse Core Ops, SparseCore 0:
  11.3 162.2 all-gather.4
  176.4 99.7 all-gather.2
where the time goes:
time: 458 us; the launch traced here: 455 us
  waiting for transfers between devices  200 us (44%)
  local copies, waits for them, and re-layouts  159 us (35%)
  other arithmetic  35.5 us (8%)
  matrix products  34.8 us (8%)
  between operations  13.7 us (3%)
  starting transfers between devices  12 us (3%)
    all_gather x1, waiting for transfers between devices, local(): gathered_two = lax.all_gather(columns_two, 'leaf', axis=1, tiled=True)  114 us
    gather x16, local copies, waits for them, and re-layouts, near_step(): return near_terms(target_block, table_rows[leaf_ids])  86.3 us
    all_gather x1, waiting for transfers between devices, local(): gathered_one = lax.all_gather(columns_one, 'leaf', axis=1, tiled=True)  86.2 us
    dot_general x16, matrix products, near_terms(): jnp.einsum('gkpq,gknq->gnp', weights, sources[:, :, DIM:], preferred_elem...  29.7 us
    reshape x2, local copies, waits for them, and re-layouts, local(): table_one = gathered_one.reshape(row_width, -1, RANK)  28.9 us
    gather x1, local copies, waits for them, and re-layouts, local(): packed = local_blocks[safe_ids]  14.5 us
    all_to_all x1, starting transfers between devices, local(): lax.all_to_all(jnp.where((my_rows >= 0)[..., None, None], packed, jnp.zer...  11.9 us
    reshape x2, local copies, waits for them, and re-layouts, local(): table_two = gathered_two.reshape(row_width, -1, RANK)  11 us
  transfers between devices with their start and end apart: 3, of which 2 were waited for; matrix products, arithmetic and copies ran while one was open for 20% of the time, Pallas kernels for 0%

commit v1 on v0

v1 whole, which is shorter than its diff:
```python
import jax
import jax.numpy as jnp
from jax import lax
from jax.experimental import pallas as pl
from jax.experimental.pallas import tpu as pltpu
from jax.sharding import PartitionSpec as P

DIM = 32
NRHS = 16
RANK = 64
LEAF = 256
NEAR = 10
FAR = 8
LEAVES = 32
ONE = 8
TWO = 2
PAIRS = ONE // 2 + TWO // 2
ROWS = DIM + NRHS
PEERS = 128
LOCAL = 2 * PEERS + 4
TABLE = LOCAL + LEAVES
LOG2E = 1.4426950408889634
MIB = 1 << 20

NT = (((1,), (1,)), ((), ()))
NN = (((1,), (0,)), ((), ()))


def dot(a, b, dims=NN):
    return lax.dot_general(a, b, dims, preferred_element_type=jnp.float32)


def vmem(limit=48):
    return pltpu.CompilerParams(vmem_limit_bytes=limit * MIB)


ANY = pl.BlockSpec(memory_space=pl.ANY)
VM = pl.BlockSpec(memory_space=pltpu.VMEM)
SM = pl.BlockSpec(memory_space=pltpu.SMEM)


def pack_kernel(
    source_ref, points_ref, rhs_ref, msg_ref, right_ref, left_ref, block_ref,
    row_ref, row_smem, row_sem, msg_sem, side_sem,
):
    me = lax.axis_index("leaf")
    for leaf in range(LEAVES):
        columns = pl.ds(leaf * LEAF, LEAF)
        block_ref[leaf, :DIM, :] = points_ref[:, columns]
        block_ref[leaf, DIM:, :] = rhs_ref[:, columns]
    width = PEERS * LEAVES
    low = high = bits = None
    for k in range(NEAR):
        mine = source_ref[k : k + 1, :] - me * LEAVES
        inside = (mine >> 5) == 0
        a = jnp.where(inside, mine, LEAVES)
        b = jnp.where(inside, mine, -1)
        c = jnp.where(inside, 1 << (mine & 31), 0)
        low = a if k == 0 else jnp.minimum(low, a)
        high = b if k == 0 else jnp.maximum(high, b)
        bits = c if k == 0 else bits | c
    low, high, bits = (jnp.broadcast_to(v, (8, width)) for v in (low, high, bits))
    for step in (16, 8, 4, 2, 1):
        low = jnp.minimum(low, pltpu.roll(low, width - step, 1))
        high = jnp.maximum(high, pltpu.roll(high, width - step, 1))
        bits = bits | pltpu.roll(bits, width - step, 1)
    place = lax.broadcasted_iota(jnp.int32, (8, width), 1) & 31
    row_ref[...] = jnp.where(
        place == 0, low, jnp.where(place == 1, pltpu.roll(high, 1, 1), pltpu.roll(bits, 2, 1))
    )
    copy = pltpu.make_async_copy(row_ref.at[0:1], row_smem, row_sem)
    copy.start()
    copy.wait()

    def send(peer, _):
        for slot in range(2):
            leaf = row_smem[0, peer * LEAVES + slot] & 31
            pltpu.make_async_copy(block_ref.at[leaf], msg_ref.at[peer, slot], msg_sem).start()
        return 0

    lax.fori_loop(0, PEERS, send, 0, unroll=4)
    for side, (ref, step) in enumerate(((right_ref, 1), (left_ref, PEERS - 1))):
        at = lax.rem(me + step, PEERS) * LEAVES
        between = row_smem[0, at + 2]
        between = between & ~(1 << (row_smem[0, at] & 31)) & ~(1 << (row_smem[0, at + 1] & 31))

        def scan(bit, found):
            has = ((between >> bit) & 1) == 1
            return jnp.where(has & (found[0] < 0), bit, found[0]), jnp.where(has, bit, found[1])

        first, last = lax.fori_loop(0, LEAVES, scan, (jnp.int32(-1), jnp.int32(0)))
        for slot, leaf in enumerate((first & 31, last & 31)):
            pltpu.make_async_copy(block_ref.at[leaf], ref.at[slot], side_sem.at[side]).start()
    pltpu.make_async_copy(msg_ref, msg_ref, msg_sem).wait()
    for side, ref in enumerate((right_ref, left_ref)):
        pltpu.make_async_copy(ref, ref, side_sem.at[side]).wait()


def pack(source, points, rhs):
    block = jax.ShapeDtypeStruct((LEAVES, ROWS, LEAF), jnp.bfloat16)
    side = jax.ShapeDtypeStruct((2, ROWS, LEAF), jnp.bfloat16)
    return pl.pallas_call(
        pack_kernel,
        out_shape=(
            jax.ShapeDtypeStruct((PEERS, 2, ROWS, LEAF), jnp.bfloat16), side, side, block,
        ),
        in_specs=[VM, VM, VM],
        out_specs=(ANY, ANY, ANY, VM),
        scratch_shapes=[
            pltpu.VMEM((8, PEERS * LEAVES), jnp.int32),
            pltpu.SMEM((1, PEERS * LEAVES), jnp.int32),
            pltpu.SemaphoreType.DMA,
            pltpu.SemaphoreType.DMA,
            pltpu.SemaphoreType.DMA((2,)),
        ],
        compiler_params=vmem(),
        name="pack",
    )(source.T, points, rhs)


def upper(b):
    return jnp.concatenate([b, jnp.zeros_like(b)], axis=0)


def below(b):
    return jnp.concatenate([jnp.zeros_like(b), b], axis=0)


def coeff_kernel(rhs_ref, basis_ref, one_ref, two_ref, skel_one_ref, skel_two_ref, out_ref):
    def leaf_pair(leaf):
        a, b = (pl.ds((leaf + i) * LEAF, LEAF) for i in range(2))
        return (
            dot(rhs_ref[:, a], upper(basis_ref[:, a]), NT)
            + dot(rhs_ref[:, b], below(basis_ref[:, b]), NT)
        ).astype(jnp.bfloat16)

    def lift_pair(children, transfer_ref, cluster):
        return (
            dot(children[0], upper(transfer_ref[cluster]), NT)
            + dot(children[1], below(transfer_ref[cluster + 1]), NT)
        ).astype(jnp.bfloat16)

    pairs = []
    for pair in range(ONE // 2):
        joined = [
            jnp.concatenate([leaf_pair(4 * c), leaf_pair(4 * c + 2)], axis=1)
            for c in (2 * pair, 2 * pair + 1)
        ]
        pairs.append(lift_pair(joined, one_ref, 2 * pair))
        out_ref[pair, :DIM, :] = skel_one_ref[:, pl.ds(pair * 2 * RANK, 2 * RANK)]
        out_ref[pair, DIM:, :] = pairs[-1]
    joined = [jnp.concatenate(pairs[2 * e : 2 * e + 2], axis=1) for e in range(TWO)]
    out_ref[PAIRS - 1, :DIM, :] = skel_two_ref[...]
    out_ref[PAIRS - 1, DIM:, :] = lift_pair(joined, two_ref, 0)


def coefficients(rhs, basis, transfer_one, transfer_two, skeleton_one, skeleton_two):
    return pl.pallas_call(
        coeff_kernel,
        out_shape=jax.ShapeDtypeStruct((PAIRS, ROWS, 2 * RANK), jnp.bfloat16),
        in_specs=[VM] * 6,
        out_specs=VM,
        compiler_params=vmem(),
        name="coefficients",
    )(rhs, basis, transfer_one, transfer_two, skeleton_one, skeleton_two)


def table_rows(near_source, me):
    mine = lax.dynamic_slice_in_dim(near_source, me * LEAVES, LEAVES, 0).reshape(-1)
    device, leaf = mine >> 5, mine & 31
    from_peer = device[:, None] == jnp.arange(PEERS, dtype=jnp.int32)[None, :]
    low = jnp.min(jnp.where(from_peer, leaf[:, None], LEAVES), axis=0)
    high = jnp.max(jnp.where(from_peer, leaf[:, None], -1), axis=0)
    low_of = jnp.sum(jnp.where(from_peer, low[None, :], 0), axis=1)
    high_of = jnp.sum(jnp.where(from_peer, high[None, :], 0), axis=1)
    row = 2 * device + (leaf != low_of)
    inner = (leaf > low_of) & (leaf < high_of)
    for side, step in enumerate((PEERS - 1, 1)):
        chosen = inner & (device == (me + step) % PEERS)
        first = jnp.min(jnp.where(chosen, leaf, LEAVES))
        row = jnp.where(chosen, 2 * PEERS + 2 * side + (leaf != first), row)
    return jnp.where(device == me, LOCAL + leaf, row)


def near_kernel(
    row_ref, arrived_ref, left_ref, right_ref, own_ref, out_ref, table_ref, sem
):
    copies = [
        pltpu.make_async_copy(ref, table_ref.at[pl.ds(at, ref.shape[0])], sem.at[i])
        for i, (ref, at) in enumerate(
            ((arrived_ref, 0), (left_ref, 2 * PEERS), (right_ref, 2 * PEERS + 2), (own_ref, LOCAL))
        )
    ]
    for copy in copies:
        copy.start()
    for copy in copies:
        copy.wait()

    def step(leaf, _):
        target = table_ref[LOCAL + leaf, :DIM, :].astype(jnp.float32).T
        target_sq = jnp.sum(target * target, axis=1, keepdims=True) * (2 * LOG2E)
        target = target.astype(jnp.bfloat16)
        total = jnp.zeros((NRHS, LEAF), jnp.float32)
        for k in range(NEAR):
            row = row_ref[leaf * NEAR + k]
            source = table_ref[row, :DIM, :]
            wide = source.astype(jnp.float32)
            source_sq = jnp.sum(wide * wide, axis=0, keepdims=True) * (2 * LOG2E)
            power = dot(target, source) * (4 * LOG2E) - target_sq - source_sq
            weights = jnp.exp2(power).astype(jnp.bfloat16)
            total += dot(table_ref[row, DIM:, :], weights, NT)
        out_ref[:, pl.ds(pl.multiple_of(leaf * LEAF, LEAF), LEAF)] = total
        return 0

    lax.fori_loop(0, LEAVES, step, 0)


def near_field(rows, arrived, left, right, own):
    return pl.pallas_call(
        near_kernel,
        out_shape=jax.ShapeDtypeStruct((NRHS, LEAVES * LEAF), jnp.float32),
        in_specs=[SM, ANY, ANY, ANY, ANY],
        out_specs=VM,
        scratch_shapes=[
            pltpu.VMEM((TABLE, ROWS, LEAF), jnp.bfloat16),
            pltpu.SemaphoreType.DMA((4,)),
        ],
        compiler_params=vmem(),
        cost_estimate=pl.CostEstimate(
            flops=2 * 320 * 65536 * 48, bytes_accessed=8 * MIB, transcendentals=320 * 65536
        ),
        name="near_field",
    )(rows, arrived, left, right, own)


def far_kernel(
    far_one_ref, far_two_ref, gathered_ref, skel_one_ref, skel_two_ref, one_ref, two_ref,
    basis_ref, near_ref, out_ref, picked_ref, sem,
):
    for c in range(ONE):
        for j in range(FAR):
            b = far_one_ref[c, j]
            pltpu.make_async_copy(
                gathered_ref.at[(b >> 3) * PAIRS + ((b & 7) >> 1)], picked_ref.at[c * FAR + j], sem
            ).start()
    for e in range(TWO):
        for j in range(FAR):
            b = far_two_ref[e, j]
            pltpu.make_async_copy(
                gathered_ref.at[(b >> 1) * PAIRS + PAIRS - 1],
                picked_ref.at[(ONE + e) * FAR + j],
                sem,
            ).start()
    pltpu.make_async_copy(picked_ref, picked_ref, sem).wait()
    half_of = lax.broadcasted_iota(jnp.int32, (NRHS, 2 * RANK), 1) >> 6

    def split(x):
        high = x.astype(jnp.bfloat16)
        return jnp.concatenate([high, (x - high.astype(jnp.float32)).astype(jnp.bfloat16)], axis=0)

    def exact(parts, b):
        both = dot(parts, b)
        return both[:NRHS] + both[NRHS:]

    def turned(skel_ref, pair):
        return skel_ref[:, pl.ds(pair * 2 * RANK, 2 * RANK)].astype(jnp.float32).T

    def field_pair(skel_ref, partners_ref, pair, at):
        both = turned(skel_ref, pair)
        total = None
        for i, padded in enumerate((upper, below)):
            c = 2 * pair + i
            target = both[i * RANK : (i + 1) * RANK]
            target_sq = jnp.sum(target * target, axis=1, keepdims=True) * (2 * LOG2E)
            blocks = [picked_ref[(at + c) * FAR + j] for j in range(FAR)]
            source = jnp.concatenate([block[:DIM] for block in blocks], axis=1)
            coeffs = jnp.concatenate(
                [
                    jnp.where(half_of == (partners_ref[c, j] & 1), blocks[j][DIM:], 0)
                    for j in range(FAR)
                ],
                axis=1,
            )
            wide = source.astype(jnp.float32)
            source_sq = jnp.sum(wide * wide, axis=0, keepdims=True) * (2 * LOG2E)
            power = dot(target.astype(jnp.bfloat16), source) * (4 * LOG2E) - target_sq - source_sq
            weights = jnp.exp2(power).astype(jnp.bfloat16)
            term = dot(coeffs, padded(weights), NT)
            total = term if i == 0 else total + term
        return total

    field_two = split(field_pair(skel_two_ref, far_two_ref, 0, ONE))
    from_two = [
        exact(field_two, padded(two_ref[e])) for e, padded in enumerate((upper, below))
    ]
    for pair in range(ONE // 2):
        parent = from_two[pair // 2][:, (pair % 2) * 2 * RANK : (pair % 2 + 1) * 2 * RANK]
        down_one = split(field_pair(skel_one_ref, far_one_ref, pair, 0) + parent)
        for i, padded in enumerate((upper, below)):
            c = 2 * pair + i
            down_leaf = exact(down_one, padded(one_ref[c])).astype(jnp.bfloat16)
            for leaf in range(4):
                columns = pl.ds((4 * c + leaf) * LEAF, LEAF)
                half = down_leaf[:, (leaf // 2) * 2 * RANK : (leaf // 2 + 1) * 2 * RANK]
                basis = (upper, below)[leaf % 2](basis_ref[:, columns])
                out_ref[:, columns] = (near_ref[:, columns] + dot(half, basis)).astype(
                    jnp.bfloat16
                )


def far_field(far_one, far_two, gathered, skeleton_one, skeleton_two, transfer_one, transfer_two,
              basis, near):
    return pl.pallas_call(
        far_kernel,
        out_shape=jax.ShapeDtypeStruct((NRHS, LEAVES * LEAF), jnp.bfloat16),
        in_specs=[SM, SM, ANY] + [VM] * 6,
        out_specs=VM,
        scratch_shapes=[
            pltpu.VMEM(((ONE + TWO) * FAR, ROWS, 2 * RANK), jnp.bfloat16),
            pltpu.SemaphoreType.DMA,
        ],
        compiler_params=vmem(),
        name="far_field",
    )(far_one, far_two, gathered, skeleton_one, skeleton_two, transfer_one, transfer_two, basis,
      near)


def shift(x, step):
    return lax.ppermute(x, "leaf", [(i, (i + step) % PEERS) for i in range(PEERS)])


def local(
    points, rhs, basis, transfer_one, transfer_two, skeleton_one, skeleton_two, near_source,
    far_one, far_two,
):
    me = lax.axis_index("leaf")
    message, to_right, to_left, own = pack(near_source, points, rhs)
    columns = coefficients(rhs, basis, transfer_one, transfer_two, skeleton_one, skeleton_two)
    gathered = lax.all_gather(columns, "leaf", axis=0, tiled=True)
    arrived = lax.all_to_all(message, "leaf", split_axis=0, concat_axis=0, tiled=True)
    from_left, from_right = shift(to_right, 1), shift(to_left, -1)
    rows = table_rows(near_source, me)
    near = near_field(
        rows, arrived.reshape(2 * PEERS, ROWS, LEAF), from_left, from_right, own
    )
    return far_field(far_one, far_two, gathered, skeleton_one, skeleton_two, transfer_one,
                     transfer_two, basis, near)


def solution(mesh):
    placed = (
        P(None, "leaf"),
        P(None, "leaf"),
        P(None, "leaf"),
        P("leaf", None, None),
        P("leaf", None, None),
        P(None, "leaf"),
        P(None, "leaf"),
        P(),
        P("leaf", None),
        P("leaf", None),
    )
    return jax.shard_map(
        local, mesh=mesh, in_specs=placed, out_specs=P(None, "leaf"), check_vma=False
    )
```

time: 458 us -> 164 us (0.36)
  local copies, waits for them, and re-layouts: 159 us -> 9.66 us
  waiting for transfers between devices: 200 us -> 72.3 us
  Pallas kernels: 0 us -> 51.8 us
  matrix products: 34.8 us -> 0 us
  other arithmetic: 35.5 us -> 2.42 us
    all_gather x2 -> x1, waiting for transfers between devices: 200 us -> 0.02 us  [local(): gathered = lax.all_gather(columns, 'leaf', axis=0, tiled=True)]
    gather x21 -> x0, local copies, waits for them, and re-layouts: 110 us -> none  [the longest x16 86.3 us: near_step(): return near_terms(target_block, table_rows[leaf_ids])]
    ppermute x0 -> x2, waiting for transfers between devices: none -> 63.6 us  [shift(): lax.ppermute(x, 'leaf', [(i, (i + step) % PEERS) for i in range(PEERS)])]
    pallas_call x0 -> x4, Pallas kernels: none -> 51.8 us  [the longest x1 39.3 us: near_field(): pl.pallas_call(near_kernel, out_shape=jax.ShapeDtypeStruct((NRHS, LEAVES...]
    reshape x11 -> x0, local copies, waits for them, and re-layouts: 40.7 us -> none  [the longest x2 28.9 us: local(): table_one = gathered_one.reshape(row_width, -1, RANK)]
    dot_general x24 -> x0, matrix products: 34.8 us -> none  [the longest x16 29.7 us: near_terms(): jnp.einsum('gkpq,gknq->gnp', weights, sources[:, :, DIM:], preferred_elem...]
    concatenate x4 -> x0, other arithmetic: 13.7 us -> none  [the longest x1 11 us: local(): jnp.concatenate([arrived.reshape(peer_count * CAP, row_width, LEAF), loca...]
    select_n x21 -> x1, other arithmetic: 10.9 us -> 1.25 us  [table_rows(): return jnp.where(device == me, LOCAL + leaf, row)]
  transfers between devices with their start and end apart: 3 -> 4, of which waited for: 2 -> 2; matrix products, arithmetic and copies ran while one was open for 20% -> 2% of each run, Pallas kernels for 0% -> 27%
where the time goes in v1:
time: 164 us
  waiting for transfers between devices  72.3 us (44%)
  Pallas kernels  51.8 us (32%)
  starting transfers between devices  13.7 us (8%)
  between operations  13.6 us (8%)
  local copies, waits for them, and re-layouts  9.66 us (6%)
  other arithmetic  2.42 us (1%)
    ppermute x2, waiting for transfers between devices, shift(): lax.ppermute(x, 'leaf', [(i, (i + step) % PEERS) for i in range(PEERS)])  63.6 us
    pallas_call x1, Pallas kernels, near_field(): pl.pallas_call(near_kernel, out_shape=jax.ShapeDtypeStruct((NRHS, LEAVES...  39.3 us
    all_to_all x1, starting transfers between devices, local(): lax.all_to_all(message, 'leaf', split_axis=0, concat_axis=0, tiled=True)  11.9 us
    all_to_all x1, waiting for transfers between devices, local(): lax.all_to_all(message, 'leaf', split_axis=0, concat_axis=0, tiled=True)  8.67 us
    unnamed x33, local copies, waits for them, and re-layouts  8.47 us
    pallas_call x1, Pallas kernels, far_field(): pl.pallas_call(far_kernel, out_shape=jax.ShapeDtypeStruct((NRHS, LEAVES *...  6.52 us
    pallas_call x1, Pallas kernels, pack(): pl.pallas_call(pack_kernel, out_shape=(jax.ShapeDtypeStruct((PEERS, 2, RO...  4.13 us
  transfers between devices with their start and end apart: 4, of which 2 were waited for; matrix products, arithmetic and copies ran while one was open for 2% of the time, Pallas kernels for 27%

profile of v1, /device:TPU:1, one launch (start us, length us, event | category | flops | bytes accessed | tf_op | source)
XLA Modules:
  0.0 163.5 jit_solution(14941176676395007441)
XLA Ops:
  6.5 1.2 copy-done
  7.8 0.9 copy-done.2
  8.7 0.9 copy-done.4
  9.7 0.8 copy-done.8
  10.5 0.8 copy-done.10
  11.3 0.7 copy-done.12
  12.0 1.8 %coefficients.1 = bf16[5,48,128]{2,1,0:T(8,128)(2,1)} custom-call(bf16[16,8192]{1,0:T(8,128)(2,1)S(1)} %copy-done.4, bf16[64,8192]{1,0:T(8,128)(2,1)S(1)} %copy-done, bf16[8,64,256]{2,1,0:T(8,128)(2,1)S(1)} %copy-done.2, bf16[2,64,256]{2,1,0:T(8,128)(2,1)S(1)} %copy-done.8, bf16[32,512]{1,0:T(8,128)(2,1)S(1)} %copy-done.10, bf16[32,128]{1,0:T(8,128)(2,1)S(1)} %copy-done.12), custom_call_target="tpu_custom_call" | custom-call | tf_op jit(solution)/shard_map/coefficients/pallas_call | solution.py:158
  13.8 0.9 copy-done.5
  14.8 1.0 copy-done.6
  15.8 0.9 copy-done.7
  16.8 4.1 %pack.1 = (bf16[128,2,48,256]{3,2,1,0:T(8,128)(2,1)}, bf16[2,48,256]{2,1,0:T(8,128)(2,1)S(1)}, bf16[2,48,256]{2,1,0:T(8,128)(2,1)S(1)}, bf16[32,48,256]{2,1,0:T(8,128)(2,1)S(1)}) custom-call(s32[10,4096]{1,0:T(8,128)S(1)} %bitcast.2, bf16[32,8192]{1,0:T(8,128)(2,1)S(1)} %copy-done.6, bf16[16,8192]{1,0:T(8,128)(2,1)S(1)} %copy-done.5), custom_call_target="tpu_custom_call" | custom-call | tf_op jit(solution)/shard_map/pack/pallas_call | solution.py:102
  20.9 11.9 %all-to-all-start = ((bf16[128,2,48,256]{3,2,1,0:T(8,128)(2,1)}), bf16[128,2,48,256]{3,2,1,0:T(8,128)(2,1)}, u32[]{:S(2)}, u32[]{:S(2)}) async-start(bf16[128,2,48,256]{3,2,1,0:T(8,128)(2,1)} %get-tuple-element.9), calls=%async_computation | async-start | bytes 12582912 | tf_op jit(solution)/shard_map/all_to_all | solution.py:340
  32.8 1.8 %collective-permute-start = (bf16[2,48,256]{2,1,0:T(8,128)(2,1)S(1)}, bf16[2,48,256]{2,1,0:T(8,128)(2,1)S(1)}, u32[]{:S(2)}, u32[]{:S(2)}) collective-permute-start(bf16[2,48,256]{2,1,0:T(8,128)(2,1)S(1)} %get-tuple-element.10), channel_id=1, source_target_pairs={{0,1},{1,2},{2,3},{3,4},{4,5},{5,6},{6,7},{7,8},{8,9},{9,10},{10,1... | collective-permute-start | bytes 147464 | tf_op jit(solution)/shard_map/ppermute | solution.py:329
  34.7 0.8 constant_dynamic-slice_fusion
  35.5 0.1 shift_right_arithmetic.17
  35.7 0.2 select_reduce_fusion.1
  35.9 0.3 select_reduce_fusion
  36.2 0.1 reduce_sum.24
  36.4 0.7 select_reduce_fusion.5
  37.1 1.3 select_select_fusion.row_ref
  38.4 63.6 %collective-permute-done.left_ref = bf16[2,48,256]{2,1,0:T(8,128)(2,1)S(1)} collective-permute-done((bf16[2,48,256]{2,1,0:T(8,128)(2,1)S(1)}, bf16[2,48,256]{2,1,0:T(8,128)(2,1)S(1)}, u32[]{:S(2)}, u32[]{:S(2)}) %collective-permute-start) | collective-permute-done | bytes 49184 | tf_op jit(solution)/shard_map/ppermute | solution.py:329
  102.0 8.7 %all-to-all-done = bf16[128,2,48,256]{3,2,1,0:T(8,128)(2,1)} async-done(((bf16[128,2,48,256]{3,2,1,0:T(8,128)(2,1)}), bf16[128,2,48,256]{3,2,1,0:T(8,128)(2,1)}, u32[]{:S(2)}, u32[]{:S(2)}) %all-to-all-start) | async-done | bytes 6291488 | tf_op jit(solution)/shard_map/all_to_all | solution.py:340
  110.7 39.3 %near_field.1.near_ref = f32[16,8192]{1,0:T(8,128)S(1)} custom-call(s32[320]{0:T(512)S(1)} %select_select_fusion.row_ref, bf16[256,48,256]{2,1,0:T(8,128)(2,1)} %bitcast.1.arrived_ref, bf16[2,48,256]{2,1,0:T(8,128)(2,1)S(1)} %collective-permute-done.left_ref, bf16[2,48,256]{2,1,0:T(8,128)(2,1)S(1)} %collective-permute-done.1.right_ref, ...), custom_call_target="tpu_custom_call" | custom-call | flops 2013265920 | bytes 8388608 | tf_op jit(solution)/shard_map/near_field/pallas_call | solution.py:219
  150.1 6.5 %far_field.1 = bf16[16,8192]{1,0:T(8,128)(2,1)} custom-call(s32[8,8]{1,0:T(8,128)S(1)} %copy-done.14, s32[2,8]{1,0:T(2,128)S(1)} %copy-done.15, bf16[640,48,128]{2,1,0:T(8,128)(2,1)} %all-gather.2.cloned.1.call-done.gathered_ref, bf16[32,512]{1,0:T(8,128)(2,1)S(1)} %copy-done.11, bf16[32,128]{1,0:T(8,128)(2,1)S(1)} %copy-done.13, ...), custom_call_target="tpu_custom_call" | custom-call | tf_op jit(solution)/shard_map/far_field/pallas_call | solution.py:313
  (32 shorter events, 0.4 us)
Async XLA Ops:
  6.5 143.5 %all-gather.2.cloned.1.call-start = ((), (), s32[]{:S(2)}) async-start(), calls=%async_computation.1 | async-start | bytes 7925760 | tf_op jit(solution)/shard_map/all_gather | solution.py:339
  6.5 1.2 copy-start
  7.8 0.9 copy-start.2
  8.7 0.9 copy-start.4
  9.7 0.8 copy-start.8
  10.5 0.8 copy-start.10
  11.3 0.7 copy-start.12
  13.8 1.0 copy-start.5
  14.8 1.0 copy-start.6
  15.8 0.9 copy-start.7
  20.9 89.7 %all-to-all-start = ((bf16[128,2,48,256]{3,2,1,0:T(8,128)(2,1)}), bf16[128,2,48,256]{3,2,1,0:T(8,128)(2,1)}, u32[]{:S(2)}, u32[]{:S(2)}) async-start(bf16[128,2,48,256]{3,2,1,0:T(8,128)(2,1)} %get-tuple-element.9), calls=%async_computation | async-start | bytes 12582912 | tf_op jit(solution)/shard_map/all_to_all | solution.py:340
  32.8 69.2 %collective-permute-start = (bf16[2,48,256]{2,1,0:T(8,128)(2,1)S(1)}, bf16[2,48,256]{2,1,0:T(8,128)(2,1)S(1)}, u32[]{:S(2)}, u32[]{:S(2)}) collective-permute-start(bf16[2,48,256]{2,1,0:T(8,128)(2,1)S(1)} %get-tuple-element.10), channel_id=1, source_target_pairs={{0,1},{1,2},{2,3},{3,4},{4,5},{5,6},{6,7},{7,8},{8,9},{9,10},{10,1... | collective-permute-start | bytes 147464 | tf_op jit(solution)/shard_map/ppermute | solution.py:329
  34.6 67.3 %collective-permute-start.1 = (bf16[2,48,256]{2,1,0:T(8,128)(2,1)S(1)}, bf16[2,48,256]{2,1,0:T(8,128)(2,1)S(1)}, u32[]{:S(2)}, u32[]{:S(2)}) collective-permute-start(bf16[2,48,256]{2,1,0:T(8,128)(2,1)S(1)} %get-tuple-element.11), channel_id=1, source_target_pairs={{0,127},{1,0},{2,1},{3,2},{4,3},{5,4},{6,5},{7,6},{8,7},{9,8},{10,... | collective-permute-start | bytes 147464 | tf_op jit(solution)/shard_map/ppermute | solution.py:329
  110.7 39.4 %copy-start.1 = (bf16[64,8192]{1,0:T(8,128)(2,1)S(1)}, bf16[64,8192]{1,0:T(8,128)(2,1)}, u32[]{:S(2)}) copy-start(bf16[64,8192]{1,0:T(8,128)(2,1)} %basis_ref.3) | copy-start | bytes 3145732
  110.7 39.4 %copy-start.3 = (bf16[8,64,256]{2,1,0:T(8,128)(2,1)S(1)}, bf16[8,64,256]{2,1,0:T(8,128)(2,1)}, u32[]{:S(2)}) copy-start(bf16[8,64,256]{2,1,0:T(8,128)(2,1)} %one_ref.3) | copy-start | bytes 786436
  110.7 39.4 %copy-start.9 = (bf16[2,64,256]{2,1,0:T(8,128)(2,1)S(1)}, bf16[2,64,256]{2,1,0:T(8,128)(2,1)}, u32[]{:S(2)}) copy-start(bf16[2,64,256]{2,1,0:T(8,128)(2,1)} %two_ref.3) | copy-start | bytes 196612
  110.7 39.4 %copy-start.11 = (bf16[32,512]{1,0:T(8,128)(2,1)S(1)}, bf16[32,512]{1,0:T(8,128)(2,1)}, u32[]{:S(2)}) copy-start(bf16[32,512]{1,0:T(8,128)(2,1)} %skel_one_ref.3) | copy-start | bytes 98308
  110.7 39.4 %copy-start.13 = (bf16[32,128]{1,0:T(8,128)(2,1)S(1)}, bf16[32,128]{1,0:T(8,128)(2,1)}, u32[]{:S(2)}) copy-start(bf16[32,128]{1,0:T(8,128)(2,1)} %skel_two_ref.3) | copy-start | bytes 24580
  110.7 39.4 %copy-start.14 = (s32[8,8]{1,0:T(8,128)S(1)}, s32[8,8]{1,0:T(8,128)}, u32[]{:S(2)}) copy-start(s32[8,8]{1,0:T(8,128)} %far_one_ref.1) | copy-start | bytes 772
  110.7 39.4 %copy-start.15 = (s32[2,8]{1,0:T(2,128)S(1)}, s32[2,8]{1,0:T(2,128)}, u32[]{:S(2)}) copy-start(s32[2,8]{1,0:T(2,128)} %far_two_ref.1) | copy-start | bytes 196
Sparse Core Ops, SparseCore 0:
  13.9 131.5 all-gather.1

commit v2 on v1

v2 whole, which is shorter than its diff:
```python
import jax
import jax.numpy as jnp
from jax import lax
from jax.experimental import pallas as pl
from jax.experimental.pallas import tpu as pltpu
from jax.sharding import PartitionSpec as P

DIM = 32
NRHS = 16
RANK = 64
LEAF = 256
NEAR = 10
FAR = 8
LEAVES = 32
ONE = 8
TWO = 2
PAIRS = ONE // 2
ROWS = DIM + NRHS
PEERS = 128
LOCAL = 2 * PEERS + 4
TABLE = LOCAL + LEAVES
GROUP = 16
LIST = 384
STRIDE = 512
HALF_ROWS = ROWS // 2
MESSAGE = ROWS + HALF_ROWS
MIB = 1 << 20

NT = (((1,), (1,)), ((), ()))
NN = (((1,), (0,)), ((), ()))


def dot(a, b, dims=NN):
    return lax.dot_general(a, b, dims, preferred_element_type=jnp.float32)


def vmem(limit=56):
    return pltpu.CompilerParams(vmem_limit_bytes=limit * MIB)


def cost(flops, moved, exps=0):
    return pl.CostEstimate(flops=flops, bytes_accessed=moved, transcendentals=exps)


def fetch(sem, *pairs):
    copies = [pltpu.make_async_copy(a, b, sem.at[i]) for i, (a, b) in enumerate(pairs)]
    for copy in copies:
        copy.start()
    return copies


def bf16(*shape):
    return pltpu.VMEM(shape, jnp.bfloat16)


ANY = pl.BlockSpec(memory_space=pl.ANY)
VM = pl.BlockSpec(memory_space=pltpu.VMEM)
SM = pl.BlockSpec(memory_space=pltpu.SMEM)


def ask_kernel(far_ref, ask_ref, low_ref):
    peer = lax.broadcasted_iota(jnp.int32, (PEERS, FAR), 0) * ONE
    low = high = None
    for i in range(ONE):
        at = far_ref[i : i + 1, :] - peer
        inside = (at >> 3) == 0
        a, b = jnp.where(inside, at, ONE), jnp.where(inside, at, -1)
        low = a if i == 0 else jnp.minimum(low, a)
        high = b if i == 0 else jnp.maximum(high, b)
    low = jnp.min(low.astype(jnp.float32), axis=1, keepdims=True)
    high = jnp.max(high.astype(jnp.float32), axis=1, keepdims=True)
    lane = lax.broadcasted_iota(jnp.int32, (PEERS, PEERS), 1)
    ask_ref[...] = jnp.where(lane == 0, low, high).astype(jnp.int32)
    across = lax.broadcasted_iota(jnp.int32, (ONE, PEERS), 1) * ONE
    low = None
    for j in range(FAR):
        at = far_ref[:, j : j + 1] - across
        a = jnp.where((at >> 3) == 0, at, ONE)
        low = a if j == 0 else jnp.minimum(low, a)
    low = jnp.min(low.astype(jnp.float32), axis=0, keepdims=True)
    low_ref[...] = jnp.broadcast_to(low, (ONE, PEERS)).astype(jnp.int32)


def ask(far_one):
    return pl.pallas_call(
        ask_kernel,
        out_shape=(
            jax.ShapeDtypeStruct((PEERS, PEERS), jnp.int32),
            jax.ShapeDtypeStruct((ONE, PEERS), jnp.int32),
        ),
        in_specs=[VM],
        out_specs=(VM, VM),
        compiler_params=vmem(),
        name="ask",
    )(far_one)


def pack_kernel(
    source_ref, points_ref, rhs_ref, msg_ref, right_ref, left_ref, own_ref,
    lists_ref, block_ref, row_ref, row_smem, in_sem, row_sem, msg_sem, side_sem,
):
    me = lax.axis_index("leaf")
    listed = pltpu.make_async_copy(source_ref, lists_ref, row_sem)
    listed.start()
    filled = fetch(
        in_sem,
        *(
            (ref.at[:, pl.ds(leaf * LEAF, LEAF)], block_ref.at[leaf, rows])
            for leaf in range(LEAVES)
            for ref, rows in ((points_ref, pl.ds(0, DIM)), (rhs_ref, pl.ds(DIM, NRHS)))
        ),
    )
    listed.wait()
    width = PEERS * LEAVES
    low = high = bits = None
    for k in range(NEAR):
        mine = lists_ref[k : k + 1, :] - me * LEAVES
        inside = (mine >> 5) == 0
        a = jnp.where(inside, mine, LEAVES)
        b = jnp.where(inside, mine, -1)
        c = jnp.where(inside, 1 << (mine & 31), 0)
        low = a if k == 0 else jnp.minimum(low, a)
        high = b if k == 0 else jnp.maximum(high, b)
        bits = c if k == 0 else bits | c
    low, high, bits = (jnp.broadcast_to(v, (8, width)) for v in (low, high, bits))
    for step in (16, 8, 4, 2, 1):
        low = jnp.minimum(low, pltpu.roll(low, width - step, 1))
        high = jnp.maximum(high, pltpu.roll(high, width - step, 1))
        bits = bits | pltpu.roll(bits, width - step, 1)
    place = lax.broadcasted_iota(jnp.int32, (8, width), 1) & 31
    row_ref[...] = jnp.where(
        place == 0, low, jnp.where(place == 1, pltpu.roll(high, 1, 1), pltpu.roll(bits, 2, 1))
    )
    copy = pltpu.make_async_copy(row_ref.at[0:1], row_smem, row_sem)
    copy.start()
    for fill in filled:
        fill.wait()
    own = pltpu.make_async_copy(block_ref, own_ref, in_sem.at[0])
    own.start()
    copy.wait()

    def send(peer, _):
        for slot in range(2):
            leaf = row_smem[0, peer * LEAVES + slot] & 31
            pltpu.make_async_copy(block_ref.at[leaf], msg_ref.at[peer, slot], msg_sem).start()
        return 0

    lax.fori_loop(0, PEERS, send, 0, unroll=4)
    for side, (ref, step) in enumerate(((right_ref, 1), (left_ref, PEERS - 1))):
        at = lax.rem(me + step, PEERS) * LEAVES
        between = row_smem[0, at + 2]
        between = between & ~(1 << (row_smem[0, at] & 31)) & ~(1 << (row_smem[0, at + 1] & 31))

        def scan(bit, found):
            has = ((between >> bit) & 1) == 1
            return jnp.where(has & (found[0] < 0), bit, found[0]), jnp.where(has, bit, found[1])

        first, last = lax.fori_loop(0, LEAVES, scan, (jnp.int32(-1), jnp.int32(0)))
        for slot, leaf in enumerate((first & 31, last & 31)):
            pltpu.make_async_copy(block_ref.at[leaf], ref.at[slot], side_sem.at[side]).start()
    pltpu.make_async_copy(msg_ref, msg_ref, msg_sem).wait()
    for side, ref in enumerate((right_ref, left_ref)):
        pltpu.make_async_copy(ref, ref, side_sem.at[side]).wait()
    own.wait()


def pack(source, points, rhs):
    block = jax.ShapeDtypeStruct((LEAVES, ROWS, LEAF), jnp.bfloat16)
    side = jax.ShapeDtypeStruct((2, ROWS, LEAF), jnp.bfloat16)
    return pl.pallas_call(
        pack_kernel,
        out_shape=(
            jax.ShapeDtypeStruct((PEERS, 2, ROWS, LEAF), jnp.bfloat16), side, side, block,
        ),
        in_specs=[ANY, ANY, ANY],
        out_specs=(ANY, ANY, ANY, ANY),
        scratch_shapes=[
            pltpu.VMEM((NEAR, PEERS * LEAVES), jnp.int32),
            bf16(LEAVES, ROWS, LEAF),
            pltpu.VMEM((8, PEERS * LEAVES), jnp.int32),
            pltpu.SMEM((1, PEERS * LEAVES), jnp.int32),
            pltpu.SemaphoreType.DMA((2 * LEAVES,)),
            pltpu.SemaphoreType.DMA,
            pltpu.SemaphoreType.DMA,
            pltpu.SemaphoreType.DMA((2,)),
        ],
        compiler_params=vmem(),
        cost_estimate=cost(1 << 20, 14 * MIB),
        name="pack",
    )(source.T, points, rhs)


def upper(b):
    return jnp.concatenate([b, jnp.zeros_like(b)], axis=0)


def below(b):
    return jnp.concatenate([jnp.zeros_like(b), b], axis=0)


def coeff_kernel(
    rhs_hbm, basis_hbm, one_hbm, two_hbm, skel_one_hbm, skel_two_hbm, out_ref,
    rhs_ref, basis_ref, one_ref, two_ref, skel_one_ref, skel_two_ref, sem,
):
    for copy in fetch(
        sem, (rhs_hbm, rhs_ref), (basis_hbm, basis_ref), (one_hbm, one_ref), (two_hbm, two_ref),
        (skel_one_hbm, skel_one_ref), (skel_two_hbm, skel_two_ref),
    ):
        copy.wait()

    def leaf_pair(leaf):
        a, b = (pl.ds((leaf + i) * LEAF, LEAF) for i in range(2))
        return (
            dot(rhs_ref[:, a], upper(basis_ref[:, a]), NT)
            + dot(rhs_ref[:, b], below(basis_ref[:, b]), NT)
        ).astype(jnp.bfloat16)

    def lift_pair(children, transfer_ref, cluster):
        return (
            dot(children[0], upper(transfer_ref[cluster]), NT)
            + dot(children[1], below(transfer_ref[cluster + 1]), NT)
        ).astype(jnp.bfloat16)

    pairs = []
    for pair in range(PAIRS):
        joined = [
            jnp.concatenate([leaf_pair(4 * c), leaf_pair(4 * c + 2)], axis=1)
            for c in (2 * pair, 2 * pair + 1)
        ]
        pairs.append(lift_pair(joined, one_ref, 2 * pair))
        out_ref[pair, :DIM, :] = skel_one_ref[:, pl.ds(pair * 2 * RANK, 2 * RANK)]
        out_ref[pair, DIM:, :] = pairs[-1]
    joined = [jnp.concatenate(pairs[2 * e : 2 * e + 2], axis=1) for e in range(TWO)]
    out_ref[PAIRS, :DIM, :] = skel_two_ref[...]
    out_ref[PAIRS, DIM:, :] = lift_pair(joined, two_ref, 0)


def coefficients(*args):
    return pl.pallas_call(
        coeff_kernel,
        out_shape=jax.ShapeDtypeStruct((PAIRS + 1, ROWS, 2 * RANK), jnp.bfloat16),
        in_specs=[ANY] * 6,
        out_specs=VM,
        scratch_shapes=[bf16(*a.shape) for a in args] + [pltpu.SemaphoreType.DMA((6,))],
        compiler_params=vmem(),
        cost_estimate=cost(1 << 26, 2 * MIB),
        name="coefficients",
    )(*args)


def far_pack_kernel(asked_ref, columns_ref, out_ref, low_ref, high_ref):
    left = lax.broadcasted_iota(jnp.int32, (ROWS, 2 * RANK), 1) < RANK
    for pair in range(PAIRS):
        wide = columns_ref[pair].astype(jnp.float32)
        turned = pltpu.roll(wide, RANK, 1)
        low_ref[2 * pair] = high_ref[2 * pair + 1] = wide
        low_ref[2 * pair + 1] = high_ref[2 * pair] = turned
    wide = columns_ref[PAIRS].astype(jnp.float32)
    turned = pltpu.roll(wide, RANK, 1)
    half = left[:HALF_ROWS]
    second = (
        jnp.where(half, wide[:HALF_ROWS], turned[HALF_ROWS:]),
        jnp.where(half, turned[:HALF_ROWS], wide[HALF_ROWS:]),
    )

    def fill(chip, _):
        for core in range(2):
            peer = 2 * chip + core
            first = jnp.where(
                left, low_ref[asked_ref[2 * peer] & 7], high_ref[asked_ref[2 * peer + 1] & 7]
            )
            out_ref[peer] = jnp.concatenate([first, second[core]], axis=0).astype(jnp.bfloat16)
        return 0

    lax.fori_loop(0, PEERS // 2, fill, 0, unroll=2)


def far_pack(asked, columns):
    return pl.pallas_call(
        far_pack_kernel,
        out_shape=jax.ShapeDtypeStruct((PEERS, MESSAGE, 2 * RANK), jnp.bfloat16),
        in_specs=[SM, VM],
        out_specs=VM,
        scratch_shapes=[pltpu.VMEM((ONE, ROWS, 2 * RANK), jnp.float32)] * 2,
        compiler_params=vmem(),
        cost_estimate=cost(1 << 20, 5 * MIB),
        name="far_pack",
    )(asked, columns)


def table_rows(near_source, me):
    mine = lax.dynamic_slice_in_dim(near_source, me * LEAVES, LEAVES, 0).reshape(-1)
    device, leaf = mine >> 5, mine & 31
    from_peer = device[:, None] == jnp.arange(PEERS, dtype=jnp.int32)[None, :]
    low = jnp.min(jnp.where(from_peer, leaf[:, None], LEAVES), axis=0)
    high = jnp.max(jnp.where(from_peer, leaf[:, None], -1), axis=0)
    low_of = jnp.sum(jnp.where(from_peer, low[None, :], 0), axis=1)
    high_of = jnp.sum(jnp.where(from_peer, high[None, :], 0), axis=1)
    row = 2 * device + (leaf != low_of)
    inner = (leaf > low_of) & (leaf < high_of)
    for side, step in enumerate((PEERS - 1, 1)):
        chosen = inner & (device == (me + step) % PEERS)
        first = jnp.min(jnp.where(chosen, leaf, LEAVES))
        row = jnp.where(chosen, 2 * PEERS + 2 * side + (leaf != first), row)
    return jnp.where(device == me, LOCAL + leaf, row)


def with_square(block, first):
    wide = block.astype(jnp.float32)
    square = jnp.sum(wide * wide, axis=0, keepdims=True) * -2
    high = square.astype(jnp.bfloat16).astype(jnp.float32)
    middle = (square - high).astype(jnp.bfloat16).astype(jnp.float32)
    low = square - high - middle
    at = lax.broadcasted_iota(jnp.int32, (16, LEAF), 0)
    ones, parts = (3, 0) if first else (0, 3)
    extra = jnp.where((at >= ones) & (at < ones + 3), 1.0, 0.0)
    for i, part in enumerate((high, middle, low)):
        extra = jnp.where(at == parts + i, part, extra)
    if first:
        return jnp.concatenate([wide * 4, extra], axis=0).T.astype(jnp.bfloat16)
    return jnp.concatenate([block, extra.astype(jnp.bfloat16)], axis=0)


def turn_targets(own_ref, target_ref):
    def turn(leaf, _):
        target_ref[leaf, :, :ROWS] = with_square(own_ref[leaf, :DIM, :], True)
        return 0

    lax.fori_loop(0, LEAVES, turn, 0, unroll=2)


def add_pairs(list_ref, start, table_ref, target_ref, out_ref):
    def step(i, _):
        terms = []
        for u in range(GROUP):
            pair = list_ref[start + i * GROUP + u]
            target, row = pair // STRIDE, pair & (STRIDE - 1)
            weights = jnp.exp(
                dot(target_ref[target, :, :ROWS], with_square(table_ref[row, :DIM, :], False))
            ).astype(jnp.bfloat16)
            terms.append((target, dot(table_ref[row, DIM:, :], weights, NT)))
        for target, term in terms:
            columns = pl.ds(pl.multiple_of(target * LEAF, LEAF), LEAF)
            out_ref[:, columns] += term
        return 0

    lax.fori_loop(0, (list_ref[start + LIST - 1] + GROUP - 1) // GROUP, step, 0)


def own_kernel(row_ref, own_hbm, out_ref, list_ref, own_ref, target_ref, sem):
    (copy,) = fetch(sem, (own_hbm, own_ref.at[pl.ds(0, LEAVES)]))

    def sort(target, counts):
        mine, others = counts
        for k in range(NEAR):
            row = row_ref[target * NEAR + k]
            list_ref[mine] = target * STRIDE + jnp.maximum(row - LOCAL, 0)
            list_ref[LIST + others] = target * STRIDE + row
            is_mine = (row >= LOCAL).astype(jnp.int32)
            mine, others = mine + is_mine, others + 1 - is_mine
        return mine, others

    mine, others = lax.fori_loop(0, LEAVES, sort, (jnp.int32(0), jnp.int32(0)))
    for u in range(GROUP):
        list_ref[mine + u] = LEAVES
        list_ref[LIST + others + u] = LOCAL
    list_ref[LIST - 1] = mine
    list_ref[2 * LIST - 1] = others
    own_ref[LEAVES] = jnp.zeros((ROWS, LEAF), jnp.bfloat16)
    copy.wait()
    turn_targets(own_ref, target_ref)
    out_ref[...] = jnp.zeros_like(out_ref)
    add_pairs(list_ref, 0, own_ref, target_ref, out_ref)


def own_pairs(rows, own):
    return pl.pallas_call(
        own_kernel,
        out_shape=(
            jax.ShapeDtypeStruct((NRHS, LEAVES * LEAF), jnp.float32),
            jax.ShapeDtypeStruct((2 * LIST,), jnp.int32),
        ),
        in_specs=[SM, ANY],
        out_specs=(VM, SM),
        scratch_shapes=[
            bf16(LEAVES + 1, ROWS, LEAF),
            bf16(LEAVES, LEAF, 128),
            pltpu.SemaphoreType.DMA((1,)),
        ],
        compiler_params=vmem(),
        cost_estimate=cost(2 * 120 * 65536 * 272, 2 * MIB, 120 * 65536),
        name="own_pairs",
    )(rows, own)


def remote_kernel(
    list_ref, arrived_ref, left_ref, right_ref, own_hbm, field_ref, out_ref,
    table_ref, own_ref, target_ref, sem,
):
    near = fetch(
        sem,
        (own_hbm, own_ref),
        (field_ref, out_ref),
        (arrived_ref, table_ref.at[pl.ds(0, 2 * PEERS)]),
        (left_ref, table_ref.at[pl.ds(2 * PEERS, 2)]),
        (right_ref, table_ref.at[pl.ds(2 * PEERS + 2, 2)]),
    )
    table_ref[LOCAL] = jnp.zeros((ROWS, LEAF), jnp.bfloat16)
    near[0].wait()
    turn_targets(own_ref, target_ref)
    for copy in near[1:]:
        copy.wait()
    add_pairs(list_ref, LIST, table_ref, target_ref, out_ref)


def remote_pairs(lists, arrived, left, right, own, field):
    return pl.pallas_call(
        remote_kernel,
        out_shape=jax.ShapeDtypeStruct((NRHS, LEAVES * LEAF), jnp.float32),
        in_specs=[SM, ANY, ANY, ANY, ANY, ANY],
        out_specs=VM,
        scratch_shapes=[
            bf16(LOCAL + 1, ROWS, LEAF),
            bf16(LEAVES, ROWS, LEAF),
            bf16(LEAVES, LEAF, 128),
            pltpu.SemaphoreType.DMA((5,)),
        ],
        compiler_params=vmem(),
        cost_estimate=cost(2 * 200 * 65536 * 272, 8 * MIB, 200 * 65536),
        name="remote_pairs",
    )(lists, arrived, left, right, own, field)


def turned(skel_ref, pair):
    return skel_ref[:, pl.ds(pair * 2 * RANK, 2 * RANK)].astype(jnp.float32).T


def field_pair(targets, blocks, halves):
    half_of = lax.broadcasted_iota(jnp.int32, (NRHS, 2 * RANK), 1) >> 6
    total = None
    for i, padded in enumerate((upper, below)):
        target = targets[i * RANK : (i + 1) * RANK]
        target_sq = jnp.sum(target * target, axis=1, keepdims=True) * 2
        source = jnp.concatenate([block[:DIM] for block in blocks[i]], axis=1)
        coeffs = jnp.concatenate(
            [
                jnp.where(half_of == half, block[DIM:], 0)
                for block, half in zip(blocks[i], halves[i], strict=True)
            ],
            axis=1,
        )
        wide = source.astype(jnp.float32)
        source_sq = jnp.sum(wide * wide, axis=0, keepdims=True) * 2
        power = dot((target * 4).astype(jnp.bfloat16), source) - target_sq - source_sq
        weights = jnp.exp(power).astype(jnp.bfloat16)
        term = dot(coeffs, padded(weights), NT)
        total = term if i == 0 else total + term
    return total


def far_one_kernel(far_ref, low_ref, arrived_ref, skel_hbm, out_ref, skel_ref, picked_ref, sem, in_sem):
    (copy,) = fetch(in_sem, (skel_hbm, skel_ref))
    for c in range(ONE):
        for j in range(FAR):
            pltpu.make_async_copy(
                arrived_ref.at[far_ref[c, j] >> 3, pl.ds(0, ROWS)], picked_ref.at[c * FAR + j], sem
            ).start()
    copy.wait()
    pltpu.make_async_copy(picked_ref, picked_ref, sem).wait()
    for pair in range(PAIRS):
        clusters = (2 * pair, 2 * pair + 1)
        blocks = [[picked_ref[c * FAR + j] for j in range(FAR)] for c in clusters]
        halves = [
            [
                ((far_ref[c, j] & 7) != low_ref[0, far_ref[c, j] >> 3]).astype(jnp.int32)
                for j in range(FAR)
            ]
            for c in clusters
        ]
        out_ref[pair] = field_pair(turned(skel_ref, pair), blocks, halves)


def far_one_field(far_one, low, arrived, skeleton_one):
    return pl.pallas_call(
        far_one_kernel,
        out_shape=jax.ShapeDtypeStruct((PAIRS, NRHS, 2 * RANK), jnp.float32),
        in_specs=[SM, SM, ANY, ANY],
        out_specs=VM,
        scratch_shapes=[
            bf16(DIM, ONE * RANK),
            bf16(ONE * FAR, ROWS, 2 * RANK),
            pltpu.SemaphoreType.DMA,
            pltpu.SemaphoreType.DMA((1,)),
        ],
        compiler_params=vmem(),
        cost_estimate=cost(1 << 28, 2 * MIB, 1 << 19),
        name="far_one_field",
    )(far_one, low, arrived, skeleton_one)


def final_kernel(
    far_ref, mine_ref, theirs_ref, field_one_hbm, skel_hbm, one_hbm, two_hbm, basis_hbm, near_hbm,
    out_ref, field_one_ref, skel_ref, one_ref, two_ref, basis_ref, near_ref, picked_ref, sem, in_sem,
):
    core = lax.rem(lax.axis_index("leaf"), 2)
    copies = fetch(
        in_sem, (skel_hbm, skel_ref), (field_one_hbm, field_one_ref), (one_hbm, one_ref),
        (two_hbm, two_ref), (basis_hbm, basis_ref), (near_hbm, near_ref),
    )
    for e in range(TWO):
        for j in range(FAR):
            b = far_ref[e, j]
            place = picked_ref.at[e * FAR + j]

            @pl.when((b & 1) == core)
            def _():
                pltpu.make_async_copy(mine_ref.at[b >> 1], place, sem).start()

            @pl.when((b & 1) != core)
            def _():
                pltpu.make_async_copy(theirs_ref.at[b >> 1], place, sem).start()

    for copy in copies:
        copy.wait()
    pltpu.make_async_copy(picked_ref, picked_ref, sem).wait()

    def split(x):
        high = x.astype(jnp.bfloat16)
        return jnp.concatenate([high, (x - high.astype(jnp.float32)).astype(jnp.bfloat16)], axis=0)

    def exact(parts, b):
        both = dot(parts, b)
        return both[:NRHS] + both[NRHS:]

    def whole(at):
        rows = picked_ref[at].astype(jnp.float32)
        return jnp.concatenate([rows, pltpu.roll(rows, RANK, 1)], axis=0).astype(jnp.bfloat16)

    blocks = [[whole(e * FAR + j) for j in range(FAR)] for e in range(TWO)]
    field_two = split(field_pair(turned(skel_ref, 0), blocks, [[0] * FAR] * TWO))
    from_two = [
        exact(field_two, padded(two_ref[e])) for e, padded in enumerate((upper, below))
    ]
    for pair in range(PAIRS):
        parent = from_two[pair // 2][:, (pair % 2) * 2 * RANK : (pair % 2 + 1) * 2 * RANK]
        down_one = split(field_one_ref[pair] + parent)
        for i, padded in enumerate((upper, below)):
            c = 2 * pair + i
            down_leaf = exact(down_one, padded(one_ref[c])).astype(jnp.bfloat16)
            for leaf in range(4):
                columns = pl.ds((4 * c + leaf) * LEAF, LEAF)
                half = down_leaf[:, (leaf // 2) * 2 * RANK : (leaf // 2 + 1) * 2 * RANK]
                basis = (upper, below)[leaf % 2](basis_ref[:, columns])
                out_ref[:, columns] = (near_ref[:, columns] + dot(half, basis)).astype(
                    jnp.bfloat16
                )


def finish(far_two, mine, theirs, field_one, skeleton_two, transfer_one, transfer_two, basis, near):
    scratch = (field_one, skeleton_two, transfer_one, transfer_two, basis, near)
    return pl.pallas_call(
        final_kernel,
        out_shape=jax.ShapeDtypeStruct((NRHS, LEAVES * LEAF), jnp.bfloat16),
        in_specs=[SM] + [ANY] * 8,
        out_specs=VM,
        scratch_shapes=[pltpu.VMEM(a.shape, a.dtype) for a in scratch]
        + [
            bf16(TWO * FAR, HALF_ROWS, 2 * RANK),
            pltpu.SemaphoreType.DMA,
            pltpu.SemaphoreType.DMA((6,)),
        ],
        compiler_params=vmem(),
        cost_estimate=cost(1 << 28, 3 * MIB, 1 << 17),
        name="finish",
    )(far_two, mine, theirs, *scratch)


def shift(x, step):
    return lax.ppermute(x, "leaf", [(i, (i + step) % PEERS) for i in range(PEERS)])


def swap(x):
    return lax.ppermute(x, "leaf", [(i, i ^ 1) for i in range(PEERS)])


def exchange(x):
    return lax.all_to_all(x, "leaf", split_axis=0, concat_axis=0, tiled=True)


def local(
    points, rhs, basis, transfer_one, transfer_two, skeleton_one, skeleton_two, near_source,
    far_one, far_two,
):
    me = lax.axis_index("leaf")
    wanted, low = ask(far_one)
    asked = exchange(wanted.reshape(PEERS, 1, PEERS)).reshape(PEERS, PEERS)
    message, to_right, to_left, own = pack(near_source, points, rhs)
    message, asked = lax.optimization_barrier((message, asked))
    arrived = exchange(message)
    from_left, from_right = shift(to_right, 1), shift(to_left, -1)
    columns = coefficients(rhs, basis, transfer_one, transfer_two, skeleton_one, skeleton_two)
    far_message = far_pack(asked[:, :2].reshape(-1), columns)
    field, lists = own_pairs(table_rows(near_source, me), own)
    far_message, arrived = lax.optimization_barrier((far_message, arrived))
    far_arrived = exchange(far_message)
    near = remote_pairs(
        lists, arrived.reshape(2 * PEERS, ROWS, LEAF), from_left, from_right, own, field
    )
    mine = far_arrived[:, ROWS:, :]
    theirs = swap(mine)
    field_one = far_one_field(far_one, low, far_arrived, skeleton_one)
    return finish(far_two, mine, theirs, field_one, skeleton_two, transfer_one, transfer_two,
                  basis, near)


def solution(mesh):
    placed = (
        P(None, "leaf"),
        P(None, "leaf"),
        P(None, "leaf"),
        P("leaf", None, None),
        P("leaf", None, None),
        P(None, "leaf"),
        P(None, "leaf"),
        P(),
        P("leaf", None),
        P("leaf", None),
    )
    return jax.shard_map(
        local, mesh=mesh, in_specs=placed, out_specs=P(None, "leaf"), check_vma=False
    )
```

time: 164 us -> 199 us (1.21)
  waiting for transfers between devices: 72.3 us -> 99.9 us
  starting transfers between devices: 13.7 us -> 30.2 us
  between operations: 13.6 us -> 0.21 us
  Pallas kernels: 51.8 us -> 61.2 us
  local copies, waits for them, and re-layouts: 9.66 us -> 3.54 us
    all_to_all x1 -> x3, waiting for transfers between devices: 8.67 us -> 99.9 us  [exchange(): return lax.all_to_all(x, 'leaf', split_axis=0, concat_axis=0, tiled=True)]
    ppermute x2, waiting for transfers between devices: 63.6 us -> 0.01 us  [shift(): lax.ppermute(x, 'leaf', [(i, (i + step) % PEERS) for i in range(PEERS)])]
    all_to_all x1 -> x3, starting transfers between devices: 11.9 us -> 26.7 us  [exchange(): return lax.all_to_all(x, 'leaf', split_axis=0, concat_axis=0, tiled=True)]
    pallas_call x3 -> x7, Pallas kernels: 47.7 us -> 55.1 us  [the longest x1 22.5 us: remote_pairs(): pl.pallas_call(remote_kernel, out_shape=jax.ShapeDtypeStruct((NRHS, LEAVE...]
    unnamed x33 -> x15, local copies, waits for them, and re-layouts: 8.47 us -> 1.6 us
    pallas_call x1, Pallas kernels: 4.13 us -> 6.13 us  [pack(): pl.pallas_call(pack_kernel, out_shape=(jax.ShapeDtypeStruct((PEERS, 2, RO...]
  transfers between devices with their start and end apart: 4 -> 6, of which waited for: 2 -> 3; matrix products, arithmetic and copies ran while one was open for 2% -> 3% of each run, Pallas kernels for 27% -> 27%
where the time goes in v2:
time: 199 us; the launch traced here: 198 us
  waiting for transfers between devices  99.9 us (50%)
  Pallas kernels  61.2 us (31%)
  starting transfers between devices  30.2 us (15%)
  local copies, waits for them, and re-layouts  3.54 us (2%)
  other arithmetic  3.07 us (2%)
    all_to_all x3, waiting for transfers between devices, exchange(): return lax.all_to_all(x, 'leaf', split_axis=0, concat_axis=0, tiled=True)  99.9 us
    all_to_all x3, starting transfers between devices, exchange(): return lax.all_to_all(x, 'leaf', split_axis=0, concat_axis=0, tiled=True)  26.7 us
    pallas_call x1, Pallas kernels, remote_pairs(): pl.pallas_call(remote_kernel, out_shape=jax.ShapeDtypeStruct((NRHS, LEAVE...  22.5 us
    pallas_call x1, Pallas kernels, own_pairs(): pl.pallas_call(own_kernel, out_shape=(jax.ShapeDtypeStruct((NRHS, LEAVES...  15.9 us
    pallas_call x1, Pallas kernels, pack(): pl.pallas_call(pack_kernel, out_shape=(jax.ShapeDtypeStruct((PEERS, 2, RO...  6.13 us
    pallas_call x1, Pallas kernels, finish(): pl.pallas_call(final_kernel, out_shape=jax.ShapeDtypeStruct((NRHS, LEAVES...  5.15 us
  transfers between devices with their start and end apart: 6, of which 3 were waited for; matrix products, arithmetic and copies ran while one was open for 3% of the time, Pallas kernels for 27%

profile of v2, /device:TPU:1, one launch (start us, length us, event | category | flops | bytes accessed | tf_op | source)
XLA Modules:
  0.0 198.1 jit_solution(14999041259356441214)
XLA Ops:
  0.0 1.6 ask.1
  1.6 11.5 %all-to-all-start = ((s32[128,1,128]{2,1,0:T(1,128)}), s32[128,1,128]{2,1,0:T(1,128)S(1)}, u32[]{:S(2)}, u32[]{:S(2)}) async-start(s32[128,1,128]{2,1,0:T(1,128)} %bitcast.9), calls=%async_computation | async-start | bytes 131072 | tf_op jit(solution)/shard_map/all_to_all | solution.py:587
  13.1 6.1 %pack.1 = (bf16[128,2,48,256]{3,2,1,0:T(8,128)(2,1)}, bf16[2,48,256]{2,1,0:T(8,128)(2,1)}, bf16[2,48,256]{2,1,0:T(8,128)(2,1)}, bf16[32,48,256]{2,1,0:T(8,128)(2,1)}) custom-call(s32[10,4096]{1,0:T(8,128)} %bitcast.7, bf16[32,8192]{1,0:T(8,128)(2,1)} %points_ref.1, bf16[16,8192]{1,0:T(8,128)(2,1)} %rhs_hbm.1), custom_call_target="tpu_custom_call" | custom-call | flops 1048576 | bytes 14680064 | tf_op jit(solution)/shard_map/pack/pallas_call | solution.py:170
  19.3 3.2 %all-to-all-done = s32[128,1,128]{2,1,0:T(1,128)S(1)} async-done(((s32[128,1,128]{2,1,0:T(1,128)}), s32[128,1,128]{2,1,0:T(1,128)S(1)}, u32[]{:S(2)}, u32[]{:S(2)}) %all-to-all-start) | async-done | bytes 65568 | tf_op jit(solution)/shard_map/all_to_all | solution.py:587
  22.4 7.0 %all-to-all-start.1 = ((bf16[128,2,48,256]{3,2,1,0:T(8,128)(2,1)}), bf16[128,2,48,256]{3,2,1,0:T(8,128)(2,1)}, u32[]{:S(2)}, u32[]{:S(2)}) async-start(bf16[128,2,48,256]{3,2,1,0:T(8,128)(2,1)} %get-tuple-element.20), calls=%async_computation.1 | async-start | bytes 12582912 | tf_op jit(solution)/shard_map/all_to_all | solution.py:587
  29.5 3.3 %coefficients.1.columns_ref = bf16[5,48,128]{2,1,0:T(8,128)(2,1)} custom-call(bf16[16,8192]{1,0:T(8,128)(2,1)} %rhs_hbm.1, bf16[64,8192]{1,0:T(8,128)(2,1)} %basis_hbm.3, bf16[8,64,256]{2,1,0:T(8,128)(2,1)} %one_hbm.3, bf16[2,64,256]{2,1,0:T(8,128)(2,1)} %two_hbm.3, bf16[32,512]{1,0:T(8,128)(2,1)} %skel_hbm.2, bf16[32,128]{1,0:T(8,128)(2,1)} %skel_hbm.3), custom_call_target="tpu_custom_call" | custom-call | flops 67108864 | bytes 2097152 | tf_op jit(solution)/shard_map/coefficients/pallas_call | solution.py:239
  32.7 0.7 reshape.35.asked_ref
  33.4 3.0 %far_pack.1 = bf16[128,72,128]{2,1,0:T(8,128)(2,1)} custom-call(s32[256]{0:T(256)} %reshape.35.asked_ref, bf16[5,48,128]{2,1,0:T(8,128)(2,1)} %coefficients.1.columns_ref), custom_call_target="tpu_custom_call" | custom-call | flops 1048576 | bytes 5242880 | tf_op jit(solution)/shard_map/far_pack/pallas_call | solution.py:279
  36.4 69.9 %all-to-all-done.1 = bf16[128,2,48,256]{3,2,1,0:T(8,128)(2,1)} async-done(((bf16[128,2,48,256]{3,2,1,0:T(8,128)(2,1)}), bf16[128,2,48,256]{3,2,1,0:T(8,128)(2,1)}, u32[]{:S(2)}, u32[]{:S(2)}) %all-to-all-start.1) | async-done | bytes 6291488 | tf_op jit(solution)/shard_map/all_to_all | solution.py:587
  106.3 8.2 %all-to-all-start.2 = ((bf16[128,72,128]{2,1,0:T(8,128)(2,1)}), bf16[128,72,128]{2,1,0:T(8,128)(2,1)S(1)}, u32[]{:S(2)}, u32[]{:S(2)}) async-start(bf16[128,72,128]{2,1,0:T(8,128)(2,1)} %far_pack.1), calls=%async_computation.2 | async-start | bytes 4718592 | tf_op jit(solution)/shard_map/all_to_all | solution.py:587
  114.5 1.8 collective-permute-start.1
  116.3 0.8 constant_dynamic-slice_fusion
  117.4 0.2 select_reduce_fusion.1
  117.6 0.3 select_reduce_fusion
  118.1 0.7 select_reduce_fusion.5
  118.8 1.9 select_select_fusion.row_ref
  120.7 26.8 %all-to-all-done.2.arrived_ref = bf16[128,72,128]{2,1,0:T(8,128)(2,1)S(1)} async-done(((bf16[128,72,128]{2,1,0:T(8,128)(2,1)}), bf16[128,72,128]{2,1,0:T(8,128)(2,1)S(1)}, u32[]{:S(2)}, u32[]{:S(2)}) %all-to-all-start.2) | async-done | bytes 2359328 | tf_op jit(solution)/shard_map/all_to_all | solution.py:587
  147.6 1.7 collective-permute-start
  149.3 15.9 %own_pairs.1 = (f32[16,8192]{1,0:T(8,128)}, s32[768]{0:T(1024)}) custom-call(s32[320]{0:T(512)} %select_select_fusion.row_ref, bf16[32,48,256]{2,1,0:T(8,128)(2,1)} %get-tuple-element.23.own_hbm), custom_call_target="tpu_custom_call" | custom-call | flops 4278190080 | bytes 2097152 | tf_op jit(solution)/shard_map/own_pairs/pallas_call | solution.py:377
  165.3 0.6 copy-done.5
  165.9 22.5 %remote_pairs.1.near_hbm = f32[16,8192]{1,0:T(8,128)} custom-call(s32[768]{0:T(1024)} %get-tuple-element.24.list_ref, bf16[256,48,256]{2,1,0:T(8,128)(2,1)} %bitcast.4.arrived_ref, bf16[2,48,256]{2,1,0:T(8,128)(2,1)} %copy-done.5, bf16[2,48,256]{2,1,0:T(8,128)(2,1)} %copy-done.6, bf16[32,48,256]{2,1,0:T(8,128)(2,1)} %get-tuple-element.23.own_hbm, ...), custom_call_target="tpu_custom_call" | custom-call | flops 7130316800 | bytes 8388608 | tf_op jit(solution)/shard_map/remote_pairs/pallas_call | solution.py:417
  188.4 3.7 %far_one_field.1.field_one_hbm = f32[4,16,128]{2,1,0:T(8,128)} custom-call(s32[8,8]{1,0:T(8,128)} %far_ref.4, s32[8,128]{1,0:T(8,128)} %get-tuple-element.22.low_ref, bf16[128,72,128]{2,1,0:T(8,128)(2,1)} %copy-done, bf16[32,512]{1,0:T(8,128)(2,1)} %skel_hbm.2), custom_call_target="tpu_custom_call" | custom-call | flops 268435456 | bytes 2097152 | tf_op jit(solution)/shard_map/far_one_field/pallas_call | solution.py:484
  192.1 0.9 copy-done.2
  193.0 5.2 %finish.1 = bf16[16,8192]{1,0:T(8,128)(2,1)} custom-call(s32[2,8]{1,0:T(2,128)} %far_ref.5, bf16[128,24,128]{2,1,0:T(8,128)(2,1)} %copy-done.1, bf16[128,24,128]{2,1,0:T(8,128)(2,1)} %copy-done.2, f32[4,16,128]{2,1,0:T(8,128)} %far_one_field.1.field_one_hbm, bf16[32,128]{1,0:T(8,128)(2,1)} %skel_hbm.3, bf16[8,64,256]{2,1,0:T(8,128)(2,1)} %one_hbm.3, ...), custom_call_target="tpu_custom_call" | custom-call | flops 268435456 | bytes 3145728 | tf_op jit(solution)/shard_map/finish/pallas_call | solution.py:561
  (23 shorter events, 0.6 us)
Async XLA Ops:
  1.6 20.8 %all-to-all-start = ((s32[128,1,128]{2,1,0:T(1,128)}), s32[128,1,128]{2,1,0:T(1,128)S(1)}, u32[]{:S(2)}, u32[]{:S(2)}) async-start(s32[128,1,128]{2,1,0:T(1,128)} %bitcast.9), calls=%async_computation | async-start | bytes 131072 | tf_op jit(solution)/shard_map/all_to_all | solution.py:587
  22.4 83.8 %all-to-all-start.1 = ((bf16[128,2,48,256]{3,2,1,0:T(8,128)(2,1)}), bf16[128,2,48,256]{3,2,1,0:T(8,128)(2,1)}, u32[]{:S(2)}, u32[]{:S(2)}) async-start(bf16[128,2,48,256]{3,2,1,0:T(8,128)(2,1)} %get-tuple-element.20), calls=%async_computation.1 | async-start | bytes 12582912 | tf_op jit(solution)/shard_map/all_to_all | solution.py:587
  29.4 85.0 %copy-start.4 = (bf16[2,48,256]{2,1,0:T(8,128)(2,1)S(1)}, bf16[2,48,256]{2,1,0:T(8,128)(2,1)}, u32[]{:S(2)}) copy-start(bf16[2,48,256]{2,1,0:T(8,128)(2,1)} %get-tuple-element.26) | copy-start | bytes 147460
  29.5 86.9 %copy-start.3 = (bf16[2,48,256]{2,1,0:T(8,128)(2,1)S(1)}, bf16[2,48,256]{2,1,0:T(8,128)(2,1)}, u32[]{:S(2)}) copy-start(bf16[2,48,256]{2,1,0:T(8,128)(2,1)} %get-tuple-element.27) | copy-start | bytes 147460
  106.3 41.2 %all-to-all-start.2 = ((bf16[128,72,128]{2,1,0:T(8,128)(2,1)}), bf16[128,72,128]{2,1,0:T(8,128)(2,1)S(1)}, u32[]{:S(2)}, u32[]{:S(2)}) async-start(bf16[128,72,128]{2,1,0:T(8,128)(2,1)} %far_pack.1), calls=%async_computation.2 | async-start | bytes 4718592 | tf_op jit(solution)/shard_map/all_to_all | solution.py:587
  114.5 50.8 %collective-permute-start.1 = (bf16[2,48,256]{2,1,0:T(8,128)(2,1)S(1)}, bf16[2,48,256]{2,1,0:T(8,128)(2,1)S(1)}, u32[]{:S(2)}, u32[]{:S(2)}) collective-permute-start(bf16[2,48,256]{2,1,0:T(8,128)(2,1)S(1)} %copy-done.4), channel_id=1, source_target_pairs={{0,1},{1,2},{2,3},{3,4},{4,5},{5,6},{6,7},{7,8},{8,9},{9,10},{10,1... | collective-permute-start | bytes 147464 | tf_op jit(solution)/shard_map/ppermute | solution.py:579
  116.3 49.0 %collective-permute-start.2 = (bf16[2,48,256]{2,1,0:T(8,128)(2,1)S(1)}, bf16[2,48,256]{2,1,0:T(8,128)(2,1)S(1)}, u32[]{:S(2)}, u32[]{:S(2)}) collective-permute-start(bf16[2,48,256]{2,1,0:T(8,128)(2,1)S(1)} %copy-done.3), channel_id=1, source_target_pairs={{0,127},{1,0},{2,1},{3,2},{4,3},{5,4},{6,5},{7,6},{8,7},{9,8},{10,... | collective-permute-start | bytes 147464 | tf_op jit(solution)/shard_map/ppermute | solution.py:579
  147.5 17.7 %copy-start = (bf16[128,72,128]{2,1,0:T(8,128)(2,1)}, bf16[128,72,128]{2,1,0:T(8,128)(2,1)S(1)}, u32[]{:S(2)}) copy-start(bf16[128,72,128]{2,1,0:T(8,128)(2,1)S(1)} %all-to-all-done.2.arrived_ref) | copy-start | bytes 7077892
  147.6 17.7 %copy-start.1 = (bf16[128,24,128]{2,1,0:T(8,128)(2,1)}, bf16[128,24,128]{2,1,0:T(8,128)(2,1)S(1)}, u32[]{:S(2)}) copy-start(bf16[128,24,128]{2,1,0:T(8,128)(2,1)S(1)} %slice.8.mine_ref) | copy-start | bytes 2359300
  147.6 44.5 %collective-permute-start = (bf16[128,24,128]{2,1,0:T(8,128)(2,1)S(1)}, bf16[128,24,128]{2,1,0:T(8,128)(2,1)S(1)}, u32[]{:S(2)}, u32[]{:S(2)}) collective-permute-start(bf16[128,24,128]{2,1,0:T(8,128)(2,1)S(1)} %slice.8.mine_ref), channel_id=1, source_target_pairs={{0,1},{1,0},{2,3},{3,2},{4,5},{5,4},{6,7},{7,6},{8,9},{9,8},{10,11... | collective-permute-start | bytes 2359304 | tf_op jit(solution)/shard_map/ppermute | solution.py:583
  165.3 0.6 copy-start.5
  165.3 0.6 copy-start.6
  192.1 0.9 copy-start.2

commit v3 on v2

--- a/solution.py
+++ b/solution.py
@@ -597,15 +597,21 @@
     message, to_right, to_left, own = pack(near_source, points, rhs)
     message, asked = lax.optimization_barrier((message, asked))
     arrived = exchange(message)
-    from_left, from_right = shift(to_right, 1), shift(to_left, -1)
     columns = coefficients(rhs, basis, transfer_one, transfer_two, skeleton_one, skeleton_two)
     far_message = far_pack(asked[:, :2].reshape(-1), columns)
     field, lists = own_pairs(table_rows(near_source, me), own)
-    far_message, arrived = lax.optimization_barrier((far_message, arrived))
+    to_right, to_left, far_message, field, lists = lax.optimization_barrier(
+        (to_right, to_left, far_message, field, lists)
+    )
+    from_left, from_right = shift(to_right, 1), shift(to_left, -1)
+    far_message, arrived, from_left, from_right = lax.optimization_barrier(
+        (far_message, arrived, from_left, from_right)
+    )
     far_arrived = exchange(far_message)
     near = remote_pairs(
         lists, arrived.reshape(2 * PEERS, ROWS, LEAF), from_left, from_right, own, field
     )
+    far_arrived, near = lax.optimization_barrier((far_arrived, near))
     mine = far_arrived[:, ROWS:, :]
     theirs = swap(mine)
     field_one = far_one_field(far_one, low, far_arrived, skeleton_one)

time: 199 us -> 160 us (0.80)
  waiting for transfers between devices: 99.9 us -> 62.5 us
    all_to_all x3, waiting for transfers between devices: 99.9 us -> 24 us  [exchange(): return lax.all_to_all(x, 'leaf', split_axis=0, concat_axis=0, tiled=True)]
    ppermute x2, waiting for transfers between devices: 0.01 us -> 38.5 us  [shift(): lax.ppermute(x, 'leaf', [(i, (i + step) % PEERS) for i in range(PEERS)])]
  transfers between devices with their start and end apart: 6 -> 6, of which waited for: 3 -> 4; matrix products, arithmetic and copies ran while one was open for 3% -> 3% of each run, Pallas kernels for 27% -> 34%
where the time goes in v3:
time: 160 us; the launch traced here: 159 us
  waiting for transfers between devices  62.5 us (39%)
  Pallas kernels  61.4 us (38%)
  starting transfers between devices  28.6 us (18%)
  other arithmetic  3.08 us (2%)
  local copies, waits for them, and re-layouts  3 us (2%)
    ppermute x2, waiting for transfers between devices, shift(): lax.ppermute(x, 'leaf', [(i, (i + step) % PEERS) for i in range(PEERS)])  38.5 us
    all_to_all x3, starting transfers between devices, exchange(): return lax.all_to_all(x, 'leaf', split_axis=0, concat_axis=0, tiled=True)  26.7 us
    all_to_all x3, waiting for transfers between devices, exchange(): return lax.all_to_all(x, 'leaf', split_axis=0, concat_axis=0, tiled=True)  24 us
    pallas_call x1, Pallas kernels, remote_pairs(): pl.pallas_call(remote_kernel, out_shape=jax.ShapeDtypeStruct((NRHS, LEAVE...  21.1 us
    pallas_call x1, Pallas kernels, own_pairs(): pl.pallas_call(own_kernel, out_shape=(jax.ShapeDtypeStruct((NRHS, LEAVES...  17.4 us
    pallas_call x1, Pallas kernels, pack(): pl.pallas_call(pack_kernel, out_shape=(jax.ShapeDtypeStruct((PEERS, 2, RO...  6.17 us
    pallas_call x1, Pallas kernels, finish(): pl.pallas_call(final_kernel, out_shape=jax.ShapeDtypeStruct((NRHS, LEAVES...  5.15 us
    pallas_call x1, Pallas kernels, far_one_field(): pl.pallas_call(far_one_kernel, out_shape=jax.ShapeDtypeStruct((PAIRS, NRH...  3.69 us
  transfers between devices with their start and end apart: 6, of which 4 were waited for; matrix products, arithmetic and copies ran while one was open for 3% of the time, Pallas kernels for 34%

profile of v3, /device:TPU:1, one launch (start us, length us, event | category | flops | bytes accessed | tf_op | source)
XLA Modules:
  0.0 158.8 jit_solution(17377587019820215759)
XLA Ops:
  0.0 1.6 %ask.1 = (s32[128,128]{1,0:T(8,128)}, s32[8,128]{1,0:T(8,128)}) custom-call(s32[8,8]{1,0:T(8,128)} %far_ref.4), custom_call_target="tpu_custom_call" | custom-call | tf_op jit(solution)/shard_map/ask/pallas_call | solution.py:85
  1.6 11.5 %all-to-all-start = ((s32[128,1,128]{2,1,0:T(1,128)}), s32[128,1,128]{2,1,0:T(1,128)S(1)}, u32[]{:S(2)}, u32[]{:S(2)}) async-start(s32[128,1,128]{2,1,0:T(1,128)} %bitcast.9), calls=%async_computation | async-start | bytes 131072 | tf_op jit(solution)/shard_map/all_to_all | solution.py:587
  13.1 6.2 %pack.1 = (bf16[128,2,48,256]{3,2,1,0:T(8,128)(2,1)}, bf16[2,48,256]{2,1,0:T(8,128)(2,1)}, bf16[2,48,256]{2,1,0:T(8,128)(2,1)}, bf16[32,48,256]{2,1,0:T(8,128)(2,1)}) custom-call(s32[10,4096]{1,0:T(8,128)} %bitcast.7, bf16[32,8192]{1,0:T(8,128)(2,1)} %points_ref.1, bf16[16,8192]{1,0:T(8,128)(2,1)} %rhs_hbm.1), custom_call_target="tpu_custom_call" | custom-call | flops 1048576 | bytes 14680064 | tf_op jit(solution)/shard_map/pack/pallas_call | solution.py:170
  19.3 3.2 %all-to-all-done = s32[128,1,128]{2,1,0:T(1,128)S(1)} async-done(((s32[128,1,128]{2,1,0:T(1,128)}), s32[128,1,128]{2,1,0:T(1,128)S(1)}, u32[]{:S(2)}, u32[]{:S(2)}) %all-to-all-start) | async-done | bytes 65568 | tf_op jit(solution)/shard_map/all_to_all | solution.py:587
  22.4 7.0 %all-to-all-start.1 = ((bf16[128,2,48,256]{3,2,1,0:T(8,128)(2,1)}), bf16[128,2,48,256]{3,2,1,0:T(8,128)(2,1)}, u32[]{:S(2)}, u32[]{:S(2)}) async-start(bf16[128,2,48,256]{3,2,1,0:T(8,128)(2,1)} %get-tuple-element.35), calls=%async_computation.1 | async-start | bytes 12582912 | tf_op jit(solution)/shard_map/all_to_all | solution.py:587
  29.5 0.8 constant_dynamic-slice_fusion
  30.6 0.2 select_reduce_fusion.1
  30.8 0.3 select_reduce_fusion
  31.3 3.3 %coefficients.1.columns_ref = bf16[5,48,128]{2,1,0:T(8,128)(2,1)} custom-call(bf16[16,8192]{1,0:T(8,128)(2,1)} %rhs_hbm.1, bf16[64,8192]{1,0:T(8,128)(2,1)} %basis_hbm.3, bf16[8,64,256]{2,1,0:T(8,128)(2,1)} %one_hbm.3, bf16[2,64,256]{2,1,0:T(8,128)(2,1)} %two_hbm.3, bf16[32,512]{1,0:T(8,128)(2,1)} %skel_hbm.2, bf16[32,128]{1,0:T(8,128)(2,1)} %skel_hbm.3), custom_call_target="tpu_custom_call" | custom-call | flops 67108864 | bytes 2097152 | tf_op jit(solution)/shard_map/coefficients/pallas_call | solution.py:239
  34.5 0.7 select_reduce_fusion.5
  35.3 1.9 %select_select_fusion.row_ref = s32[320]{0:T(512)} fusion(s32[320]{0:T(512)S(1)} %shift_right_arithmetic.17, s32[320]{0:T(512)S(1)} %and.46, s32[320]{0:T(512)S(1)} %get-tuple-element.52, s32[320]{0:T(512)S(1)} %get-tuple-element.51, s32[]{:T(128)} %get-tuple-element.48, s32[]{:T(128)S(6)} %select_n.55, s32[]{:T(128)} %get-tuple-element.47, ...), kind=kLoop, calls=%fused_computation.10 | loop fusion | flops 7040 | bytes 6420 | tf_op jit(solution)/shard_map/jit(_where)/select_n | solution.py:305
  37.2 17.4 %own_pairs.1 = (f32[16,8192]{1,0:T(8,128)}, s32[768]{0:T(1024)}) custom-call(s32[320]{0:T(512)} %select_select_fusion.row_ref, bf16[32,48,256]{2,1,0:T(8,128)(2,1)} %get-tuple-element.31.own_hbm), custom_call_target="tpu_custom_call" | custom-call | flops 4278190080 | bytes 2097152 | tf_op jit(solution)/shard_map/own_pairs/pallas_call | solution.py:377
  54.6 0.7 reshape.35.asked_ref
  55.3 3.0 %far_pack.1 = bf16[128,72,128]{2,1,0:T(8,128)(2,1)} custom-call(s32[256]{0:T(256)} %reshape.35.asked_ref, bf16[5,48,128]{2,1,0:T(8,128)(2,1)} %coefficients.1.columns_ref), custom_call_target="tpu_custom_call" | custom-call | flops 1048576 | bytes 5242880 | tf_op jit(solution)/shard_map/far_pack/pallas_call | solution.py:279
  58.3 0.4 collective-permute-start
  58.8 38.5 %collective-permute-done.left_ref = bf16[2,48,256]{2,1,0:T(8,128)(2,1)S(1)} collective-permute-done((bf16[2,48,256]{2,1,0:T(8,128)(2,1)S(1)}, bf16[2,48,256]{2,1,0:T(8,128)(2,1)S(1)}, u32[]{:S(2)}, u32[]{:S(2)}) %collective-permute-start) | collective-permute-done | bytes 49184 | tf_op jit(solution)/shard_map/ppermute | solution.py:579
  97.3 8.9 %all-to-all-done.1 = bf16[128,2,48,256]{3,2,1,0:T(8,128)(2,1)} async-done(((bf16[128,2,48,256]{3,2,1,0:T(8,128)(2,1)}), bf16[128,2,48,256]{3,2,1,0:T(8,128)(2,1)}, u32[]{:S(2)}, u32[]{:S(2)}) %all-to-all-start.1) | async-done | bytes 6291488 | tf_op jit(solution)/shard_map/all_to_all | solution.py:587
  106.3 8.2 %all-to-all-start.2 = ((bf16[128,72,128]{2,1,0:T(8,128)(2,1)}), bf16[128,72,128]{2,1,0:T(8,128)(2,1)S(1)}, u32[]{:S(2)}, u32[]{:S(2)}) async-start(bf16[128,72,128]{2,1,0:T(8,128)(2,1)} %far_pack.1), calls=%async_computation.2 | async-start | bytes 4718592 | tf_op jit(solution)/shard_map/all_to_all | solution.py:587
  114.5 21.1 %remote_pairs.1.near_hbm = f32[16,8192]{1,0:T(8,128)} custom-call(s32[768]{0:T(1024)} %get-tuple-element.39.list_ref, bf16[256,48,256]{2,1,0:T(8,128)(2,1)} %bitcast.4.arrived_ref, bf16[2,48,256]{2,1,0:T(8,128)(2,1)} %copy-done.5, bf16[2,48,256]{2,1,0:T(8,128)(2,1)} %copy-done.6, bf16[32,48,256]{2,1,0:T(8,128)(2,1)} %get-tuple-element.31.own_hbm, ...), custom_call_target="tpu_custom_call" | custom-call | flops 7130316800 | bytes 8388608 | tf_op jit(solution)/shard_map/remote_pairs/pallas_call | solution.py:417
  135.7 11.9 %all-to-all-done.2.arrived_ref = bf16[128,72,128]{2,1,0:T(8,128)(2,1)S(1)} async-done(((bf16[128,72,128]{2,1,0:T(8,128)(2,1)}), bf16[128,72,128]{2,1,0:T(8,128)(2,1)S(1)}, u32[]{:S(2)}, u32[]{:S(2)}) %all-to-all-start.2) | async-done | bytes 2359328 | tf_op jit(solution)/shard_map/all_to_all | solution.py:587
  147.6 1.4 collective-permute-start.2
  149.0 3.7 %far_one_field.1.field_one_hbm = f32[4,16,128]{2,1,0:T(8,128)} custom-call(s32[8,8]{1,0:T(8,128)} %far_ref.4, s32[8,128]{1,0:T(8,128)} %get-tuple-element.45.low_ref, bf16[128,72,128]{2,1,0:T(8,128)(2,1)} %copy-done, bf16[32,512]{1,0:T(8,128)(2,1)} %skel_hbm.2), custom_call_target="tpu_custom_call" | custom-call | flops 268435456 | bytes 2097152 | tf_op jit(solution)/shard_map/far_one_field/pallas_call | solution.py:484
  152.7 0.9 copy-done.2
  153.6 5.2 %finish.1 = bf16[16,8192]{1,0:T(8,128)(2,1)} custom-call(s32[2,8]{1,0:T(2,128)} %far_ref.5, bf16[128,24,128]{2,1,0:T(8,128)(2,1)} %copy-done.1, bf16[128,24,128]{2,1,0:T(8,128)(2,1)} %copy-done.2, f32[4,16,128]{2,1,0:T(8,128)} %far_one_field.1.field_one_hbm, bf16[32,128]{1,0:T(8,128)(2,1)} %skel_hbm.3, bf16[8,64,256]{2,1,0:T(8,128)(2,1)} %one_hbm.3, ...), custom_call_target="tpu_custom_call" | custom-call | flops 268435456 | bytes 3145728 | tf_op jit(solution)/shard_map/finish/pallas_call | solution.py:561
  (23 shorter events, 0.7 us)
Async XLA Ops:
  1.6 20.8 %all-to-all-start = ((s32[128,1,128]{2,1,0:T(1,128)}), s32[128,1,128]{2,1,0:T(1,128)S(1)}, u32[]{:S(2)}, u32[]{:S(2)}) async-start(s32[128,1,128]{2,1,0:T(1,128)} %bitcast.9), calls=%async_computation | async-start | bytes 131072 | tf_op jit(solution)/shard_map/all_to_all | solution.py:587
  22.4 83.8 %all-to-all-start.1 = ((bf16[128,2,48,256]{3,2,1,0:T(8,128)(2,1)}), bf16[128,2,48,256]{3,2,1,0:T(8,128)(2,1)}, u32[]{:S(2)}, u32[]{:S(2)}) async-start(bf16[128,2,48,256]{3,2,1,0:T(8,128)(2,1)} %get-tuple-element.35), calls=%async_computation.1 | async-start | bytes 12582912 | tf_op jit(solution)/shard_map/all_to_all | solution.py:587
  37.2 21.1 %copy-start.4 = (bf16[2,48,256]{2,1,0:T(8,128)(2,1)S(1)}, bf16[2,48,256]{2,1,0:T(8,128)(2,1)}, u32[]{:S(2)}) copy-start(bf16[2,48,256]{2,1,0:T(8,128)(2,1)} %get-tuple-element.36) | copy-start | bytes 147460
  37.2 21.5 %copy-start.3 = (bf16[2,48,256]{2,1,0:T(8,128)(2,1)S(1)}, bf16[2,48,256]{2,1,0:T(8,128)(2,1)}, u32[]{:S(2)}) copy-start(bf16[2,48,256]{2,1,0:T(8,128)(2,1)} %get-tuple-element.37) | copy-start | bytes 147460
  58.3 39.0 %collective-permute-start = (bf16[2,48,256]{2,1,0:T(8,128)(2,1)S(1)}, bf16[2,48,256]{2,1,0:T(8,128)(2,1)S(1)}, u32[]{:S(2)}, u32[]{:S(2)}) collective-permute-start(bf16[2,48,256]{2,1,0:T(8,128)(2,1)S(1)} %copy-done.4), channel_id=1, source_target_pairs={{0,1},{1,2},{2,3},{3,4},{4,5},{5,6},{6,7},{7,8},{8,9},{9,10},{10,1... | collective-permute-start | bytes 147464 | tf_op jit(solution)/shard_map/ppermute | solution.py:579
  58.7 38.6 %collective-permute-start.1 = (bf16[2,48,256]{2,1,0:T(8,128)(2,1)S(1)}, bf16[2,48,256]{2,1,0:T(8,128)(2,1)S(1)}, u32[]{:S(2)}, u32[]{:S(2)}) collective-permute-start(bf16[2,48,256]{2,1,0:T(8,128)(2,1)S(1)} %copy-done.3), channel_id=1, source_target_pairs={{0,127},{1,0},{2,1},{3,2},{4,3},{5,4},{6,5},{7,6},{8,7},{9,8},{10,... | collective-permute-start | bytes 147464 | tf_op jit(solution)/shard_map/ppermute | solution.py:579
  97.3 17.2 %copy-start.5 = (bf16[2,48,256]{2,1,0:T(8,128)(2,1)}, bf16[2,48,256]{2,1,0:T(8,128)(2,1)S(1)}, u32[]{:S(2)}) copy-start(bf16[2,48,256]{2,1,0:T(8,128)(2,1)S(1)} %collective-permute-done.left_ref) | copy-start | bytes 147460
  97.3 17.2 %copy-start.6 = (bf16[2,48,256]{2,1,0:T(8,128)(2,1)}, bf16[2,48,256]{2,1,0:T(8,128)(2,1)S(1)}, u32[]{:S(2)}) copy-start(bf16[2,48,256]{2,1,0:T(8,128)(2,1)S(1)} %collective-permute-done.1.right_ref) | copy-start | bytes 147460
  106.3 41.2 %all-to-all-start.2 = ((bf16[128,72,128]{2,1,0:T(8,128)(2,1)}), bf16[128,72,128]{2,1,0:T(8,128)(2,1)S(1)}, u32[]{:S(2)}, u32[]{:S(2)}) async-start(bf16[128,72,128]{2,1,0:T(8,128)(2,1)} %far_pack.1), calls=%async_computation.2 | async-start | bytes 4718592 | tf_op jit(solution)/shard_map/all_to_all | solution.py:587
  147.5 1.5 copy-start
  147.6 5.1 %copy-start.1 = (bf16[128,24,128]{2,1,0:T(8,128)(2,1)}, bf16[128,24,128]{2,1,0:T(8,128)(2,1)S(1)}, u32[]{:S(2)}) copy-start(bf16[128,24,128]{2,1,0:T(8,128)(2,1)S(1)} %slice.7.mine_ref) | copy-start | bytes 2359300
  147.6 5.1 %collective-permute-start.2 = (bf16[128,24,128]{2,1,0:T(8,128)(2,1)S(1)}, bf16[128,24,128]{2,1,0:T(8,128)(2,1)S(1)}, u32[]{:S(2)}, u32[]{:S(2)}) collective-permute-start(bf16[128,24,128]{2,1,0:T(8,128)(2,1)S(1)} %slice.7.mine_ref), channel_id=1, source_target_pairs={{0,1},{1,0},{2,3},{3,2},{4,5},{5,4},{6,7},{7,6},{8,9},{9,8},{10,11... | collective-permute-start | bytes 2359304 | tf_op jit(solution)/shard_map/ppermute | solution.py:583
  152.7 0.9 copy-start.2

commit v4 on v3

--- a/solution.py
+++ b/solution.py
@@ -34,7 +34,7 @@
     return lax.dot_general(a, b, dims, preferred_element_type=jnp.float32)
 
 
-def vmem(limit=56):
+def vmem(limit):
     return pltpu.CompilerParams(vmem_limit_bytes=limit * MIB)
 
 
@@ -90,7 +90,7 @@
         ),
         in_specs=[VM],
         out_specs=(VM, VM),
-        compiler_params=vmem(),
+        compiler_params=vmem(8),
         name="ask",
     )(far_one)
 
@@ -184,7 +184,7 @@
             pltpu.SemaphoreType.DMA,
             pltpu.SemaphoreType.DMA((2,)),
         ],
-        compiler_params=vmem(),
+        compiler_params=vmem(56),
         cost_estimate=cost(1 << 20, 14 * MIB),
         name="pack",
     )(source.T, points, rhs)
@@ -242,7 +242,7 @@
         in_specs=[ANY] * 6,
         out_specs=VM,
         scratch_shapes=[bf16(*a.shape) for a in args] + [pltpu.SemaphoreType.DMA((6,))],
-        compiler_params=vmem(),
+        compiler_params=vmem(24),
         cost_estimate=cost(1 << 26, 2 * MIB),
         name="coefficients",
     )(*args)
@@ -282,7 +282,7 @@
         in_specs=[SM, VM],
         out_specs=VM,
         scratch_shapes=[pltpu.VMEM((ONE, ROWS, 2 * RANK), jnp.float32)] * 2,
-        compiler_params=vmem(),
+        compiler_params=vmem(16),
         cost_estimate=cost(1 << 20, 5 * MIB),
         name="far_pack",
     )(asked, columns)
@@ -387,7 +387,7 @@
             bf16(LEAVES, LEAF, 128),
             pltpu.SemaphoreType.DMA((1,)),
         ],
-        compiler_params=vmem(),
+        compiler_params=vmem(24),
         cost_estimate=cost(2 * 120 * 65536 * 272, 2 * MIB, 120 * 65536),
         name="own_pairs",
     )(rows, own)
@@ -425,7 +425,7 @@
             bf16(LEAVES, LEAF, 128),
             pltpu.SemaphoreType.DMA((5,)),
         ],
-        compiler_params=vmem(),
+        compiler_params=vmem(32),
         cost_estimate=cost(2 * 200 * 65536 * 272, 8 * MIB, 200 * 65536),
         name="remote_pairs",
     )(lists, arrived, left, right, own, field)
@@ -458,18 +458,14 @@
     return total
 
 
-def far_one_kernel(far_ref, low_ref, arrived_ref, skel_hbm, out_ref, skel_ref, picked_ref, sem, in_sem):
+def far_one_kernel(far_ref, low_ref, arrived_ref, skel_hbm, out_ref, skel_ref, in_sem):
     (copy,) = fetch(in_sem, (skel_hbm, skel_ref))
-    for c in range(ONE):
-        for j in range(FAR):
-            pltpu.make_async_copy(
-                arrived_ref.at[far_ref[c, j] >> 3, pl.ds(0, ROWS)], picked_ref.at[c * FAR + j], sem
-            ).start()
     copy.wait()
-    pltpu.make_async_copy(picked_ref, picked_ref, sem).wait()
     for pair in range(PAIRS):
         clusters = (2 * pair, 2 * pair + 1)
-        blocks = [[picked_ref[c * FAR + j] for j in range(FAR)] for c in clusters]
+        blocks = [
+            [arrived_ref[far_ref[c, j] >> 3, :ROWS, :] for j in range(FAR)] for c in clusters
+        ]
         halves = [
             [
                 ((far_ref[c, j] & 7) != low_ref[0, far_ref[c, j] >> 3]).astype(jnp.int32)
@@ -484,45 +480,23 @@
     return pl.pallas_call(
         far_one_kernel,
         out_shape=jax.ShapeDtypeStruct((PAIRS, NRHS, 2 * RANK), jnp.float32),
-        in_specs=[SM, SM, ANY, ANY],
+        in_specs=[SM, SM, VM, ANY],
         out_specs=VM,
-        scratch_shapes=[
-            bf16(DIM, ONE * RANK),
-            bf16(ONE * FAR, ROWS, 2 * RANK),
-            pltpu.SemaphoreType.DMA,
-            pltpu.SemaphoreType.DMA((1,)),
-        ],
-        compiler_params=vmem(),
+        scratch_shapes=[bf16(DIM, ONE * RANK), pltpu.SemaphoreType.DMA((1,))],
+        compiler_params=vmem(16),
         cost_estimate=cost(1 << 28, 2 * MIB, 1 << 19),
         name="far_one_field",
     )(far_one, low, arrived, skeleton_one)
 
 
 def final_kernel(
-    far_ref, mine_ref, theirs_ref, field_one_hbm, skel_hbm, one_hbm, two_hbm, basis_hbm, near_hbm,
-    out_ref, field_one_ref, skel_ref, one_ref, two_ref, basis_ref, near_ref, picked_ref, sem, in_sem,
+    far_ref, mine_ref, theirs_ref, field_one_ref, near_ref, skel_hbm, one_hbm, two_hbm, basis_hbm,
+    out_ref, skel_ref, one_ref, two_ref, basis_ref, in_sem,
 ):
     core = lax.rem(lax.axis_index("leaf"), 2)
-    copies = fetch(
-        in_sem, (skel_hbm, skel_ref), (field_one_hbm, field_one_ref), (one_hbm, one_ref),
-        (two_hbm, two_ref), (basis_hbm, basis_ref), (near_hbm, near_ref),
-    )
-    for e in range(TWO):
-        for j in range(FAR):
-            b = far_ref[e, j]
-            place = picked_ref.at[e * FAR + j]
-
-            @pl.when((b & 1) == core)
-            def _():
-                pltpu.make_async_copy(mine_ref.at[b >> 1], place, sem).start()
-
-            @pl.when((b & 1) != core)
-            def _():
-                pltpu.make_async_copy(theirs_ref.at[b >> 1], place, sem).start()
-
-    for copy in copies:
-        copy.wait()
-    pltpu.make_async_copy(picked_ref, picked_ref, sem).wait()
+    skel_copy, two_copy, one_copy, basis_copy = fetch(
+        in_sem, (skel_hbm, skel_ref), (two_hbm, two_ref), (one_hbm, one_ref), (basis_hbm, basis_ref)
+    )
 
     def split(x):
         high = x.astype(jnp.bfloat16)
@@ -532,47 +506,45 @@
         both = dot(parts, b)
         return both[:NRHS] + both[NRHS:]
 
-    def whole(at):
-        rows = picked_ref[at].astype(jnp.float32)
+    def whole(e, j):
+        b = far_ref[e, j]
+        rows = jnp.where((b & 1) == core, mine_ref[b >> 1], theirs_ref[b >> 1]).astype(jnp.float32)
         return jnp.concatenate([rows, pltpu.roll(rows, RANK, 1)], axis=0).astype(jnp.bfloat16)
 
-    blocks = [[whole(e * FAR + j) for j in range(FAR)] for e in range(TWO)]
+    blocks = [[whole(e, j) for j in range(FAR)] for e in range(TWO)]
+    skel_copy.wait()
     field_two = split(field_pair(turned(skel_ref, 0), blocks, [[0] * FAR] * TWO))
+    two_copy.wait()
     from_two = [
         exact(field_two, padded(two_ref[e])) for e, padded in enumerate((upper, below))
     ]
+    one_copy.wait()
+    down_leaf = []
     for pair in range(PAIRS):
         parent = from_two[pair // 2][:, (pair % 2) * 2 * RANK : (pair % 2 + 1) * 2 * RANK]
         down_one = split(field_one_ref[pair] + parent)
         for i, padded in enumerate((upper, below)):
-            c = 2 * pair + i
-            down_leaf = exact(down_one, padded(one_ref[c])).astype(jnp.bfloat16)
-            for leaf in range(4):
-                columns = pl.ds((4 * c + leaf) * LEAF, LEAF)
-                half = down_leaf[:, (leaf // 2) * 2 * RANK : (leaf // 2 + 1) * 2 * RANK]
-                basis = (upper, below)[leaf % 2](basis_ref[:, columns])
-                out_ref[:, columns] = (near_ref[:, columns] + dot(half, basis)).astype(
-                    jnp.bfloat16
-                )
-
-
-def finish(far_two, mine, theirs, field_one, skeleton_two, transfer_one, transfer_two, basis, near):
-    scratch = (field_one, skeleton_two, transfer_one, transfer_two, basis, near)
+            down_leaf.append(exact(down_one, padded(one_ref[2 * pair + i])).astype(jnp.bfloat16))
+    basis_copy.wait()
+    for leaf in range(LEAVES):
+        columns = pl.ds(leaf * LEAF, LEAF)
+        at = (leaf % 4) // 2
+        half = down_leaf[leaf // 4][:, at * 2 * RANK : (at + 1) * 2 * RANK]
+        basis = (upper, below)[leaf % 2](basis_ref[:, columns])
+        out_ref[:, columns] = (near_ref[:, columns] + dot(half, basis)).astype(jnp.bfloat16)
+
+
+def finish(far_two, mine, theirs, field_one, near, *arrays):
     return pl.pallas_call(
         final_kernel,
         out_shape=jax.ShapeDtypeStruct((NRHS, LEAVES * LEAF), jnp.bfloat16),
-        in_specs=[SM] + [ANY] * 8,
+        in_specs=[SM] + [VM] * 4 + [ANY] * 4,
         out_specs=VM,
-        scratch_shapes=[pltpu.VMEM(a.shape, a.dtype) for a in scratch]
-        + [
-            bf16(TWO * FAR, HALF_ROWS, 2 * RANK),
-            pltpu.SemaphoreType.DMA,
-            pltpu.SemaphoreType.DMA((6,)),
-        ],
-        compiler_params=vmem(),
+        scratch_shapes=[bf16(*a.shape) for a in arrays] + [pltpu.SemaphoreType.DMA((4,))],
+        compiler_params=vmem(16),
         cost_estimate=cost(1 << 28, 3 * MIB, 1 << 17),
         name="finish",
-    )(far_two, mine, theirs, *scratch)
+    )(far_two, mine, theirs, field_one, near, *arrays)
 
 
 def shift(x, step):
@@ -615,8 +587,9 @@
     mine = far_arrived[:, ROWS:, :]
     theirs = swap(mine)
     field_one = far_one_field(far_one, low, far_arrived, skeleton_one)
-    return finish(far_two, mine, theirs, field_one, skeleton_two, transfer_one, transfer_two,
-                  basis, near)
+    return finish(
+        far_two, mine, theirs, field_one, near, skeleton_two, transfer_one, transfer_two, basis
+    )
 
 
 def solution(mesh):

time: 160 us -> 157 us (0.981)
  Pallas kernels: 61.4 us -> 51.5 us
  local copies, waits for them, and re-layouts: 3 us -> 11.4 us
    unnamed x15 -> x47, local copies, waits for them, and re-layouts: 1 us -> 10 us
    all_to_all x3, waiting for transfers between devices: 24 us -> 19.5 us  [exchange(): return lax.all_to_all(x, 'leaf', split_axis=0, concat_axis=0, tiled=True)]
    ppermute x2, waiting for transfers between devices: 38.5 us -> 42 us  [shift(): lax.ppermute(x, 'leaf', [(i, (i + step) % PEERS) for i in range(PEERS)])]
    pallas_call x1, Pallas kernels: 5.15 us -> 2.91 us  [finish(): pl.pallas_call(final_kernel, out_shape=jax.ShapeDtypeStruct((NRHS, LEAVES...]
    pallas_call x1, Pallas kernels: 3.69 us -> 1.87 us  [far_one_field(): pl.pallas_call(far_one_kernel, out_shape=jax.ShapeDtypeStruct((PAIRS, NRH...]
    pallas_call x1, Pallas kernels: 3.26 us -> 1.53 us  [coefficients(): pl.pallas_call(coeff_kernel, out_shape=jax.ShapeDtypeStruct((PAIRS + 1, R...]
    pallas_call x1, Pallas kernels: 2.95 us -> 1.23 us  [far_pack(): pl.pallas_call(far_pack_kernel, out_shape=jax.ShapeDtypeStruct((PEERS, ME...]
  transfers between devices with their start and end apart: 6 -> 6, of which waited for: 4 -> 4; matrix products, arithmetic and copies ran while one was open for 3% -> 3% of each run, Pallas kernels for 34% -> 31%
where the time goes in v4:
time: 157 us; the launch traced here: 156 us
  waiting for transfers between devices  61.5 us (39%)
  Pallas kernels  51.5 us (33%)
  starting transfers between devices  28.6 us (18%)
  local copies, waits for them, and re-layouts  11.4 us (7%)
  other arithmetic  2.51 us (2%)
    ppermute x2, waiting for transfers between devices, shift(): lax.ppermute(x, 'leaf', [(i, (i + step) % PEERS) for i in range(PEERS)])  42 us
    all_to_all x3, starting transfers between devices, exchange(): return lax.all_to_all(x, 'leaf', split_axis=0, concat_axis=0, tiled=True)  26.7 us
    pallas_call x1, Pallas kernels, remote_pairs(): pl.pallas_call(remote_kernel, out_shape=jax.ShapeDtypeStruct((NRHS, LEAVE...  19.9 us
    all_to_all x3, waiting for transfers between devices, exchange(): return lax.all_to_all(x, 'leaf', split_axis=0, concat_axis=0, tiled=True)  19.5 us
    pallas_call x1, Pallas kernels, own_pairs(): pl.pallas_call(own_kernel, out_shape=(jax.ShapeDtypeStruct((NRHS, LEAVES...  17.1 us
    unnamed x47, local copies, waits for them, and re-layouts  10 us
    pallas_call x1, Pallas kernels, pack(): pl.pallas_call(pack_kernel, out_shape=(jax.ShapeDtypeStruct((PEERS, 2, RO...  6.09 us
  transfers between devices with their start and end apart: 6, of which 4 were waited for; matrix products, arithmetic and copies ran while one was open for 3% of the time, Pallas kernels for 31%

profile of v4, /device:TPU:1, one launch (start us, length us, event | category | flops | bytes accessed | tf_op | source)
XLA Modules:
  0.0 155.8 jit_solution(10345454181378179202)
XLA Ops:
  0.7 1.0 ask.1
  1.6 11.5 %all-to-all-start = ((s32[128,1,128]{2,1,0:T(1,128)}), s32[128,1,128]{2,1,0:T(1,128)S(1)}, u32[]{:S(2)}, u32[]{:S(2)}) async-start(s32[128,1,128]{2,1,0:T(1,128)} %bitcast.2), calls=%async_computation | async-start | bytes 131072 | tf_op jit(solution)/shard_map/all_to_all | solution.py:559
  13.2 6.1 %pack.1 = (bf16[128,2,48,256]{3,2,1,0:T(8,128)(2,1)}, bf16[2,48,256]{2,1,0:T(8,128)(2,1)}, bf16[2,48,256]{2,1,0:T(8,128)(2,1)}, bf16[32,48,256]{2,1,0:T(8,128)(2,1)}) custom-call(s32[10,4096]{1,0:T(8,128)} %bitcast.7, bf16[32,8192]{1,0:T(8,128)(2,1)} %points_ref.1, bf16[16,8192]{1,0:T(8,128)(2,1)} %rhs_hbm.1), custom_call_target="tpu_custom_call" | custom-call | flops 1048576 | bytes 14680064 | tf_op jit(solution)/shard_map/pack/pallas_call | solution.py:170
  19.3 3.2 %all-to-all-done = s32[128,1,128]{2,1,0:T(1,128)S(1)} async-done(((s32[128,1,128]{2,1,0:T(1,128)}), s32[128,1,128]{2,1,0:T(1,128)S(1)}, u32[]{:S(2)}, u32[]{:S(2)}) %all-to-all-start) | async-done | bytes 65568 | tf_op jit(solution)/shard_map/all_to_all | solution.py:559
  22.5 7.0 %all-to-all-start.1 = ((bf16[128,2,48,256]{3,2,1,0:T(8,128)(2,1)}), bf16[128,2,48,256]{3,2,1,0:T(8,128)(2,1)}, u32[]{:S(2)}, u32[]{:S(2)}) async-start(bf16[128,2,48,256]{3,2,1,0:T(8,128)(2,1)} %get-tuple-element.35), calls=%async_computation.1 | async-start | bytes 12582912 | tf_op jit(solution)/shard_map/all_to_all | solution.py:559
  31.4 1.5 coefficients.1.columns_ref
  33.6 1.3 select_select_fusion.row_ref
  35.0 17.1 %own_pairs.1 = (f32[16,8192]{1,0:T(8,128)S(1)}, s32[768]{0:T(1024)S(1)}) custom-call(s32[320]{0:T(512)S(1)} %select_select_fusion.row_ref, bf16[32,48,256]{2,1,0:T(8,128)(2,1)S(1)} %copy-done.13), custom_call_target="tpu_custom_call" | custom-call | flops 4278190080 | bytes 2097152 | tf_op jit(solution)/shard_map/own_pairs/pallas_call | solution.py:377
  52.2 1.2 far_pack.1
  53.5 1.4 copy-done
  55.4 42.0 %collective-permute-done.left_ref = bf16[2,48,256]{2,1,0:T(8,128)(2,1)S(1)} collective-permute-done((bf16[2,48,256]{2,1,0:T(8,128)(2,1)S(1)}, bf16[2,48,256]{2,1,0:T(8,128)(2,1)S(1)}, u32[]{:S(2)}, u32[]{:S(2)}) %collective-permute-start) | collective-permute-done | bytes 49184 | tf_op jit(solution)/shard_map/ppermute | solution.py:551
  98.6 7.7 %all-to-all-done.1 = bf16[128,2,48,256]{3,2,1,0:T(8,128)(2,1)} async-done(((bf16[128,2,48,256]{3,2,1,0:T(8,128)(2,1)}), bf16[128,2,48,256]{3,2,1,0:T(8,128)(2,1)}, u32[]{:S(2)}, u32[]{:S(2)}) %all-to-all-start.1) | async-done | bytes 6291488 | tf_op jit(solution)/shard_map/all_to_all | solution.py:559
  106.3 8.2 %all-to-all-start.2 = ((bf16[128,72,128]{2,1,0:T(8,128)(2,1)}), bf16[128,72,128]{2,1,0:T(8,128)(2,1)S(1)}, u32[]{:S(2)}, u32[]{:S(2)}) async-start(bf16[128,72,128]{2,1,0:T(8,128)(2,1)} %copy-done), calls=%async_computation.2 | async-start | bytes 4718592 | tf_op jit(solution)/shard_map/all_to_all | solution.py:559
  114.6 1.1 copy-done.14
  115.7 0.8 copy-done.16
  116.5 0.8 copy-done.18
  117.3 1.0 copy-done.20
  118.3 19.9 %remote_pairs.1.near_ref = f32[16,8192]{1,0:T(8,128)S(1)} custom-call(s32[768]{0:T(1024)S(1)} %get-tuple-element.39.list_ref, bf16[256,48,256]{2,1,0:T(8,128)(2,1)} %bitcast.4.arrived_ref, bf16[2,48,256]{2,1,0:T(8,128)(2,1)S(1)} %copy-done.16, bf16[2,48,256]{2,1,0:T(8,128)(2,1)S(1)} %copy-done.18, bf16[32,48,256]{2,1,0:T(8,128)(2,1)S(1)} %copy-done.14, ...), custom_call_target="tpu_custom_call" | custom-call | flops 7130316800 | bytes 8388608 | tf_op jit(solution)/shard_map/remote_pairs/pallas_call | solution.py:417
  139.0 8.6 %all-to-all-done.2.arrived_ref = bf16[128,72,128]{2,1,0:T(8,128)(2,1)S(1)} async-done(((bf16[128,72,128]{2,1,0:T(8,128)(2,1)}), bf16[128,72,128]{2,1,0:T(8,128)(2,1)S(1)}, u32[]{:S(2)}, u32[]{:S(2)}) %all-to-all-start.2) | async-done | bytes 2359328 | tf_op jit(solution)/shard_map/all_to_all | solution.py:559
  147.7 1.4 collective-permute-start.2
  149.0 1.9 %far_one_field.1.field_one_ref = f32[4,16,128]{2,1,0:T(8,128)S(1)} custom-call(s32[8,8]{1,0:T(8,128)S(1)} %copy-done.11, s32[8,128]{1,0:T(8,128)S(1)} %get-tuple-element.45.low_ref, bf16[128,72,128]{2,1,0:T(8,128)(2,1)S(1)} %all-to-all-done.2.arrived_ref, bf16[32,512]{1,0:T(8,128)(2,1)S(1)} %copy-done.8), custom_call_target="tpu_custom_call" | custom-call | flops 268435456 | bytes 2097152 | tf_op jit(solution)/shard_map/far_one_field/pallas_call | solution.py:480
  150.9 0.9 copy-done.3
  151.9 1.0 copy-done.6
  152.9 2.9 %finish.1 = bf16[16,8192]{1,0:T(8,128)(2,1)} custom-call(s32[2,8]{1,0:T(2,128)S(1)} %copy-done.12, bf16[128,24,128]{2,1,0:T(8,128)(2,1)S(1)} %slice.7.mine_ref, bf16[128,24,128]{2,1,0:T(8,128)(2,1)S(1)} %collective-permute-done.2.theirs_ref, f32[4,16,128]{2,1,0:T(8,128)S(1)} %far_one_field.1.field_one_ref, f32[16,8192]{1,0:T(8,128)S(1)} %copy-done.6, ...), custom_call_target="tpu_custom_call" | custom-call | flops 268435456 | bytes 3145728 | tf_op jit(solution)/shard_map/finish/pallas_call | solution.py:538
  (55 shorter events, 6.0 us)
Async XLA Ops:
  1.6 20.8 %all-to-all-start = ((s32[128,1,128]{2,1,0:T(1,128)}), s32[128,1,128]{2,1,0:T(1,128)S(1)}, u32[]{:S(2)}, u32[]{:S(2)}) async-start(s32[128,1,128]{2,1,0:T(1,128)} %bitcast.2), calls=%async_computation | async-start | bytes 131072 | tf_op jit(solution)/shard_map/all_to_all | solution.py:559
  22.5 8.8 %copy-start.1 = (bf16[64,8192]{1,0:T(8,128)(2,1)S(1)}, bf16[64,8192]{1,0:T(8,128)(2,1)}, u32[]{:S(2)}) copy-start(bf16[64,8192]{1,0:T(8,128)(2,1)} %basis_hbm.3) | copy-start | bytes 3145732
  22.5 8.8 %copy-start.2 = (bf16[8,64,256]{2,1,0:T(8,128)(2,1)S(1)}, bf16[8,64,256]{2,1,0:T(8,128)(2,1)}, u32[]{:S(2)}) copy-start(bf16[8,64,256]{2,1,0:T(8,128)(2,1)} %one_hbm.3) | copy-start | bytes 786436
  22.5 8.8 %copy-start.4 = (bf16[16,8192]{1,0:T(8,128)(2,1)S(1)}, bf16[16,8192]{1,0:T(8,128)(2,1)}, u32[]{:S(2)}) copy-start(bf16[16,8192]{1,0:T(8,128)(2,1)} %rhs_hbm.1) | copy-start | bytes 786436
  22.5 8.8 %copy-start.7 = (bf16[2,64,256]{2,1,0:T(8,128)(2,1)S(1)}, bf16[2,64,256]{2,1,0:T(8,128)(2,1)}, u32[]{:S(2)}) copy-start(bf16[2,64,256]{2,1,0:T(8,128)(2,1)} %two_hbm.3) | copy-start | bytes 196612
  22.5 8.9 %copy-start.8 = (bf16[32,512]{1,0:T(8,128)(2,1)S(1)}, bf16[32,512]{1,0:T(8,128)(2,1)}, u32[]{:S(2)}) copy-start(bf16[32,512]{1,0:T(8,128)(2,1)} %skel_hbm.2) | copy-start | bytes 98308
  22.5 8.8 %copy-start.9 = (bf16[32,128]{1,0:T(8,128)(2,1)S(1)}, bf16[32,128]{1,0:T(8,128)(2,1)}, u32[]{:S(2)}) copy-start(bf16[32,128]{1,0:T(8,128)(2,1)} %skel_hbm.3) | copy-start | bytes 24580
  22.5 12.5 %copy-start.13 = (bf16[32,48,256]{2,1,0:T(8,128)(2,1)S(1)}, bf16[32,48,256]{2,1,0:T(8,128)(2,1)}, u32[]{:S(2)}) copy-start(bf16[32,48,256]{2,1,0:T(8,128)(2,1)} %get-tuple-element.31.own_hbm) | copy-start | bytes 2359300
  22.5 83.8 %all-to-all-start.1 = ((bf16[128,2,48,256]{3,2,1,0:T(8,128)(2,1)}), bf16[128,2,48,256]{3,2,1,0:T(8,128)(2,1)}, u32[]{:S(2)}, u32[]{:S(2)}) async-start(bf16[128,2,48,256]{3,2,1,0:T(8,128)(2,1)} %get-tuple-element.35), calls=%async_computation.1 | async-start | bytes 12582912 | tf_op jit(solution)/shard_map/all_to_all | solution.py:559
  35.0 19.9 %copy-start.22 = (bf16[2,48,256]{2,1,0:T(8,128)(2,1)S(1)}, bf16[2,48,256]{2,1,0:T(8,128)(2,1)}, u32[]{:S(2)}) copy-start(bf16[2,48,256]{2,1,0:T(8,128)(2,1)} %get-tuple-element.36) | copy-start | bytes 147460
  35.0 20.3 %copy-start.21 = (bf16[2,48,256]{2,1,0:T(8,128)(2,1)S(1)}, bf16[2,48,256]{2,1,0:T(8,128)(2,1)}, u32[]{:S(2)}) copy-start(bf16[2,48,256]{2,1,0:T(8,128)(2,1)} %get-tuple-element.37) | copy-start | bytes 147460
  52.1 54.2 %copy-start.19 = (f32[16,8192]{1,0:T(8,128)}, f32[16,8192]{1,0:T(8,128)S(1)}, u32[]{:S(2)}) copy-start(f32[16,8192]{1,0:T(8,128)S(1)} %get-tuple-element.43.field_ref) | copy-start | bytes 1572868
  53.5 1.4 copy-start
  54.9 42.5 %collective-permute-start = (bf16[2,48,256]{2,1,0:T(8,128)(2,1)S(1)}, bf16[2,48,256]{2,1,0:T(8,128)(2,1)S(1)}, u32[]{:S(2)}, u32[]{:S(2)}) collective-permute-start(bf16[2,48,256]{2,1,0:T(8,128)(2,1)S(1)} %copy-done.22), channel_id=1, source_target_pairs={{0,1},{1,2},{2,3},{3,4},{4,5},{5,6},{6,7},{7,8},{8,9},{9,10},{10,1... | collective-permute-start | bytes 147464 | tf_op jit(solution)/shard_map/ppermute | solution.py:551
  55.3 42.7 %collective-permute-start.1 = (bf16[2,48,256]{2,1,0:T(8,128)(2,1)S(1)}, bf16[2,48,256]{2,1,0:T(8,128)(2,1)S(1)}, u32[]{:S(2)}, u32[]{:S(2)}) collective-permute-start(bf16[2,48,256]{2,1,0:T(8,128)(2,1)S(1)} %copy-done.21), channel_id=1, source_target_pairs={{0,127},{1,0},{2,1},{3,2},{4,3},{5,4},{6,5},{7,6},{8,7},{9,8},{10,... | collective-permute-start | bytes 147464 | tf_op jit(solution)/shard_map/ppermute | solution.py:551
  106.3 41.2 %all-to-all-start.2 = ((bf16[128,72,128]{2,1,0:T(8,128)(2,1)}), bf16[128,72,128]{2,1,0:T(8,128)(2,1)S(1)}, u32[]{:S(2)}, u32[]{:S(2)}) async-start(bf16[128,72,128]{2,1,0:T(8,128)(2,1)} %copy-done), calls=%async_computation.2 | async-start | bytes 4718592 | tf_op jit(solution)/shard_map/all_to_all | solution.py:559
  114.6 1.1 copy-start.14
  117.3 1.0 copy-start.20
  118.3 30.7 %copy-start.11 = (s32[8,8]{1,0:T(8,128)S(1)}, s32[8,8]{1,0:T(8,128)}, u32[]{:S(2)}) copy-start(s32[8,8]{1,0:T(8,128)} %far_ref.4) | copy-start | bytes 772
  118.3 32.6 %copy-start.12 = (s32[2,8]{1,0:T(2,128)S(1)}, s32[2,8]{1,0:T(2,128)}, u32[]{:S(2)}) copy-start(s32[2,8]{1,0:T(2,128)} %far_ref.5) | copy-start | bytes 196
  138.2 0.8 copy-start.5
  147.7 3.3 %collective-permute-start.2 = (bf16[128,24,128]{2,1,0:T(8,128)(2,1)S(1)}, bf16[128,24,128]{2,1,0:T(8,128)(2,1)S(1)}, u32[]{:S(2)}, u32[]{:S(2)}) collective-permute-start(bf16[128,24,128]{2,1,0:T(8,128)(2,1)S(1)} %slice.7.mine_ref), channel_id=1, source_target_pairs={{0,1},{1,0},{2,3},{3,2},{4,5},{5,4},{6,7},{7,6},{8,9},{9,8},{10,11... | collective-permute-start | bytes 2359304 | tf_op jit(solution)/shard_map/ppermute | solution.py:555
  150.9 1.0 copy-start.3
  151.9 1.0 copy-start.6
  (5 other events, 3.5 us)

commit v5 on v4

--- a/solution.py
+++ b/solution.py
@@ -24,6 +24,9 @@
 STRIDE = 512
 HALF_ROWS = ROWS // 2
 MESSAGE = ROWS + HALF_ROWS
+BLOCK = 2 * ROWS
+ASK = 2 * BLOCK
+NEAR_MESSAGE = ASK + 16
 MIB = 1 << 20
 
 NT = (((1,), (1,)), ((), ()))
@@ -58,7 +61,15 @@
 SM = pl.BlockSpec(memory_space=pltpu.SMEM)
 
 
-def ask_kernel(far_ref, ask_ref, low_ref):
+def pack_kernel(
+    source_ref, far_ref, points_ref, rhs_ref, msg_ref, right_ref, left_ref, own_ref, low_ref,
+    lists_ref, points_vmem, rhs_vmem, block_ref, ask_ref, row_ref, row_smem,
+    in_sem, row_sem, ask_sem, msg_sem, side_sem,
+):
+    me = lax.axis_index("leaf")
+    listed = pltpu.make_async_copy(source_ref, lists_ref, row_sem)
+    listed.start()
+    filled = fetch(in_sem, (points_ref, points_vmem), (rhs_ref, rhs_vmem))
     peer = lax.broadcasted_iota(jnp.int32, (PEERS, FAR), 0) * ONE
     low = high = None
     for i in range(ONE):
@@ -70,7 +81,12 @@
     low = jnp.min(low.astype(jnp.float32), axis=1, keepdims=True)
     high = jnp.max(high.astype(jnp.float32), axis=1, keepdims=True)
     lane = lax.broadcasted_iota(jnp.int32, (PEERS, PEERS), 1)
-    ask_ref[...] = jnp.where(lane == 0, low, high).astype(jnp.int32)
+    wanted = jnp.where(lane < RANK, low, high)
+    ask_ref[...] = jnp.broadcast_to(
+        wanted[:, None, :], (PEERS, NEAR_MESSAGE - ASK, 2 * RANK)
+    ).astype(jnp.bfloat16)
+    asked = pltpu.make_async_copy(ask_ref, msg_ref.at[:, pl.ds(ASK, NEAR_MESSAGE - ASK)], ask_sem)
+    asked.start()
     across = lax.broadcasted_iota(jnp.int32, (ONE, PEERS), 1) * ONE
     low = None
     for j in range(FAR):
@@ -79,54 +95,31 @@
         low = a if j == 0 else jnp.minimum(low, a)
     low = jnp.min(low.astype(jnp.float32), axis=0, keepdims=True)
     low_ref[...] = jnp.broadcast_to(low, (ONE, PEERS)).astype(jnp.int32)
-
-
-def ask(far_one):
-    return pl.pallas_call(
-        ask_kernel,
-        out_shape=(
-            jax.ShapeDtypeStruct((PEERS, PEERS), jnp.int32),
-            jax.ShapeDtypeStruct((ONE, PEERS), jnp.int32),
-        ),
-        in_specs=[VM],
-        out_specs=(VM, VM),
-        compiler_params=vmem(8),
-        name="ask",
-    )(far_one)
-
-
-def pack_kernel(
-    source_ref, points_ref, rhs_ref, msg_ref, right_ref, left_ref, own_ref,
-    lists_ref, block_ref, row_ref, row_smem, in_sem, row_sem, msg_sem, side_sem,
-):
-    me = lax.axis_index("leaf")
-    listed = pltpu.make_async_copy(source_ref, lists_ref, row_sem)
-    listed.start()
-    filled = fetch(
-        in_sem,
-        *(
-            (ref.at[:, pl.ds(leaf * LEAF, LEAF)], block_ref.at[leaf, rows])
-            for leaf in range(LEAVES)
-            for ref, rows in ((points_ref, pl.ds(0, DIM)), (rhs_ref, pl.ds(DIM, NRHS)))
-        ),
-    )
     listed.wait()
     width = PEERS * LEAVES
-    low = high = bits = None
-    for k in range(NEAR):
-        mine = lists_ref[k : k + 1, :] - me * LEAVES
+    def marks(lists):
+        mine = lists - me * LEAVES
         inside = (mine >> 5) == 0
-        a = jnp.where(inside, mine, LEAVES)
-        b = jnp.where(inside, mine, -1)
-        c = jnp.where(inside, 1 << (mine & 31), 0)
-        low = a if k == 0 else jnp.minimum(low, a)
-        high = b if k == 0 else jnp.maximum(high, b)
-        bits = c if k == 0 else bits | c
-    low, high, bits = (jnp.broadcast_to(v, (8, width)) for v in (low, high, bits))
+        return (
+            jnp.where(inside, mine, LEAVES),
+            jnp.where(inside, -mine, 1),
+            jnp.where(inside, 1 << (mine & 31), 0),
+        )
+
+    low, high, bits = marks(lists_ref[:8, :])
+    for k in range(8, NEAR):
+        a, b, c = (jnp.broadcast_to(v, (8, width)) for v in marks(lists_ref[k : k + 1, :]))
+        low, high, bits = jnp.minimum(low, a), jnp.minimum(high, b), bits | c
+    for step in (4, 2, 1):
+        low = jnp.minimum(low, pltpu.roll(low, step, 0))
+        high = jnp.minimum(high, pltpu.roll(high, step, 0))
+        bits = bits | pltpu.roll(bits, step, 0)
+    upper_rows = lax.broadcasted_iota(jnp.int32, (8, width), 0) < 4
+    both = jnp.where(upper_rows, low, high)
     for step in (16, 8, 4, 2, 1):
-        low = jnp.minimum(low, pltpu.roll(low, width - step, 1))
-        high = jnp.maximum(high, pltpu.roll(high, width - step, 1))
+        both = jnp.minimum(both, pltpu.roll(both, width - step, 1))
         bits = bits | pltpu.roll(bits, width - step, 1)
+    low, high = both, -pltpu.roll(both, 4, 0)
     place = lax.broadcasted_iota(jnp.int32, (8, width), 1) & 31
     row_ref[...] = jnp.where(
         place == 0, low, jnp.where(place == 1, pltpu.roll(high, 1, 1), pltpu.roll(bits, 2, 1))
@@ -135,6 +128,11 @@
     copy.start()
     for fill in filled:
         fill.wait()
+    for leaf in range(LEAVES):
+        for half in range(2):
+            columns = pl.ds(leaf * LEAF + half * 128, 128)
+            block_ref[leaf, pl.ds(half * ROWS, DIM), :] = points_vmem[:, columns]
+            block_ref[leaf, pl.ds(half * ROWS + DIM, NRHS), :] = rhs_vmem[:, columns]
     own = pltpu.make_async_copy(block_ref, own_ref, in_sem.at[0])
     own.start()
     copy.wait()
@@ -142,10 +140,12 @@
     def send(peer, _):
         for slot in range(2):
             leaf = row_smem[0, peer * LEAVES + slot] & 31
-            pltpu.make_async_copy(block_ref.at[leaf], msg_ref.at[peer, slot], msg_sem).start()
+            pltpu.make_async_copy(
+                block_ref.at[leaf], msg_ref.at[peer, pl.ds(slot * BLOCK, BLOCK)], msg_sem
+            ).start()
         return 0
 
-    lax.fori_loop(0, PEERS, send, 0, unroll=4)
+    lax.fori_loop(0, PEERS, send, 0, unroll=8)
     for side, (ref, step) in enumerate(((right_ref, 1), (left_ref, PEERS - 1))):
         at = lax.rem(me + step, PEERS) * LEAVES
         between = row_smem[0, at + 2]
@@ -158,28 +158,35 @@
         first, last = lax.fori_loop(0, LEAVES, scan, (jnp.int32(-1), jnp.int32(0)))
         for slot, leaf in enumerate((first & 31, last & 31)):
             pltpu.make_async_copy(block_ref.at[leaf], ref.at[slot], side_sem.at[side]).start()
-    pltpu.make_async_copy(msg_ref, msg_ref, msg_sem).wait()
+    sent = msg_ref.at[:, pl.ds(0, ASK)]
+    pltpu.make_async_copy(sent, sent, msg_sem).wait()
+    asked.wait()
     for side, ref in enumerate((right_ref, left_ref)):
         pltpu.make_async_copy(ref, ref, side_sem.at[side]).wait()
     own.wait()
 
 
-def pack(source, points, rhs):
-    block = jax.ShapeDtypeStruct((LEAVES, ROWS, LEAF), jnp.bfloat16)
-    side = jax.ShapeDtypeStruct((2, ROWS, LEAF), jnp.bfloat16)
+def pack(source, far_one, points, rhs):
+    block = jax.ShapeDtypeStruct((LEAVES, BLOCK, 128), jnp.bfloat16)
+    side = jax.ShapeDtypeStruct((2, BLOCK, 128), jnp.bfloat16)
     return pl.pallas_call(
         pack_kernel,
         out_shape=(
-            jax.ShapeDtypeStruct((PEERS, 2, ROWS, LEAF), jnp.bfloat16), side, side, block,
+            jax.ShapeDtypeStruct((PEERS, NEAR_MESSAGE, 128), jnp.bfloat16), side, side, block,
+            jax.ShapeDtypeStruct((ONE, PEERS), jnp.int32),
         ),
-        in_specs=[ANY, ANY, ANY],
-        out_specs=(ANY, ANY, ANY, ANY),
+        in_specs=[ANY, VM, ANY, ANY],
+        out_specs=(ANY, ANY, ANY, ANY, VM),
         scratch_shapes=[
             pltpu.VMEM((NEAR, PEERS * LEAVES), jnp.int32),
-            bf16(LEAVES, ROWS, LEAF),
+            bf16(*points.shape),
+            bf16(*rhs.shape),
+            bf16(LEAVES, BLOCK, 128),
+            bf16(PEERS, NEAR_MESSAGE - ASK, 2 * RANK),
             pltpu.VMEM((8, PEERS * LEAVES), jnp.int32),
             pltpu.SMEM((1, PEERS * LEAVES), jnp.int32),
-            pltpu.SemaphoreType.DMA((2 * LEAVES,)),
+            pltpu.SemaphoreType.DMA((2,)),
+            pltpu.SemaphoreType.DMA,
             pltpu.SemaphoreType.DMA,
             pltpu.SemaphoreType.DMA,
             pltpu.SemaphoreType.DMA((2,)),
@@ -187,7 +194,7 @@
         compiler_params=vmem(56),
         cost_estimate=cost(1 << 20, 14 * MIB),
         name="pack",
-    )(source.T, points, rhs)
+    )(source.T, far_one, points, rhs)
 
 
 def upper(b):
@@ -248,13 +255,16 @@
     )(*args)
 
 
-def far_pack_kernel(asked_ref, columns_ref, out_ref, low_ref, high_ref):
+def far_pack_kernel(
+    arrived_ref, columns_ref, out_hbm, out_ref, ask_ref, cluster_ref, sem, out_sem
+):
+    (copy,) = fetch(sem, (arrived_ref.at[:, pl.ds(ASK, NEAR_MESSAGE - ASK)], ask_ref))
     left = lax.broadcasted_iota(jnp.int32, (ROWS, 2 * RANK), 1) < RANK
     for pair in range(PAIRS):
         wide = columns_ref[pair].astype(jnp.float32)
         turned = pltpu.roll(wide, RANK, 1)
-        low_ref[2 * pair] = high_ref[2 * pair + 1] = wide
-        low_ref[2 * pair + 1] = high_ref[2 * pair] = turned
+        cluster_ref[2 * pair] = jnp.where(left, wide, turned)
+        cluster_ref[2 * pair + 1] = jnp.where(left, turned, wide)
     wide = columns_ref[PAIRS].astype(jnp.float32)
     turned = pltpu.roll(wide, RANK, 1)
     half = left[:HALF_ROWS]
@@ -262,30 +272,46 @@
         jnp.where(half, wide[:HALF_ROWS], turned[HALF_ROWS:]),
         jnp.where(half, turned[:HALF_ROWS], wide[HALF_ROWS:]),
     )
+    copy.wait()
 
     def fill(chip, _):
         for core in range(2):
             peer = 2 * chip + core
-            first = jnp.where(
-                left, low_ref[asked_ref[2 * peer] & 7], high_ref[asked_ref[2 * peer + 1] & 7]
-            )
+            wanted = ask_ref[peer].astype(jnp.float32)[:8]
+            wanted = jnp.concatenate([wanted] * (ROWS // 8), axis=0)
+            first = cluster_ref[0]
+            for c in range(1, ONE):
+                first = jnp.where(wanted == c, cluster_ref[c], first)
             out_ref[peer] = jnp.concatenate([first, second[core]], axis=0).astype(jnp.bfloat16)
         return 0
 
-    lax.fori_loop(0, PEERS // 2, fill, 0, unroll=2)
-
-
-def far_pack(asked, columns):
+    sent = []
+    for part in range(4):
+        lax.fori_loop(part * PEERS // 8, (part + 1) * PEERS // 8, fill, 0, unroll=4)
+        peers = pl.ds(part * PEERS // 4, PEERS // 4)
+        sent.append(pltpu.make_async_copy(out_ref.at[peers], out_hbm.at[peers], out_sem.at[part]))
+        sent[-1].start()
+    for copy in sent:
+        copy.wait()
+
+
+def far_pack(arrived, columns):
     return pl.pallas_call(
         far_pack_kernel,
         out_shape=jax.ShapeDtypeStruct((PEERS, MESSAGE, 2 * RANK), jnp.bfloat16),
-        in_specs=[SM, VM],
-        out_specs=VM,
-        scratch_shapes=[pltpu.VMEM((ONE, ROWS, 2 * RANK), jnp.float32)] * 2,
-        compiler_params=vmem(16),
+        in_specs=[ANY, VM],
+        out_specs=ANY,
+        scratch_shapes=[
+            bf16(PEERS, MESSAGE, 2 * RANK),
+            bf16(PEERS, NEAR_MESSAGE - ASK, 2 * RANK),
+            pltpu.VMEM((ONE, ROWS, 2 * RANK), jnp.float32),
+            pltpu.SemaphoreType.DMA((1,)),
+            pltpu.SemaphoreType.DMA((4,)),
+        ],
+        compiler_params=vmem(56),
         cost_estimate=cost(1 << 20, 5 * MIB),
         name="far_pack",
-    )(asked, columns)
+    )(arrived, columns)
 
 
 def table_rows(near_source, me):
@@ -296,7 +322,7 @@
     high = jnp.max(jnp.where(from_peer, leaf[:, None], -1), axis=0)
     low_of = jnp.sum(jnp.where(from_peer, low[None, :], 0), axis=1)
     high_of = jnp.sum(jnp.where(from_peer, high[None, :], 0), axis=1)
-    row = 2 * device + (leaf != low_of)
+    row = device + PEERS * (leaf != low_of)
     inner = (leaf > low_of) & (leaf < high_of)
     for side, step in enumerate((PEERS - 1, 1)):
         chosen = inner & (device == (me + step) % PEERS)
@@ -321,9 +347,17 @@
     return jnp.concatenate([block, extra.astype(jnp.bfloat16)], axis=0)
 
 
+def points_of(block):
+    return jnp.concatenate([block[:DIM], block[ROWS : ROWS + DIM]], axis=1)
+
+
+def rhs_of(block):
+    return jnp.concatenate([block[DIM:ROWS], block[ROWS + DIM :]], axis=1)
+
+
 def turn_targets(own_ref, target_ref):
     def turn(leaf, _):
-        target_ref[leaf, :, :ROWS] = with_square(own_ref[leaf, :DIM, :], True)
+        target_ref[leaf, :, :ROWS] = with_square(points_of(own_ref[leaf]), True)
         return 0
 
     lax.fori_loop(0, LEAVES, turn, 0, unroll=2)
@@ -331,14 +365,15 @@
 
 def add_pairs(list_ref, start, table_ref, target_ref, out_ref):
     def step(i, _):
-        terms = []
+        pairs = []
         for u in range(GROUP):
             pair = list_ref[start + i * GROUP + u]
             target, row = pair // STRIDE, pair & (STRIDE - 1)
             weights = jnp.exp(
-                dot(target_ref[target, :, :ROWS], with_square(table_ref[row, :DIM, :], False))
+                dot(target_ref[target, :, :ROWS], with_square(points_of(table_ref[row]), False))
             ).astype(jnp.bfloat16)
-            terms.append((target, dot(table_ref[row, DIM:, :], weights, NT)))
+            pairs.append((target, row, weights))
+        terms = [(t, dot(rhs_of(table_ref[row]), weights, NT)) for t, row, weights in pairs]
         for target, term in terms:
             columns = pl.ds(pl.multiple_of(target * LEAF, LEAF), LEAF)
             out_ref[:, columns] += term
@@ -366,7 +401,7 @@
         list_ref[LIST + others + u] = LOCAL
     list_ref[LIST - 1] = mine
     list_ref[2 * LIST - 1] = others
-    own_ref[LEAVES] = jnp.zeros((ROWS, LEAF), jnp.bfloat16)
+    own_ref[LEAVES] = jnp.zeros((BLOCK, 128), jnp.bfloat16)
     copy.wait()
     turn_targets(own_ref, target_ref)
     out_ref[...] = jnp.zeros_like(out_ref)
@@ -383,7 +418,7 @@
         in_specs=[SM, ANY],
         out_specs=(VM, SM),
         scratch_shapes=[
-            bf16(LEAVES + 1, ROWS, LEAF),
+            bf16(LEAVES + 1, BLOCK, 128),
             bf16(LEAVES, LEAF, 128),
             pltpu.SemaphoreType.DMA((1,)),
         ],
@@ -401,11 +436,12 @@
         sem,
         (own_hbm, own_ref),
         (field_ref, out_ref),
-        (arrived_ref, table_ref.at[pl.ds(0, 2 * PEERS)]),
+        (arrived_ref.at[:, pl.ds(0, BLOCK)], table_ref.at[pl.ds(0, PEERS)]),
+        (arrived_ref.at[:, pl.ds(BLOCK, BLOCK)], table_ref.at[pl.ds(PEERS, PEERS)]),
         (left_ref, table_ref.at[pl.ds(2 * PEERS, 2)]),
         (right_ref, table_ref.at[pl.ds(2 * PEERS + 2, 2)]),
     )
-    table_ref[LOCAL] = jnp.zeros((ROWS, LEAF), jnp.bfloat16)
+    table_ref[LOCAL] = jnp.zeros((BLOCK, 128), jnp.bfloat16)
     near[0].wait()
     turn_targets(own_ref, target_ref)
     for copy in near[1:]:
@@ -420,10 +456,10 @@
         in_specs=[SM, ANY, ANY, ANY, ANY, ANY],
         out_specs=VM,
         scratch_shapes=[
-            bf16(LOCAL + 1, ROWS, LEAF),
-            bf16(LEAVES, ROWS, LEAF),
+            bf16(LOCAL + 1, BLOCK, 128),
+            bf16(LEAVES, BLOCK, 128),
             bf16(LEAVES, LEAF, 128),
-            pltpu.SemaphoreType.DMA((5,)),
+            pltpu.SemaphoreType.DMA((6,)),
         ],
         compiler_params=vmem(32),
         cost_estimate=cost(2 * 200 * 65536 * 272, 8 * MIB, 200 * 65536),
@@ -458,8 +494,11 @@
     return total
 
 
-def far_one_kernel(far_ref, low_ref, arrived_ref, skel_hbm, out_ref, skel_ref, in_sem):
-    (copy,) = fetch(in_sem, (skel_hbm, skel_ref))
+def far_one_kernel(
+    far_ref, low_ref, arrived_ref, skel_hbm, near_hbm, one_hbm, out_ref, near_ref, one_ref, skel_ref,
+    in_sem,
+):
+    copy, *brought = fetch(in_sem, (skel_hbm, skel_ref), (near_hbm, near_ref), (one_hbm, one_ref))
     copy.wait()
     for pair in range(PAIRS):
         clusters = (2 * pair, 2 * pair + 1)
@@ -474,28 +513,34 @@
             for c in clusters
         ]
         out_ref[pair] = field_pair(turned(skel_ref, pair), blocks, halves)
-
-
-def far_one_field(far_one, low, arrived, skeleton_one):
+    for copy in brought:
+        copy.wait()
+
+
+def far_one_field(far_one, low, arrived, skeleton_one, near, transfer_one):
     return pl.pallas_call(
         far_one_kernel,
-        out_shape=jax.ShapeDtypeStruct((PAIRS, NRHS, 2 * RANK), jnp.float32),
-        in_specs=[SM, SM, VM, ANY],
-        out_specs=VM,
-        scratch_shapes=[bf16(DIM, ONE * RANK), pltpu.SemaphoreType.DMA((1,))],
+        out_shape=(
+            jax.ShapeDtypeStruct((PAIRS, NRHS, 2 * RANK), jnp.float32),
+            jax.ShapeDtypeStruct(near.shape, near.dtype),
+            jax.ShapeDtypeStruct(transfer_one.shape, transfer_one.dtype),
+        ),
+        in_specs=[SM, SM, VM, ANY, ANY, ANY],
+        out_specs=(VM, VM, VM),
+        scratch_shapes=[bf16(DIM, ONE * RANK), pltpu.SemaphoreType.DMA((3,))],
         compiler_params=vmem(16),
         cost_estimate=cost(1 << 28, 2 * MIB, 1 << 19),
         name="far_one_field",
-    )(far_one, low, arrived, skeleton_one)
+    )(far_one, low, arrived, skeleton_one, near, transfer_one)
 
 
 def final_kernel(
-    far_ref, mine_ref, theirs_ref, field_one_ref, near_ref, skel_hbm, one_hbm, two_hbm, basis_hbm,
-    out_ref, skel_ref, one_ref, two_ref, basis_ref, in_sem,
+    far_ref, mine_ref, theirs_ref, field_one_ref, near_ref, one_ref, skel_hbm, two_hbm, basis_hbm,
+    out_ref, skel_ref, two_ref, basis_ref, in_sem,
 ):
     core = lax.rem(lax.axis_index("leaf"), 2)
-    skel_copy, two_copy, one_copy, basis_copy = fetch(
-        in_sem, (skel_hbm, skel_ref), (two_hbm, two_ref), (one_hbm, one_ref), (basis_hbm, basis_ref)
+    skel_copy, two_copy, basis_copy = fetch(
+        in_sem, (skel_hbm, skel_ref), (two_hbm, two_ref), (basis_hbm, basis_ref)
     )
 
     def split(x):
@@ -518,7 +563,6 @@
     from_two = [
         exact(field_two, padded(two_ref[e])) for e, padded in enumerate((upper, below))
     ]
-    one_copy.wait()
     down_leaf = []
     for pair in range(PAIRS):
         parent = from_two[pair // 2][:, (pair % 2) * 2 * RANK : (pair % 2 + 1) * 2 * RANK]
@@ -534,17 +578,17 @@
         out_ref[:, columns] = (near_ref[:, columns] + dot(half, basis)).astype(jnp.bfloat16)
 
 
-def finish(far_two, mine, theirs, field_one, near, *arrays):
+def finish(far_two, mine, theirs, field_one, near, transfer_one, *arrays):
     return pl.pallas_call(
         final_kernel,
         out_shape=jax.ShapeDtypeStruct((NRHS, LEAVES * LEAF), jnp.bfloat16),
-        in_specs=[SM] + [VM] * 4 + [ANY] * 4,
+        in_specs=[SM] + [VM] * 5 + [ANY] * 3,
         out_specs=VM,
-        scratch_shapes=[bf16(*a.shape) for a in arrays] + [pltpu.SemaphoreType.DMA((4,))],
+        scratch_shapes=[bf16(*a.shape) for a in arrays] + [pltpu.SemaphoreType.DMA((3,))],
         compiler_params=vmem(16),
         cost_estimate=cost(1 << 28, 3 * MIB, 1 << 17),
         name="finish",
-    )(far_two, mine, theirs, field_one, near, *arrays)
+    )(far_two, mine, theirs, field_one, near, transfer_one, *arrays)
 
 
 def shift(x, step):
@@ -564,31 +608,25 @@
     far_one, far_two,
 ):
     me = lax.axis_index("leaf")
-    wanted, low = ask(far_one)
-    asked = exchange(wanted.reshape(PEERS, 1, PEERS)).reshape(PEERS, PEERS)
-    message, to_right, to_left, own = pack(near_source, points, rhs)
-    message, asked = lax.optimization_barrier((message, asked))
+    message, to_right, to_left, own, low = pack(near_source, far_one, points, rhs)
     arrived = exchange(message)
     columns = coefficients(rhs, basis, transfer_one, transfer_two, skeleton_one, skeleton_two)
-    far_message = far_pack(asked[:, :2].reshape(-1), columns)
     field, lists = own_pairs(table_rows(near_source, me), own)
-    to_right, to_left, far_message, field, lists = lax.optimization_barrier(
-        (to_right, to_left, far_message, field, lists)
+    to_right, to_left, columns, field, lists = lax.optimization_barrier(
+        (to_right, to_left, columns, field, lists)
     )
     from_left, from_right = shift(to_right, 1), shift(to_left, -1)
-    far_message, arrived, from_left, from_right = lax.optimization_barrier(
-        (far_message, arrived, from_left, from_right)
-    )
-    far_arrived = exchange(far_message)
-    near = remote_pairs(
-        lists, arrived.reshape(2 * PEERS, ROWS, LEAF), from_left, from_right, own, field
-    )
+    arrived, from_left, from_right = lax.optimization_barrier((arrived, from_left, from_right))
+    far_arrived = exchange(far_pack(arrived, columns))
+    near = remote_pairs(lists, arrived, from_left, from_right, own, field)
     far_arrived, near = lax.optimization_barrier((far_arrived, near))
     mine = far_arrived[:, ROWS:, :]
     theirs = swap(mine)
-    field_one = far_one_field(far_one, low, far_arrived, skeleton_one)
+    field_one, near, transfer_one = far_one_field(
+        far_one, low, far_arrived, skeleton_one, near, transfer_one
+    )
     return finish(
-        far_two, mine, theirs, field_one, near, skeleton_two, transfer_one, transfer_two, basis
+        far_two, mine, theirs, field_one, near, transfer_one, skeleton_two, transfer_two, basis
     )
 
 

time: 157 us -> 155 us (0.987)
  waiting for transfers between devices: 61.5 us -> 67.2 us
  starting transfers between devices: 28.6 us -> 23.4 us
    all_to_all x3 -> x2, starting transfers between devices: 26.7 us -> 19.1 us  [exchange(): return lax.all_to_all(x, 'leaf', split_axis=0, concat_axis=0, tiled=True)]
    ppermute x2, waiting for transfers between devices: 42 us -> 48.9 us  [shift(): lax.ppermute(x, 'leaf', [(i, (i + step) % PEERS) for i in range(PEERS)])]
    pallas_call x1, Pallas kernels: 1.23 us -> 3.8 us  [far_pack(): pl.pallas_call(far_pack_kernel, out_shape=jax.ShapeDtypeStruct((PEERS, ME...]
    pallas_call x1, Pallas kernels: 17.1 us -> 14.5 us  [own_pairs(): pl.pallas_call(own_kernel, out_shape=(jax.ShapeDtypeStruct((NRHS, LEAVES...]
    ppermute x2, starting transfers between devices: 0.51 us -> 2.97 us  [shift(): lax.ppermute(x, 'leaf', [(i, (i + step) % PEERS) for i in range(PEERS)])]
    all_to_all x3 -> x2, waiting for transfers between devices: 19.5 us -> 18.4 us  [exchange(): return lax.all_to_all(x, 'leaf', split_axis=0, concat_axis=0, tiled=True)]
    pallas_call x3 -> x2, Pallas kernels: 8.93 us -> 8.66 us  [the longest x1 6.71 us: pack(): pl.pallas_call(pack_kernel, out_shape=(jax.ShapeDtypeStruct((PEERS, NEAR_...]
  transfers between devices with their start and end apart: 6 -> 5, of which waited for: 4 -> 3; matrix products, arithmetic and copies ran while one was open for 3% -> 2% of each run, Pallas kernels for 31% -> 24%
where the time goes in v5:
time: 155 us
  waiting for transfers between devices  67.2 us (43%)
  Pallas kernels  50.6 us (33%)
  starting transfers between devices  23.4 us (15%)
  local copies, waits for them, and re-layouts  10.6 us (7%)
  other arithmetic  2.48 us (2%)
    ppermute x2, waiting for transfers between devices, shift(): lax.ppermute(x, 'leaf', [(i, (i + step) % PEERS) for i in range(PEERS)])  48.9 us
    pallas_call x1, Pallas kernels, remote_pairs(): pl.pallas_call(remote_kernel, out_shape=jax.ShapeDtypeStruct((NRHS, LEAVE...  19.2 us
    all_to_all x2, starting transfers between devices, exchange(): return lax.all_to_all(x, 'leaf', split_axis=0, concat_axis=0, tiled=True)  19.1 us
    all_to_all x2, waiting for transfers between devices, exchange(): return lax.all_to_all(x, 'leaf', split_axis=0, concat_axis=0, tiled=True)  18.4 us
    pallas_call x1, Pallas kernels, own_pairs(): pl.pallas_call(own_kernel, out_shape=(jax.ShapeDtypeStruct((NRHS, LEAVES...  14.5 us
    unnamed x47, local copies, waits for them, and re-layouts  9.35 us
    pallas_call x1, Pallas kernels, pack(): pl.pallas_call(pack_kernel, out_shape=(jax.ShapeDtypeStruct((PEERS, NEAR_...  6.71 us
    pallas_call x1, Pallas kernels, far_pack(): pl.pallas_call(far_pack_kernel, out_shape=jax.ShapeDtypeStruct((PEERS, ME...  3.8 us
  transfers between devices with their start and end apart: 5, of which 3 were waited for; matrix products, arithmetic and copies ran while one was open for 2% of the time, Pallas kernels for 24%

profile of v5, /device:TPU:1, one launch (start us, length us, event | category | flops | bytes accessed | tf_op | source)
XLA Modules:
  0.0 154.7 jit_solution(17006672943591456559)
XLA Ops:
  0.0 6.7 %pack.1 = (bf16[128,208,128]{2,1,0:T(8,128)(2,1)}, bf16[2,96,128]{2,1,0:T(8,128)(2,1)}, bf16[2,96,128]{2,1,0:T(8,128)(2,1)}, bf16[32,96,128]{2,1,0:T(8,128)(2,1)}, s32[8,128]{1,0:T(8,128)}) custom-call(s32[10,4096]{1,0:T(8,128)} %bitcast.1, s32[8,8]{1,0:T(8,128)} %far_ref.4, bf16[32,8192]{1,0:T(8,128)(2,1)} %points_ref.1, bf16[16,8192]{1,0:T(8,128)(2,1)} %rhs_hbm.1), custom_call_target="tpu_custom_call" | custom-call | flops 1048576 | bytes 14680064 | tf_op jit(solution)/shard_map/pack/pallas_call | solution.py:172
  6.8 11.9 %all-to-all-start = ((bf16[128,208,128]{2,1,0:T(8,128)(2,1)}), bf16[128,208,128]{2,1,0:T(8,128)(2,1)}, u32[]{:S(2)}, u32[]{:S(2)}) async-start(bf16[128,208,128]{2,1,0:T(8,128)(2,1)} %get-tuple-element.25), calls=%async_computation | async-start | bytes 13631488 | tf_op jit(solution)/shard_map/all_to_all | solution.py:603
  18.7 0.8 constant_dynamic-slice_fusion
  20.5 1.5 coefficients.1.columns_ref
  23.4 1.3 select_select_fusion.row_ref
  24.8 14.5 %own_pairs.1 = (f32[16,8192]{1,0:T(8,128)S(1)}, s32[768]{0:T(1024)S(1)}) custom-call(s32[320]{0:T(512)S(1)} %select_select_fusion.row_ref, bf16[32,96,128]{2,1,0:T(8,128)(2,1)S(1)} %copy-done.13), custom_call_target="tpu_custom_call" | custom-call | flops 4278190080 | bytes 2097152 | tf_op jit(solution)/shard_map/own_pairs/pallas_call | solution.py:412
  39.3 0.8 copy-done.19
  40.1 3.0 %collective-permute-start = (bf16[2,96,128]{2,1,0:T(8,128)(2,1)S(1)}, bf16[2,96,128]{2,1,0:T(8,128)(2,1)S(1)}, u32[]{:S(2)}, u32[]{:S(2)}) collective-permute-start(bf16[2,96,128]{2,1,0:T(8,128)(2,1)S(1)} %copy-done.22), channel_id=1, source_target_pairs={{0,1},{1,2},{2,3},{3,4},{4,5},{5,6},{6,7},{7,8},{8,9},{9,10},{10,1... | collective-permute-start | bytes 147464 | tf_op jit(solution)/shard_map/ppermute | solution.py:595
  43.1 48.9 %collective-permute-done.left_ref = bf16[2,96,128]{2,1,0:T(8,128)(2,1)S(1)} collective-permute-done((bf16[2,96,128]{2,1,0:T(8,128)(2,1)S(1)}, bf16[2,96,128]{2,1,0:T(8,128)(2,1)S(1)}, u32[]{:S(2)}, u32[]{:S(2)}) %collective-permute-start) | collective-permute-done | bytes 49184 | tf_op jit(solution)/shard_map/ppermute | solution.py:595
  93.2 9.2 %all-to-all-done.arrived_ref = bf16[128,208,128]{2,1,0:T(8,128)(2,1)} async-done(((bf16[128,208,128]{2,1,0:T(8,128)(2,1)}), bf16[128,208,128]{2,1,0:T(8,128)(2,1)}, u32[]{:S(2)}, u32[]{:S(2)}) %all-to-all-start) | async-done | bytes 6815776 | tf_op jit(solution)/shard_map/all_to_all | solution.py:603
  102.4 3.8 %far_pack.1 = bf16[128,72,128]{2,1,0:T(8,128)(2,1)} custom-call(bf16[128,208,128]{2,1,0:T(8,128)(2,1)} %all-to-all-done.arrived_ref, bf16[5,48,128]{2,1,0:T(8,128)(2,1)} %copy-done.7), custom_call_target="tpu_custom_call" | custom-call | flops 1048576 | bytes 5242880 | tf_op jit(solution)/shard_map/far_pack/pallas_call | solution.py:299
  106.2 7.2 %all-to-all-start.1 = ((bf16[128,72,128]{2,1,0:T(8,128)(2,1)}), bf16[128,72,128]{2,1,0:T(8,128)(2,1)S(1)}, u32[]{:S(2)}, u32[]{:S(2)}) async-start(bf16[128,72,128]{2,1,0:T(8,128)(2,1)} %far_pack.1), calls=%async_computation.1 | async-start | bytes 4718592 | tf_op jit(solution)/shard_map/all_to_all | solution.py:603
  113.4 1.1 copy-done.14
  114.5 0.8 copy-done.16
  115.3 0.8 copy-done.18
  116.1 1.0 copy-done.20
  117.2 19.2 %remote_pairs.1.near_hbm = f32[16,8192]{1,0:T(8,128)S(1)} custom-call(s32[768]{0:T(1024)S(1)} %get-tuple-element.35.list_ref, bf16[128,208,128]{2,1,0:T(8,128)(2,1)} %all-to-all-done.arrived_ref, bf16[2,96,128]{2,1,0:T(8,128)(2,1)S(1)} %copy-done.16, bf16[2,96,128]{2,1,0:T(8,128)(2,1)S(1)} %copy-done.18, bf16[32,96,128]{2,1,0:T(8,128)(2,1)S(1)} %copy-done.14, ...), custom_call_target="tpu_custom_call" | custom-call | flops 7130316800 | bytes 8388608 | tf_op jit(solution)/shard_map/remote_pairs/pallas_call | solution.py:453
  136.4 0.8 copy-done.4
  137.2 9.2 %all-to-all-done.1.arrived_ref = bf16[128,72,128]{2,1,0:T(8,128)(2,1)S(1)} async-done(((bf16[128,72,128]{2,1,0:T(8,128)(2,1)}), bf16[128,72,128]{2,1,0:T(8,128)(2,1)S(1)}, u32[]{:S(2)}, u32[]{:S(2)}) %all-to-all-start.1) | async-done | bytes 2359328 | tf_op jit(solution)/shard_map/all_to_all | solution.py:603
  146.5 1.4 collective-permute-start.2
  147.8 0.9 copy-done.2
  148.8 1.0 copy-done.5
  149.8 1.9 %far_one_field.1 = (f32[4,16,128]{2,1,0:T(8,128)S(1)}, f32[16,8192]{1,0:T(8,128)S(1)}, bf16[8,64,256]{2,1,0:T(8,128)(2,1)S(1)}) custom-call(s32[8,8]{1,0:T(8,128)S(1)} %copy-done.10, s32[8,128]{1,0:T(8,128)S(1)} %copy-done.11, bf16[128,72,128]{2,1,0:T(8,128)(2,1)S(1)} %all-to-all-done.1.arrived_ref, bf16[32,512]{1,0:T(8,128)(2,1)S(1)} %copy-done.8, ...), custom_call_target="tpu_custom_call" | custom-call | flops 268435456 | bytes 2097152 | tf_op jit(solution)/shard_map/far_one_field/pallas_call | solution.py:521
  151.8 2.9 %finish.1 = bf16[16,8192]{1,0:T(8,128)(2,1)} custom-call(s32[2,8]{1,0:T(2,128)S(1)} %copy-done.12, bf16[128,24,128]{2,1,0:T(8,128)(2,1)S(1)} %slice.3.mine_ref, bf16[128,24,128]{2,1,0:T(8,128)(2,1)S(1)} %collective-permute-done.2.theirs_ref, f32[4,16,128]{2,1,0:T(8,128)S(1)} %get-tuple-element.42.field_one_ref, f32[16,8192]{1,0:T(8,128)S(1)} %get-tuple-element.43.near_ref, ...), custom_call_target="tpu_custom_call" | custom-call | flops 268435456 | bytes 3145728 | tf_op jit(solution)/shard_map/finish/pallas_call | solution.py:582
  (51 shorter events, 3.7 us)
Async XLA Ops:
  6.7 13.8 %copy-start = (bf16[64,8192]{1,0:T(8,128)(2,1)S(1)}, bf16[64,8192]{1,0:T(8,128)(2,1)}, u32[]{:S(2)}) copy-start(bf16[64,8192]{1,0:T(8,128)(2,1)} %basis_hbm.3) | copy-start | bytes 3145732
  6.7 13.8 %copy-start.1 = (bf16[8,64,256]{2,1,0:T(8,128)(2,1)S(1)}, bf16[8,64,256]{2,1,0:T(8,128)(2,1)}, u32[]{:S(2)}) copy-start(bf16[8,64,256]{2,1,0:T(8,128)(2,1)} %one_hbm.3) | copy-start | bytes 786436
  6.7 13.8 %copy-start.3 = (bf16[16,8192]{1,0:T(8,128)(2,1)S(1)}, bf16[16,8192]{1,0:T(8,128)(2,1)}, u32[]{:S(2)}) copy-start(bf16[16,8192]{1,0:T(8,128)(2,1)} %rhs_hbm.1) | copy-start | bytes 786436
  6.8 13.8 %copy-start.6 = (bf16[2,64,256]{2,1,0:T(8,128)(2,1)S(1)}, bf16[2,64,256]{2,1,0:T(8,128)(2,1)}, u32[]{:S(2)}) copy-start(bf16[2,64,256]{2,1,0:T(8,128)(2,1)} %two_hbm.3) | copy-start | bytes 196612
  6.8 13.8 %copy-start.8 = (bf16[32,512]{1,0:T(8,128)(2,1)S(1)}, bf16[32,512]{1,0:T(8,128)(2,1)}, u32[]{:S(2)}) copy-start(bf16[32,512]{1,0:T(8,128)(2,1)} %skel_hbm.2) | copy-start | bytes 98308
  6.8 13.8 %copy-start.9 = (bf16[32,128]{1,0:T(8,128)(2,1)S(1)}, bf16[32,128]{1,0:T(8,128)(2,1)}, u32[]{:S(2)}) copy-start(bf16[32,128]{1,0:T(8,128)(2,1)} %skel_hbm.3) | copy-start | bytes 24580
  6.8 18.0 %copy-start.13 = (bf16[32,96,128]{2,1,0:T(8,128)(2,1)S(1)}, bf16[32,96,128]{2,1,0:T(8,128)(2,1)}, u32[]{:S(2)}) copy-start(bf16[32,96,128]{2,1,0:T(8,128)(2,1)} %get-tuple-element.28.own_hbm) | copy-start | bytes 2359300
  6.8 95.6 %all-to-all-start = ((bf16[128,208,128]{2,1,0:T(8,128)(2,1)}), bf16[128,208,128]{2,1,0:T(8,128)(2,1)}, u32[]{:S(2)}, u32[]{:S(2)}) async-start(bf16[128,208,128]{2,1,0:T(8,128)(2,1)} %get-tuple-element.25), calls=%async_computation | async-start | bytes 13631488 | tf_op jit(solution)/shard_map/all_to_all | solution.py:603
  24.8 15.4 %copy-start.22 = (bf16[2,96,128]{2,1,0:T(8,128)(2,1)S(1)}, bf16[2,96,128]{2,1,0:T(8,128)(2,1)}, u32[]{:S(2)}) copy-start(bf16[2,96,128]{2,1,0:T(8,128)(2,1)} %get-tuple-element.31) | copy-start | bytes 147460
  24.8 18.3 %copy-start.21 = (bf16[2,96,128]{2,1,0:T(8,128)(2,1)S(1)}, bf16[2,96,128]{2,1,0:T(8,128)(2,1)}, u32[]{:S(2)}) copy-start(bf16[2,96,128]{2,1,0:T(8,128)(2,1)} %get-tuple-element.32) | copy-start | bytes 147460
  39.3 0.8 copy-start.19
  40.1 51.8 %collective-permute-start = (bf16[2,96,128]{2,1,0:T(8,128)(2,1)S(1)}, bf16[2,96,128]{2,1,0:T(8,128)(2,1)S(1)}, u32[]{:S(2)}, u32[]{:S(2)}) collective-permute-start(bf16[2,96,128]{2,1,0:T(8,128)(2,1)S(1)} %copy-done.22), channel_id=1, source_target_pairs={{0,1},{1,2},{2,3},{3,4},{4,5},{5,6},{6,7},{7,8},{8,9},{9,10},{10,1... | collective-permute-start | bytes 147464 | tf_op jit(solution)/shard_map/ppermute | solution.py:595
  43.1 49.5 %collective-permute-start.1 = (bf16[2,96,128]{2,1,0:T(8,128)(2,1)S(1)}, bf16[2,96,128]{2,1,0:T(8,128)(2,1)S(1)}, u32[]{:S(2)}, u32[]{:S(2)}) collective-permute-start(bf16[2,96,128]{2,1,0:T(8,128)(2,1)S(1)} %copy-done.21), channel_id=1, source_target_pairs={{0,127},{1,0},{2,1},{3,2},{4,3},{5,4},{6,5},{7,6},{8,7},{9,8},{10,... | collective-permute-start | bytes 147464 | tf_op jit(solution)/shard_map/ppermute | solution.py:595
  106.2 40.2 %all-to-all-start.1 = ((bf16[128,72,128]{2,1,0:T(8,128)(2,1)}), bf16[128,72,128]{2,1,0:T(8,128)(2,1)S(1)}, u32[]{:S(2)}, u32[]{:S(2)}) async-start(bf16[128,72,128]{2,1,0:T(8,128)(2,1)} %far_pack.1), calls=%async_computation.1 | async-start | bytes 4718592 | tf_op jit(solution)/shard_map/all_to_all | solution.py:603
  113.4 1.1 copy-start.14
  114.5 0.8 copy-start.16
  116.1 1.0 copy-start.20
  117.2 30.7 %copy-start.10 = (s32[8,8]{1,0:T(8,128)S(1)}, s32[8,8]{1,0:T(8,128)}, u32[]{:S(2)}) copy-start(s32[8,8]{1,0:T(8,128)} %far_ref.4) | copy-start | bytes 772
  117.2 30.7 %copy-start.11 = (s32[8,128]{1,0:T(8,128)S(1)}, s32[8,128]{1,0:T(8,128)}, u32[]{:S(2)}) copy-start(s32[8,128]{1,0:T(8,128)} %get-tuple-element.40.low_ref) | copy-start | bytes 12292
  117.2 34.6 %copy-start.12 = (s32[2,8]{1,0:T(2,128)S(1)}, s32[2,8]{1,0:T(2,128)}, u32[]{:S(2)}) copy-start(s32[2,8]{1,0:T(2,128)} %far_ref.5) | copy-start | bytes 196
  136.4 0.8 copy-start.4
  146.5 5.3 %collective-permute-start.2 = (bf16[128,24,128]{2,1,0:T(8,128)(2,1)S(1)}, bf16[128,24,128]{2,1,0:T(8,128)(2,1)S(1)}, u32[]{:S(2)}, u32[]{:S(2)}) collective-permute-start(bf16[128,24,128]{2,1,0:T(8,128)(2,1)S(1)} %slice.3.mine_ref), channel_id=1, source_target_pairs={{0,1},{1,0},{2,3},{3,2},{4,5},{5,4},{6,7},{7,6},{8,9},{9,8},{10,11... | collective-permute-start | bytes 2359304 | tf_op jit(solution)/shard_map/ppermute | solution.py:599
  147.8 1.0 copy-start.2
  148.8 1.0 copy-start.5
  (4 other events, 2.7 us)

commit v6 on v5

--- a/solution.py
+++ b/solution.py
@@ -622,6 +622,8 @@
     far_arrived, near = lax.optimization_barrier((far_arrived, near))
     mine = far_arrived[:, ROWS:, :]
     theirs = swap(mine)
+    near = pltpu.with_memory_space_constraint(near, pltpu.HBM)
+    transfer_one = pltpu.with_memory_space_constraint(transfer_one, pltpu.HBM)
     field_one, near, transfer_one = far_one_field(
         far_one, low, far_arrived, skeleton_one, near, transfer_one
     )

time: 155 us -> 153 us (0.987)
  local copies, waits for them, and re-layouts: 10.6 us -> 8.64 us
    unnamed x47 -> x43, local copies, waits for them, and re-layouts: 9.35 us -> 7.37 us
where the time goes in v6:
time: 153 us
  waiting for transfers between devices  67.8 us (44%)
  Pallas kernels  50.5 us (33%)
  starting transfers between devices  22.8 us (15%)
  local copies, waits for them, and re-layouts  8.64 us (6%)
  other arithmetic  2.49 us (2%)
    ppermute x2, waiting for transfers between devices, shift(): lax.ppermute(x, 'leaf', [(i, (i + step) % PEERS) for i in range(PEERS)])  49.4 us
    pallas_call x1, Pallas kernels, remote_pairs(): pl.pallas_call(remote_kernel, out_shape=jax.ShapeDtypeStruct((NRHS, LEAVE...  19.2 us
    all_to_all x2, starting transfers between devices, exchange(): return lax.all_to_all(x, 'leaf', split_axis=0, concat_axis=0, tiled=True)  19 us
    all_to_all x2, waiting for transfers between devices, exchange(): return lax.all_to_all(x, 'leaf', split_axis=0, concat_axis=0, tiled=True)  18.4 us
    pallas_call x1, Pallas kernels, own_pairs(): pl.pallas_call(own_kernel, out_shape=(jax.ShapeDtypeStruct((NRHS, LEAVES...  14.5 us
    unnamed x43, local copies, waits for them, and re-layouts  7.37 us
    pallas_call x1, Pallas kernels, pack(): pl.pallas_call(pack_kernel, out_shape=(jax.ShapeDtypeStruct((PEERS, NEAR_...  6.67 us
    pallas_call x1, Pallas kernels, far_pack(): pl.pallas_call(far_pack_kernel, out_shape=jax.ShapeDtypeStruct((PEERS, ME...  3.8 us
  transfers between devices with their start and end apart: 5, of which 3 were waited for; matrix products, arithmetic and copies ran while one was open for 2% of the time, Pallas kernels for 24%

profile of v6, /device:TPU:1, one launch (start us, length us, event | category | flops | bytes accessed | tf_op | source)
XLA Modules:
  0.0 152.6 jit_solution(18230166300966771758)
XLA Ops:
  0.0 6.7 %pack.1 = (bf16[128,208,128]{2,1,0:T(8,128)(2,1)}, bf16[2,96,128]{2,1,0:T(8,128)(2,1)}, bf16[2,96,128]{2,1,0:T(8,128)(2,1)}, bf16[32,96,128]{2,1,0:T(8,128)(2,1)}, s32[8,128]{1,0:T(8,128)}) custom-call(s32[10,4096]{1,0:T(8,128)} %bitcast.1, s32[8,8]{1,0:T(8,128)} %far_ref.4, bf16[32,8192]{1,0:T(8,128)(2,1)} %points_ref.1, bf16[16,8192]{1,0:T(8,128)(2,1)} %rhs_hbm.1), custom_call_target="tpu_custom_call" | custom-call | flops 1048576 | bytes 14680064 | tf_op jit(solution)/shard_map/pack/pallas_call | solution.py:172
  6.8 11.9 %all-to-all-start = ((bf16[128,208,128]{2,1,0:T(8,128)(2,1)}), bf16[128,208,128]{2,1,0:T(8,128)(2,1)}, u32[]{:S(2)}, u32[]{:S(2)}) async-start(bf16[128,208,128]{2,1,0:T(8,128)(2,1)} %get-tuple-element.25), calls=%async_computation | async-start | bytes 13631488 | tf_op jit(solution)/shard_map/all_to_all | solution.py:603
  18.7 0.8 constant_dynamic-slice_fusion
  20.5 1.5 %coefficients.1.columns_ref = bf16[5,48,128]{2,1,0:T(8,128)(2,1)S(1)} custom-call(bf16[16,8192]{1,0:T(8,128)(2,1)S(1)} %copy-done.2, bf16[64,8192]{1,0:T(8,128)(2,1)S(1)} %copy-done, bf16[8,64,256]{2,1,0:T(8,128)(2,1)S(1)} %copy-done.1, bf16[2,64,256]{2,1,0:T(8,128)(2,1)S(1)} %copy-done.4, bf16[32,512]{1,0:T(8,128)(2,1)S(1)} %copy-done.6, ...), custom_call_target="tpu_custom_call" | custom-call | flops 67108864 | bytes 2097152 | tf_op jit(solution)/shard_map/coefficients/pallas_call | solution.py:246
  22.7 0.7 select_reduce_fusion.5
  23.4 1.3 select_select_fusion.row_ref
  24.8 14.5 %own_pairs.1 = (f32[16,8192]{1,0:T(8,128)S(1)}, s32[768]{0:T(1024)S(1)}) custom-call(s32[320]{0:T(512)S(1)} %select_select_fusion.row_ref, bf16[32,96,128]{2,1,0:T(8,128)(2,1)S(1)} %copy-done.11), custom_call_target="tpu_custom_call" | custom-call | flops 4278190080 | bytes 2097152 | tf_op jit(solution)/shard_map/own_pairs/pallas_call | solution.py:412
  39.3 0.8 copy-done.17
  40.1 1.7 %collective-permute-start = (bf16[2,96,128]{2,1,0:T(8,128)(2,1)S(1)}, bf16[2,96,128]{2,1,0:T(8,128)(2,1)S(1)}, u32[]{:S(2)}, u32[]{:S(2)}) collective-permute-start(bf16[2,96,128]{2,1,0:T(8,128)(2,1)S(1)} %copy-done.20), channel_id=1, source_target_pairs={{0,1},{1,2},{2,3},{3,4},{4,5},{5,6},{6,7},{7,8},{8,9},{9,10},{10,1... | collective-permute-start | bytes 147464 | tf_op jit(solution)/shard_map/ppermute | solution.py:595
  41.9 0.7 collective-permute-start.1
  42.5 49.4 %collective-permute-done.left_ref = bf16[2,96,128]{2,1,0:T(8,128)(2,1)S(1)} collective-permute-done((bf16[2,96,128]{2,1,0:T(8,128)(2,1)S(1)}, bf16[2,96,128]{2,1,0:T(8,128)(2,1)S(1)}, u32[]{:S(2)}, u32[]{:S(2)}) %collective-permute-start) | collective-permute-done | bytes 49184 | tf_op jit(solution)/shard_map/ppermute | solution.py:595
  93.2 9.2 %all-to-all-done.arrived_ref = bf16[128,208,128]{2,1,0:T(8,128)(2,1)} async-done(((bf16[128,208,128]{2,1,0:T(8,128)(2,1)}), bf16[128,208,128]{2,1,0:T(8,128)(2,1)}, u32[]{:S(2)}, u32[]{:S(2)}) %all-to-all-start) | async-done | bytes 6815776 | tf_op jit(solution)/shard_map/all_to_all | solution.py:603
  102.4 3.8 %far_pack.1 = bf16[128,72,128]{2,1,0:T(8,128)(2,1)} custom-call(bf16[128,208,128]{2,1,0:T(8,128)(2,1)} %all-to-all-done.arrived_ref, bf16[5,48,128]{2,1,0:T(8,128)(2,1)} %copy-done.5), custom_call_target="tpu_custom_call" | custom-call | flops 1048576 | bytes 5242880 | tf_op jit(solution)/shard_map/far_pack/pallas_call | solution.py:299
  106.2 7.1 %all-to-all-start.1 = ((bf16[128,72,128]{2,1,0:T(8,128)(2,1)}), bf16[128,72,128]{2,1,0:T(8,128)(2,1)S(1)}, u32[]{:S(2)}, u32[]{:S(2)}) async-start(bf16[128,72,128]{2,1,0:T(8,128)(2,1)} %far_pack.1), calls=%async_computation.1 | async-start | bytes 4718592 | tf_op jit(solution)/shard_map/all_to_all | solution.py:603
  113.4 1.1 copy-done.12
  114.5 0.8 copy-done.14
  115.3 0.8 copy-done.16
  116.1 1.0 copy-done.18
  117.1 19.2 %remote_pairs.1.near_hbm = f32[16,8192]{1,0:T(8,128)S(1)} custom-call(s32[768]{0:T(1024)S(1)} %get-tuple-element.35.list_ref, bf16[128,208,128]{2,1,0:T(8,128)(2,1)} %all-to-all-done.arrived_ref, bf16[2,96,128]{2,1,0:T(8,128)(2,1)S(1)} %copy-done.14, bf16[2,96,128]{2,1,0:T(8,128)(2,1)S(1)} %copy-done.16, bf16[32,96,128]{2,1,0:T(8,128)(2,1)S(1)} %copy-done.12, ...), custom_call_target="tpu_custom_call" | custom-call | flops 7130316800 | bytes 8388608 | tf_op jit(solution)/shard_map/remote_pairs/pallas_call | solution.py:453
  136.4 0.8 copy-done.3
  137.1 9.2 %all-to-all-done.1.arrived_ref = bf16[128,72,128]{2,1,0:T(8,128)(2,1)S(1)} async-done(((bf16[128,72,128]{2,1,0:T(8,128)(2,1)}), bf16[128,72,128]{2,1,0:T(8,128)(2,1)S(1)}, u32[]{:S(2)}, u32[]{:S(2)}) %all-to-all-start.1) | async-done | bytes 2359328 | tf_op jit(solution)/shard_map/all_to_all | solution.py:603
  146.4 1.4 collective-permute-start.2
  147.8 1.9 %far_one_field.1 = (f32[4,16,128]{2,1,0:T(8,128)S(1)}, f32[16,8192]{1,0:T(8,128)S(1)}, bf16[8,64,256]{2,1,0:T(8,128)(2,1)S(1)}) custom-call(s32[8,8]{1,0:T(8,128)S(1)} %copy-done.8, s32[8,128]{1,0:T(8,128)S(1)} %copy-done.9, bf16[128,72,128]{2,1,0:T(8,128)(2,1)S(1)} %all-to-all-done.1.arrived_ref, bf16[32,512]{1,0:T(8,128)(2,1)S(1)} %copy-done.6, ...), custom_call_target="tpu_custom_call" | custom-call | flops 268435456 | bytes 2097152 | tf_op jit(solution)/shard_map/far_one_field/pallas_call | solution.py:521
  149.7 2.9 %finish.1 = bf16[16,8192]{1,0:T(8,128)(2,1)} custom-call(s32[2,8]{1,0:T(2,128)S(1)} %copy-done.10, bf16[128,24,128]{2,1,0:T(8,128)(2,1)S(1)} %slice.3.mine_ref, bf16[128,24,128]{2,1,0:T(8,128)(2,1)S(1)} %collective-permute-done.2.theirs_ref, f32[4,16,128]{2,1,0:T(8,128)S(1)} %get-tuple-element.42.field_one_ref, f32[16,8192]{1,0:T(8,128)S(1)} %get-tuple-element.43.near_ref, ...), custom_call_target="tpu_custom_call" | custom-call | flops 268435456 | bytes 3145728 | tf_op jit(solution)/shard_map/finish/pallas_call | solution.py:582
  (47 shorter events, 3.0 us)
Async XLA Ops:
  6.7 13.8 %copy-start = (bf16[64,8192]{1,0:T(8,128)(2,1)S(1)}, bf16[64,8192]{1,0:T(8,128)(2,1)}, u32[]{:S(2)}) copy-start(bf16[64,8192]{1,0:T(8,128)(2,1)} %basis_hbm.3) | copy-start | bytes 3145732
  6.7 13.8 %copy-start.1 = (bf16[8,64,256]{2,1,0:T(8,128)(2,1)S(1)}, bf16[8,64,256]{2,1,0:T(8,128)(2,1)}, u32[]{:S(2)}) copy-start(bf16[8,64,256]{2,1,0:T(8,128)(2,1)} %one_hbm.3) | copy-start | bytes 786436
  6.7 13.8 %copy-start.2 = (bf16[16,8192]{1,0:T(8,128)(2,1)S(1)}, bf16[16,8192]{1,0:T(8,128)(2,1)}, u32[]{:S(2)}) copy-start(bf16[16,8192]{1,0:T(8,128)(2,1)} %rhs_hbm.1) | copy-start | bytes 786436
  6.7 13.8 %copy-start.4 = (bf16[2,64,256]{2,1,0:T(8,128)(2,1)S(1)}, bf16[2,64,256]{2,1,0:T(8,128)(2,1)}, u32[]{:S(2)}) copy-start(bf16[2,64,256]{2,1,0:T(8,128)(2,1)} %two_hbm.3) | copy-start | bytes 196612
  6.7 13.8 %copy-start.6 = (bf16[32,512]{1,0:T(8,128)(2,1)S(1)}, bf16[32,512]{1,0:T(8,128)(2,1)}, u32[]{:S(2)}) copy-start(bf16[32,512]{1,0:T(8,128)(2,1)} %skel_hbm.2) | copy-start | bytes 98308
  6.7 13.8 %copy-start.7 = (bf16[32,128]{1,0:T(8,128)(2,1)S(1)}, bf16[32,128]{1,0:T(8,128)(2,1)}, u32[]{:S(2)}) copy-start(bf16[32,128]{1,0:T(8,128)(2,1)} %skel_hbm.3) | copy-start | bytes 24580
  6.7 18.0 %copy-start.11 = (bf16[32,96,128]{2,1,0:T(8,128)(2,1)S(1)}, bf16[32,96,128]{2,1,0:T(8,128)(2,1)}, u32[]{:S(2)}) copy-start(bf16[32,96,128]{2,1,0:T(8,128)(2,1)} %get-tuple-element.28.own_hbm) | copy-start | bytes 2359300
  6.8 95.7 %all-to-all-start = ((bf16[128,208,128]{2,1,0:T(8,128)(2,1)}), bf16[128,208,128]{2,1,0:T(8,128)(2,1)}, u32[]{:S(2)}, u32[]{:S(2)}) async-start(bf16[128,208,128]{2,1,0:T(8,128)(2,1)} %get-tuple-element.25), calls=%async_computation | async-start | bytes 13631488 | tf_op jit(solution)/shard_map/all_to_all | solution.py:603
  22.0 0.6 copy-start.5
  24.7 15.4 %copy-start.20 = (bf16[2,96,128]{2,1,0:T(8,128)(2,1)S(1)}, bf16[2,96,128]{2,1,0:T(8,128)(2,1)}, u32[]{:S(2)}) copy-start(bf16[2,96,128]{2,1,0:T(8,128)(2,1)} %get-tuple-element.31) | copy-start | bytes 147460
  24.7 17.1 %copy-start.19 = (bf16[2,96,128]{2,1,0:T(8,128)(2,1)S(1)}, bf16[2,96,128]{2,1,0:T(8,128)(2,1)}, u32[]{:S(2)}) copy-start(bf16[2,96,128]{2,1,0:T(8,128)(2,1)} %get-tuple-element.32) | copy-start | bytes 147460
  39.3 0.8 copy-start.17
  40.1 51.8 %collective-permute-start = (bf16[2,96,128]{2,1,0:T(8,128)(2,1)S(1)}, bf16[2,96,128]{2,1,0:T(8,128)(2,1)S(1)}, u32[]{:S(2)}, u32[]{:S(2)}) collective-permute-start(bf16[2,96,128]{2,1,0:T(8,128)(2,1)S(1)} %copy-done.20), channel_id=1, source_target_pairs={{0,1},{1,2},{2,3},{3,4},{4,5},{5,6},{6,7},{7,8},{8,9},{9,10},{10,1... | collective-permute-start | bytes 147464 | tf_op jit(solution)/shard_map/ppermute | solution.py:595
  41.9 50.7 %collective-permute-start.1 = (bf16[2,96,128]{2,1,0:T(8,128)(2,1)S(1)}, bf16[2,96,128]{2,1,0:T(8,128)(2,1)S(1)}, u32[]{:S(2)}, u32[]{:S(2)}) collective-permute-start(bf16[2,96,128]{2,1,0:T(8,128)(2,1)S(1)} %copy-done.19), channel_id=1, source_target_pairs={{0,127},{1,0},{2,1},{3,2},{4,3},{5,4},{6,5},{7,6},{8,7},{9,8},{10,... | collective-permute-start | bytes 147464 | tf_op jit(solution)/shard_map/ppermute | solution.py:595
  106.2 40.1 %all-to-all-start.1 = ((bf16[128,72,128]{2,1,0:T(8,128)(2,1)}), bf16[128,72,128]{2,1,0:T(8,128)(2,1)S(1)}, u32[]{:S(2)}, u32[]{:S(2)}) async-start(bf16[128,72,128]{2,1,0:T(8,128)(2,1)} %far_pack.1), calls=%async_computation.1 | async-start | bytes 4718592 | tf_op jit(solution)/shard_map/all_to_all | solution.py:603
  113.3 1.1 copy-start.12
  114.5 0.8 copy-start.14
  115.3 0.8 copy-start.16
  116.1 1.0 copy-start.18
  117.1 30.7 %copy-start.8 = (s32[8,8]{1,0:T(8,128)S(1)}, s32[8,8]{1,0:T(8,128)}, u32[]{:S(2)}) copy-start(s32[8,8]{1,0:T(8,128)} %far_ref.4) | copy-start | bytes 772
  117.1 30.7 %copy-start.9 = (s32[8,128]{1,0:T(8,128)S(1)}, s32[8,128]{1,0:T(8,128)}, u32[]{:S(2)}) copy-start(s32[8,128]{1,0:T(8,128)} %get-tuple-element.40.low_ref) | copy-start | bytes 12292
  117.1 32.6 %copy-start.10 = (s32[2,8]{1,0:T(2,128)S(1)}, s32[2,8]{1,0:T(2,128)}, u32[]{:S(2)}) copy-start(s32[2,8]{1,0:T(2,128)} %far_ref.5) | copy-start | bytes 196
  136.4 0.8 copy-start.3
  146.4 3.3 %collective-permute-start.2 = (bf16[128,24,128]{2,1,0:T(8,128)(2,1)S(1)}, bf16[128,24,128]{2,1,0:T(8,128)(2,1)S(1)}, u32[]{:S(2)}, u32[]{:S(2)}) collective-permute-start(bf16[128,24,128]{2,1,0:T(8,128)(2,1)S(1)} %slice.3.mine_ref), channel_id=1, source_target_pairs={{0,1},{1,0},{2,3},{3,2},{4,5},{5,4},{6,7},{7,6},{8,9},{9,8},{10,11... | collective-permute-start | bytes 2359304 | tf_op jit(solution)/shard_map/ppermute | solution.py:599
  (2 other events, 1.2 us)

commit v7 on v6

--- a/solution.py
+++ b/solution.py
@@ -23,7 +23,7 @@
 LIST = 384
 STRIDE = 512
 HALF_ROWS = ROWS // 2
-MESSAGE = ROWS + HALF_ROWS
+MESSAGE = ROWS + HALF_ROWS - 8
 BLOCK = 2 * ROWS
 ASK = 2 * BLOCK
 NEAR_MESSAGE = ASK + 16
@@ -62,7 +62,7 @@
 
 
 def pack_kernel(
-    source_ref, far_ref, points_ref, rhs_ref, msg_ref, right_ref, left_ref, own_ref, low_ref,
+    source_ref, far_ref, skel_ref, points_ref, rhs_ref, msg_ref, right_ref, left_ref, own_ref, low_ref,
     lists_ref, points_vmem, rhs_vmem, block_ref, ask_ref, row_ref, row_smem,
     in_sem, row_sem, ask_sem, msg_sem, side_sem,
 ):
@@ -82,8 +82,20 @@
     high = jnp.max(high.astype(jnp.float32), axis=1, keepdims=True)
     lane = lax.broadcasted_iota(jnp.int32, (PEERS, PEERS), 1)
     wanted = jnp.where(lane < RANK, low, high)
-    ask_ref[...] = jnp.broadcast_to(
-        wanted[:, None, :], (PEERS, NEAR_MESSAGE - ASK, 2 * RANK)
+    wide = skel_ref[...].astype(jnp.float32)
+    turned = pltpu.roll(wide, RANK, 1)
+    left = lane[:8] < RANK
+    tops = (
+        jnp.where(left, wide[:8], turned[HALF_ROWS:]),
+        jnp.where(left, turned[:8], wide[HALF_ROWS:]),
+    )
+    core = lax.broadcasted_iota(jnp.int32, (PEERS, 8, 2 * RANK), 0) & 1
+    ask_ref[...] = jnp.concatenate(
+        [
+            jnp.broadcast_to(wanted[:, None, :], core.shape),
+            jnp.where(core == 0, tops[0][None], tops[1][None]),
+        ],
+        axis=1,
     ).astype(jnp.bfloat16)
     asked = pltpu.make_async_copy(ask_ref, msg_ref.at[:, pl.ds(ASK, NEAR_MESSAGE - ASK)], ask_sem)
     asked.start()
@@ -166,7 +178,7 @@
     own.wait()
 
 
-def pack(source, far_one, points, rhs):
+def pack(source, far_one, skeleton_two, points, rhs):
     block = jax.ShapeDtypeStruct((LEAVES, BLOCK, 128), jnp.bfloat16)
     side = jax.ShapeDtypeStruct((2, BLOCK, 128), jnp.bfloat16)
     return pl.pallas_call(
@@ -175,7 +187,7 @@
             jax.ShapeDtypeStruct((PEERS, NEAR_MESSAGE, 128), jnp.bfloat16), side, side, block,
             jax.ShapeDtypeStruct((ONE, PEERS), jnp.int32),
         ),
-        in_specs=[ANY, VM, ANY, ANY],
+        in_specs=[ANY, VM, VM, ANY, ANY],
         out_specs=(ANY, ANY, ANY, ANY, VM),
         scratch_shapes=[
             pltpu.VMEM((NEAR, PEERS * LEAVES), jnp.int32),
@@ -194,7 +206,7 @@
         compiler_params=vmem(56),
         cost_estimate=cost(1 << 20, 14 * MIB),
         name="pack",
-    )(source.T, far_one, points, rhs)
+    )(source.T, far_one, skeleton_two, points, rhs)
 
 
 def upper(b):
@@ -282,7 +294,7 @@
             first = cluster_ref[0]
             for c in range(1, ONE):
                 first = jnp.where(wanted == c, cluster_ref[c], first)
-            out_ref[peer] = jnp.concatenate([first, second[core]], axis=0).astype(jnp.bfloat16)
+            out_ref[peer] = jnp.concatenate([first, second[core][8:]], axis=0).astype(jnp.bfloat16)
         return 0
 
     sent = []
@@ -608,7 +620,9 @@
     far_one, far_two,
 ):
     me = lax.axis_index("leaf")
-    message, to_right, to_left, own, low = pack(near_source, far_one, points, rhs)
+    message, to_right, to_left, own, low = pack(
+        near_source, far_one, skeleton_two, points, rhs
+    )
     arrived = exchange(message)
     columns = coefficients(rhs, basis, transfer_one, transfer_two, skeleton_one, skeleton_two)
     field, lists = own_pairs(table_rows(near_source, me), own)
@@ -620,7 +634,7 @@
     far_arrived = exchange(far_pack(arrived, columns))
     near = remote_pairs(lists, arrived, from_left, from_right, own, field)
     far_arrived, near = lax.optimization_barrier((far_arrived, near))
-    mine = far_arrived[:, ROWS:, :]
+    mine = jnp.concatenate([arrived[:, NEAR_MESSAGE - 8 :], far_arrived[:, ROWS:]], axis=1)
     theirs = swap(mine)
     near = pltpu.with_memory_space_constraint(near, pltpu.HBM)
     transfer_one = pltpu.with_memory_space_constraint(transfer_one, pltpu.HBM)

time: 153 us -> 151 us (0.987)
    unnamed x43 -> x35, local copies, waits for them, and re-layouts: 7.37 us -> 4.54 us
    slice x1 -> x2, local copies, waits for them, and re-layouts: 0.08 us -> 1.74 us  [the longest x1 1.67 us: local(): arrived[:, NEAR_MESSAGE - 8:]]
    all_to_all x2, waiting for transfers between devices: 18.4 us -> 16.8 us  [exchange(): return lax.all_to_all(x, 'leaf', split_axis=0, concat_axis=0, tiled=True)]
  transfers between devices with their start and end apart: 5 -> 5, of which waited for: 3 -> 3; matrix products, arithmetic and copies ran while one was open for 2% -> 3% of each run, Pallas kernels for 24% -> 25%
where the time goes in v7:
time: 151 us
  waiting for transfers between devices  66.4 us (44%)
  Pallas kernels  50.5 us (33%)
  starting transfers between devices  22.8 us (15%)
  local copies, waits for them, and re-layouts  7.47 us (5%)
  other arithmetic  3.35 us (2%)
    ppermute x2, waiting for transfers between devices, shift(): lax.ppermute(x, 'leaf', [(i, (i + step) % PEERS) for i in range(PEERS)])  49.6 us
    pallas_call x1, Pallas kernels, remote_pairs(): pl.pallas_call(remote_kernel, out_shape=jax.ShapeDtypeStruct((NRHS, LEAVE...  19.2 us
    all_to_all x2, starting transfers between devices, exchange(): return lax.all_to_all(x, 'leaf', split_axis=0, concat_axis=0, tiled=True)  19 us
    all_to_all x2, waiting for transfers between devices, exchange(): return lax.all_to_all(x, 'leaf', split_axis=0, concat_axis=0, tiled=True)  16.8 us
    pallas_call x1, Pallas kernels, own_pairs(): pl.pallas_call(own_kernel, out_shape=(jax.ShapeDtypeStruct((NRHS, LEAVES...  14.5 us
    pallas_call x1, Pallas kernels, pack(): pl.pallas_call(pack_kernel, out_shape=(jax.ShapeDtypeStruct((PEERS, NEAR_...  6.72 us
    unnamed x35, local copies, waits for them, and re-layouts  4.54 us
    pallas_call x1, Pallas kernels, far_pack(): pl.pallas_call(far_pack_kernel, out_shape=jax.ShapeDtypeStruct((PEERS, ME...  3.73 us
  transfers between devices with their start and end apart: 5, of which 3 were waited for; matrix products, arithmetic and copies ran while one was open for 3% of the time, Pallas kernels for 25%

profile of v7, /device:TPU:1, one launch (start us, length us, event | category | flops | bytes accessed | tf_op | source)
XLA Modules:
  0.0 150.8 jit_solution(5772691729303257001)
XLA Ops:
  0.0 6.7 %pack.1 = (bf16[128,208,128]{2,1,0:T(8,128)(2,1)}, bf16[2,96,128]{2,1,0:T(8,128)(2,1)}, bf16[2,96,128]{2,1,0:T(8,128)(2,1)}, bf16[32,96,128]{2,1,0:T(8,128)(2,1)}, s32[8,128]{1,0:T(8,128)}) custom-call(s32[10,4096]{1,0:T(8,128)} %bitcast.1, s32[8,8]{1,0:T(8,128)} %far_ref.4, bf16[32,128]{1,0:T(8,128)(2,1)} %skel_hbm.3, bf16[32,8192]{1,0:T(8,128)(2,1)} %points_ref.1, ...), custom_call_target="tpu_custom_call" | custom-call | flops 1048576 | bytes 14680064 | tf_op jit(solution)/shard_map/pack/pallas_call | solution.py:184
  6.8 11.9 %all-to-all-start = ((bf16[128,208,128]{2,1,0:T(8,128)(2,1)}), bf16[128,208,128]{2,1,0:T(8,128)(2,1)}, u32[]{:S(2)}, u32[]{:S(2)}) async-start(bf16[128,208,128]{2,1,0:T(8,128)(2,1)} %get-tuple-element.25), calls=%async_computation | async-start | bytes 13631488 | tf_op jit(solution)/shard_map/all_to_all | solution.py:615
  18.7 0.8 constant_dynamic-slice_fusion
  20.6 1.5 %coefficients.1.columns_ref = bf16[5,48,128]{2,1,0:T(8,128)(2,1)S(1)} custom-call(bf16[16,8192]{1,0:T(8,128)(2,1)S(1)} %copy-done.2, bf16[64,8192]{1,0:T(8,128)(2,1)S(1)} %copy-done, bf16[8,64,256]{2,1,0:T(8,128)(2,1)S(1)} %copy-done.1, bf16[2,64,256]{2,1,0:T(8,128)(2,1)S(1)} %copy-done.4, bf16[32,512]{1,0:T(8,128)(2,1)S(1)} %copy-done.6, ...), custom_call_target="tpu_custom_call" | custom-call | flops 67108864 | bytes 2097152 | tf_op jit(solution)/shard_map/coefficients/pallas_call | solution.py:258
  22.7 0.7 select_reduce_fusion.5
  23.4 1.2 select_select_fusion.row_ref
  24.6 14.5 %own_pairs.1 = (f32[16,8192]{1,0:T(8,128)S(1)}, s32[768]{0:T(1024)S(1)}) custom-call(s32[320]{0:T(512)S(1)} %select_select_fusion.row_ref, bf16[32,96,128]{2,1,0:T(8,128)(2,1)S(1)} %copy-done.11), custom_call_target="tpu_custom_call" | custom-call | flops 4278190080 | bytes 2097152 | tf_op jit(solution)/shard_map/own_pairs/pallas_call | solution.py:424
  39.2 0.8 copy-done.13
  40.0 1.7 %collective-permute-start = (bf16[2,96,128]{2,1,0:T(8,128)(2,1)S(1)}, bf16[2,96,128]{2,1,0:T(8,128)(2,1)S(1)}, u32[]{:S(2)}, u32[]{:S(2)}) collective-permute-start(bf16[2,96,128]{2,1,0:T(8,128)(2,1)S(1)} %copy-done.16), channel_id=1, source_target_pairs={{0,1},{1,2},{2,3},{3,4},{4,5},{5,6},{6,7},{7,8},{8,9},{9,10},{10,1... | collective-permute-start | bytes 147464 | tf_op jit(solution)/shard_map/ppermute | solution.py:607
  41.7 0.7 collective-permute-start.1
  42.4 49.6 %collective-permute-done.left_ref = bf16[2,96,128]{2,1,0:T(8,128)(2,1)S(1)} collective-permute-done((bf16[2,96,128]{2,1,0:T(8,128)(2,1)S(1)}, bf16[2,96,128]{2,1,0:T(8,128)(2,1)S(1)}, u32[]{:S(2)}, u32[]{:S(2)}) %collective-permute-start) | collective-permute-done | bytes 49184 | tf_op jit(solution)/shard_map/ppermute | solution.py:607
  92.0 10.5 %all-to-all-done.arrived_ref = bf16[128,208,128]{2,1,0:T(8,128)(2,1)} async-done(((bf16[128,208,128]{2,1,0:T(8,128)(2,1)}), bf16[128,208,128]{2,1,0:T(8,128)(2,1)}, u32[]{:S(2)}, u32[]{:S(2)}) %all-to-all-start) | async-done | bytes 6815776 | tf_op jit(solution)/shard_map/all_to_all | solution.py:615
  102.5 3.7 %far_pack.1 = bf16[128,64,128]{2,1,0:T(8,128)(2,1)} custom-call(bf16[128,208,128]{2,1,0:T(8,128)(2,1)} %all-to-all-done.arrived_ref, bf16[5,48,128]{2,1,0:T(8,128)(2,1)} %copy-done.5), custom_call_target="tpu_custom_call" | custom-call | flops 1048576 | bytes 5242880 | tf_op jit(solution)/shard_map/far_pack/pallas_call | solution.py:311
  106.2 7.1 %all-to-all-start.1 = ((bf16[128,64,128]{2,1,0:T(8,128)(2,1)}), bf16[128,64,128]{2,1,0:T(8,128)(2,1)S(1)}, u32[]{:S(2)}, u32[]{:S(2)}) async-start(bf16[128,64,128]{2,1,0:T(8,128)(2,1)} %far_pack.1), calls=%async_computation.1 | async-start | bytes 4194304 | tf_op jit(solution)/shard_map/all_to_all | solution.py:615
  113.3 1.7 %slice.6 = bf16[128,8,128]{2,1,0:T(8,128)(2,1)} slice(bf16[128,208,128]{2,1,0:T(8,128)(2,1)} %all-to-all-done.arrived_ref), slice={[0:128], [200:208], [0:128]} | slice | bytes 524288 | tf_op jit(solution)/shard_map/slice | solution.py:637
  115.0 1.1 copy-done.12
  116.1 1.0 copy-done.14
  117.2 19.2 %remote_pairs.1.near_hbm = f32[16,8192]{1,0:T(8,128)S(1)} custom-call(s32[768]{0:T(1024)S(1)} %get-tuple-element.35.list_ref, bf16[128,208,128]{2,1,0:T(8,128)(2,1)} %all-to-all-done.arrived_ref, bf16[2,96,128]{2,1,0:T(8,128)(2,1)S(1)} %collective-permute-done.left_ref, bf16[2,96,128]{2,1,0:T(8,128)(2,1)S(1)} %collective-permute-done.1.right_ref, ...), custom_call_target="tpu_custom_call" | custom-call | flops 7130316800 | bytes 8388608 | tf_op jit(solution)/shard_map/remote_pairs/pallas_call | solution.py:465
  136.4 0.8 copy-done.3
  137.2 6.4 %all-to-all-done.1.arrived_ref = bf16[128,64,128]{2,1,0:T(8,128)(2,1)S(1)} async-done(((bf16[128,64,128]{2,1,0:T(8,128)(2,1)}), bf16[128,64,128]{2,1,0:T(8,128)(2,1)S(1)}, u32[]{:S(2)}, u32[]{:S(2)}) %all-to-all-start.1) | async-done | bytes 2097184 | tf_op jit(solution)/shard_map/all_to_all | solution.py:615
  143.7 1.0 pad_maximum_fusion.mine_ref
  144.7 1.3 collective-permute-start.2
  146.0 1.9 %far_one_field.1 = (f32[4,16,128]{2,1,0:T(8,128)S(1)}, f32[16,8192]{1,0:T(8,128)S(1)}, bf16[8,64,256]{2,1,0:T(8,128)(2,1)S(1)}) custom-call(s32[8,8]{1,0:T(8,128)S(1)} %copy-done.8, s32[8,128]{1,0:T(8,128)S(1)} %copy-done.9, bf16[128,64,128]{2,1,0:T(8,128)(2,1)S(1)} %all-to-all-done.1.arrived_ref, bf16[32,512]{1,0:T(8,128)(2,1)S(1)} %copy-done.6, ...), custom_call_target="tpu_custom_call" | custom-call | flops 268435456 | bytes 2097152 | tf_op jit(solution)/shard_map/far_one_field/pallas_call | solution.py:533
  148.0 2.9 %finish.1 = bf16[16,8192]{1,0:T(8,128)(2,1)} custom-call(s32[2,8]{1,0:T(2,128)S(1)} %copy-done.10, bf16[128,24,128]{2,1,0:T(8,128)(2,1)S(1)} %pad_maximum_fusion.mine_ref, bf16[128,24,128]{2,1,0:T(8,128)(2,1)S(1)} %collective-permute-done.2.theirs_ref, f32[4,16,128]{2,1,0:T(8,128)S(1)} %get-tuple-element.42.field_one_ref, ...), custom_call_target="tpu_custom_call" | custom-call | flops 268435456 | bytes 3145728 | tf_op jit(solution)/shard_map/finish/pallas_call | solution.py:594
  (41 shorter events, 1.7 us)
Async XLA Ops:
  6.7 13.8 %copy-start = (bf16[64,8192]{1,0:T(8,128)(2,1)S(1)}, bf16[64,8192]{1,0:T(8,128)(2,1)}, u32[]{:S(2)}) copy-start(bf16[64,8192]{1,0:T(8,128)(2,1)} %basis_hbm.3) | copy-start | bytes 3145732
  6.7 13.8 %copy-start.1 = (bf16[8,64,256]{2,1,0:T(8,128)(2,1)S(1)}, bf16[8,64,256]{2,1,0:T(8,128)(2,1)}, u32[]{:S(2)}) copy-start(bf16[8,64,256]{2,1,0:T(8,128)(2,1)} %one_hbm.3) | copy-start | bytes 786436
  6.8 13.8 %copy-start.2 = (bf16[16,8192]{1,0:T(8,128)(2,1)S(1)}, bf16[16,8192]{1,0:T(8,128)(2,1)}, u32[]{:S(2)}) copy-start(bf16[16,8192]{1,0:T(8,128)(2,1)} %rhs_hbm.1) | copy-start | bytes 786436
  6.8 13.8 %copy-start.4 = (bf16[2,64,256]{2,1,0:T(8,128)(2,1)S(1)}, bf16[2,64,256]{2,1,0:T(8,128)(2,1)}, u32[]{:S(2)}) copy-start(bf16[2,64,256]{2,1,0:T(8,128)(2,1)} %two_hbm.3) | copy-start | bytes 196612
  6.8 13.8 %copy-start.6 = (bf16[32,512]{1,0:T(8,128)(2,1)S(1)}, bf16[32,512]{1,0:T(8,128)(2,1)}, u32[]{:S(2)}) copy-start(bf16[32,512]{1,0:T(8,128)(2,1)} %skel_hbm.2) | copy-start | bytes 98308
  6.8 13.8 %copy-start.7 = (bf16[32,128]{1,0:T(8,128)(2,1)S(1)}, bf16[32,128]{1,0:T(8,128)(2,1)}, u32[]{:S(2)}) copy-start(bf16[32,128]{1,0:T(8,128)(2,1)} %skel_hbm.3) | copy-start | bytes 24580
  6.8 17.8 %copy-start.11 = (bf16[32,96,128]{2,1,0:T(8,128)(2,1)S(1)}, bf16[32,96,128]{2,1,0:T(8,128)(2,1)}, u32[]{:S(2)}) copy-start(bf16[32,96,128]{2,1,0:T(8,128)(2,1)} %get-tuple-element.28.own_hbm) | copy-start | bytes 2359300
  6.8 95.7 %all-to-all-start = ((bf16[128,208,128]{2,1,0:T(8,128)(2,1)}), bf16[128,208,128]{2,1,0:T(8,128)(2,1)}, u32[]{:S(2)}, u32[]{:S(2)}) async-start(bf16[128,208,128]{2,1,0:T(8,128)(2,1)} %get-tuple-element.25), calls=%async_computation | async-start | bytes 13631488 | tf_op jit(solution)/shard_map/all_to_all | solution.py:615
  22.1 0.6 copy-start.5
  24.6 15.4 %copy-start.16 = (bf16[2,96,128]{2,1,0:T(8,128)(2,1)S(1)}, bf16[2,96,128]{2,1,0:T(8,128)(2,1)}, u32[]{:S(2)}) copy-start(bf16[2,96,128]{2,1,0:T(8,128)(2,1)} %get-tuple-element.31) | copy-start | bytes 147460
  24.6 17.1 %copy-start.15 = (bf16[2,96,128]{2,1,0:T(8,128)(2,1)S(1)}, bf16[2,96,128]{2,1,0:T(8,128)(2,1)}, u32[]{:S(2)}) copy-start(bf16[2,96,128]{2,1,0:T(8,128)(2,1)} %get-tuple-element.32) | copy-start | bytes 147460
  39.2 0.8 copy-start.13
  40.0 52.0 %collective-permute-start = (bf16[2,96,128]{2,1,0:T(8,128)(2,1)S(1)}, bf16[2,96,128]{2,1,0:T(8,128)(2,1)S(1)}, u32[]{:S(2)}, u32[]{:S(2)}) collective-permute-start(bf16[2,96,128]{2,1,0:T(8,128)(2,1)S(1)} %copy-done.16), channel_id=1, source_target_pairs={{0,1},{1,2},{2,3},{3,4},{4,5},{5,6},{6,7},{7,8},{8,9},{9,10},{10,1... | collective-permute-start | bytes 147464 | tf_op jit(solution)/shard_map/ppermute | solution.py:607
  41.7 50.3 %collective-permute-start.1 = (bf16[2,96,128]{2,1,0:T(8,128)(2,1)S(1)}, bf16[2,96,128]{2,1,0:T(8,128)(2,1)S(1)}, u32[]{:S(2)}, u32[]{:S(2)}) collective-permute-start(bf16[2,96,128]{2,1,0:T(8,128)(2,1)S(1)} %copy-done.15), channel_id=1, source_target_pairs={{0,127},{1,0},{2,1},{3,2},{4,3},{5,4},{6,5},{7,6},{8,7},{9,8},{10,... | collective-permute-start | bytes 147464 | tf_op jit(solution)/shard_map/ppermute | solution.py:607
  106.2 37.4 %all-to-all-start.1 = ((bf16[128,64,128]{2,1,0:T(8,128)(2,1)}), bf16[128,64,128]{2,1,0:T(8,128)(2,1)S(1)}, u32[]{:S(2)}, u32[]{:S(2)}) async-start(bf16[128,64,128]{2,1,0:T(8,128)(2,1)} %far_pack.1), calls=%async_computation.1 | async-start | bytes 4194304 | tf_op jit(solution)/shard_map/all_to_all | solution.py:615
  115.0 1.1 copy-start.12
  116.1 1.0 copy-start.14
  136.4 0.8 copy-start.3
  137.2 8.8 %copy-start.8 = (s32[8,8]{1,0:T(8,128)S(1)}, s32[8,8]{1,0:T(8,128)}, u32[]{:S(2)}) copy-start(s32[8,8]{1,0:T(8,128)} %far_ref.4) | copy-start | bytes 772
  137.2 8.8 %copy-start.9 = (s32[8,128]{1,0:T(8,128)S(1)}, s32[8,128]{1,0:T(8,128)}, u32[]{:S(2)}) copy-start(s32[8,128]{1,0:T(8,128)} %get-tuple-element.40.low_ref) | copy-start | bytes 12292
  143.6 4.3 %copy-start.10 = (s32[2,8]{1,0:T(2,128)S(1)}, s32[2,8]{1,0:T(2,128)}, u32[]{:S(2)}) copy-start(s32[2,8]{1,0:T(2,128)} %far_ref.5) | copy-start | bytes 196
  144.7 3.3 %collective-permute-start.2 = (bf16[128,24,128]{2,1,0:T(8,128)(2,1)S(1)}, bf16[128,24,128]{2,1,0:T(8,128)(2,1)S(1)}, u32[]{:S(2)}, u32[]{:S(2)}) collective-permute-start(bf16[128,24,128]{2,1,0:T(8,128)(2,1)S(1)} %pad_maximum_fusion.mine_ref), channel_id=1, source_target_pairs={{0,1},{1,0},{2,3},{3,2},{4,5},{5,4},{6,7},{7,6},{8,9},{9,8},{10,11... | collective-permute-start | bytes 2359304 | tf_op jit(solution)/shard_map/ppermute | solution.py:611
